TPU v7x, 32 devices: a whole 2x2x4 slice. The times are simulated.
32 devices in a mesh: group: 4 (over z), ctx: 2 (over y), wshard: 4 (over x, core).
Axes of the slice: x: 2, y: 2, z: 4, core: 2. Of those that a mesh axis runs over, the one named last changes fastest.
Arguments:
- tokens: bfloat16 [16, 4096, 1152], P(('group', 'wshard'), 'ctx'), may hold values from -6 to 6
- block_map: int32 [16, 4], P(('group', 'wshard')), may hold values from 0 to 3, as said below
- attention_gain: bfloat16 [1152], P(('group', 'wshard')), may hold values from 0.099609375 to 1.8984375
- query_weight: bfloat16 [1152, 1152], P(('group', 'wshard')), may hold values from -0.1875 to 0.1875
- key_matrix: bfloat16 [1152, 384], P(('group', 'wshard')), may hold values from -0.1875 to 0.1875
- value_matrix: bfloat16 [1152, 384], P(('group', 'wshard')), may hold values from -0.1875 to 0.1875
- output_weight: bfloat16 [1152, 1152], P(('group', 'wshard')), may hold values from -3 to 3
- feedforward_gain: bfloat16 [1152], P(('group', 'wshard')), may hold values from 0.099609375 to 1.8984375
- gate_weight: bfloat16 [1152, 3072], P(('group', 'wshard')), may hold values from -0.1875 to 0.1875
- up_weight: bfloat16 [1152, 3072], P(('group', 'wshard')), may hold values from -0.1875 to 0.1875
- down_weight: bfloat16 [3072, 1152], P(('group', 'wshard')), may hold values from -0.109375 to 0.109375
- out_grad: bfloat16 [16, 4096, 1152], P(('group', 'wshard'), 'ctx'), may hold values from -6 to 6
Outputs:
- layer_out: bfloat16 [16, 4096, 1152], P(('group', 'wshard'), 'ctx')
- grad_tokens: float32 [16, 4096, 1152], P(('group', 'wshard'), 'ctx')
- grad_attention_gain: float32 [1152], P(('group', 'wshard'))
- grad_query_weight: float32 [1152, 1152], P(('group', 'wshard'))
- grad_key_weight: float32 [1152, 384], P(('group', 'wshard'))
- grad_value_weight: float32 [1152, 384], P(('group', 'wshard'))
- grad_output_weight: float32 [1152, 1152], P(('group', 'wshard'))
- grad_feedforward_gain: float32 [1152], P(('group', 'wshard'))
- grad_gate_weight: float32 [1152, 3072], P(('group', 'wshard'))
- grad_up_weight: float32 [1152, 3072], P(('group', 'wshard'))
- grad_down_weight: float32 [3072, 1152], P(('group', 'wshard'))
Inputs may be any that keep to these rules, and one draw needn't show every extreme that they name: `block_map`: in every group the entries are a permutation of the 4 blocks; entries 2 d and 2 d + 1 add up to 3, and entry 2 d is below half of 4.
All inputs are finite; a program needn't handle non-finite values.
Results may differ from a plain program's by a relative error of at most 0.024.
Values may be sent and summed in bfloat16 or wider, within the bound.
A program may use at most 384 MiB of HBM per device.

v0:
```python
import jax
import jax.numpy as jnp
from jax import lax
from jax.sharding import PartitionSpec as P

HEAD_WIDTH = 64
CONTINUE_LENGTH = 512


norm_eps = 1e-05
rope_base = 10000.0
masked_score = -1e30


def as_sent(array):

    def short(part):
        return part.astype(jnp.bfloat16) if part.dtype == jnp.float32 else part

    return jax.tree.map(short, array)


def rms_scale(value_rows_list, gain):
    return (
        value_rows_list
        * lax.rsqrt(jnp.mean(value_rows_list * value_rows_list, axis=-1, keepdims=True) + norm_eps)
        * gain
    )


def rms_back(value_rows_list, gain, upstream):
    inverse = lax.rsqrt(
        jnp.mean(value_rows_list * value_rows_list, axis=-1, keepdims=True) + norm_eps
    )
    scaled = upstream * gain
    gain_grad = jnp.sum(upstream * value_rows_list * inverse, axis=0)
    values_grad = inverse * scaled - value_rows_list * (inverse * inverse * inverse) * jnp.mean(
        scaled * value_rows_list, axis=-1, keepdims=True
    )
    return (gain_grad, values_grad)


def rope_tables(token_positions, head_size):
    half_size = head_size // 2
    frequency = rope_base ** (-(jnp.arange(half_size, dtype=jnp.float32) * 2.0) / head_size)
    angles = token_positions.astype(jnp.float32)[:, None] * frequency[None, :]
    return (jnp.cos(angles), jnp.sin(angles))


def rotary_apply(value_rows_list, cosine_table, sine_table):
    half_size = value_rows_list.shape[-1] // 2
    leading = value_rows_list[..., :half_size]
    trailing = value_rows_list[..., half_size:]
    cos_rows = cosine_table[:, None, :]
    sin_rows = sine_table[:, None, :]
    return jnp.concatenate(
        [leading * cos_rows - trailing * sin_rows, trailing * cos_rows + leading * sin_rows],
        axis=-1,
    )


def visible(query_pos, query_seg, key_pos, key_seg):
    same_doc = (key_seg[None, :] == query_seg[:, None]) | (key_seg[None, :] == 0)
    return same_doc & (key_pos[None, :] <= query_pos[:, None])


def tile_scores(query_tile, key_tile, scale):
    return (
        jnp.einsum("rhgd,khd->hgrk", query_tile, key_tile, preferred_element_type=jnp.float32)
        * scale
    )


def key_tiling(key_heads, value_heads, key_pos, key_seg):
    key_block = min(256, key_heads.shape[0])
    tile_count = key_heads.shape[0] // key_block
    return (
        key_heads.reshape(tile_count, key_block, key_heads.shape[1], key_heads.shape[2]),
        value_heads.reshape(tile_count, key_block, value_heads.shape[1], value_heads.shape[2]),
        key_pos.reshape(tile_count, key_block),
        key_seg.reshape(tile_count, key_block),
    )


def query_split(value_rows_list, query_block):
    return value_rows_list.reshape(
        (value_rows_list.shape[0] // query_block, query_block) + value_rows_list.shape[1:]
    )


def attention_forward(query_heads, key_heads, value_heads, places):
    query_pos, query_seg, key_pos, key_seg = places
    count_of_rows, kv_heads, group_size, head_size = query_heads.shape
    scale = head_size ** (-0.5)
    query_block = min(512, count_of_rows)
    key_tiles, value_tiles, kpos_tiles, kseg_tiles = key_tiling(
        key_heads, value_heads, key_pos, key_seg
    )

    def one_block(block_item):
        query_tile, tile_pos, tile_seg = block_item
        state_shape = (kv_heads, group_size, query_tile.shape[0])

        def lse_step(running, tile_item):
            key_tile, tile_kpos, tile_kseg = tile_item
            allowed = visible(tile_pos, tile_seg, tile_kpos, tile_kseg)

            def lse_open_tile(state):
                row_top, row_total = state
                scores = jnp.where(allowed, tile_scores(query_tile, key_tile, scale), masked_score)
                new_top = jnp.maximum(row_top, jnp.max(scores, axis=-1))
                weights = jnp.where(allowed, jnp.exp(scores - new_top[..., None]), 0.0)
                return (new_top, row_total * jnp.exp(row_top - new_top) + jnp.sum(weights, axis=-1))

            def lse_closed_tile(state):
                return state

            return (lax.cond(jnp.any(allowed), lse_open_tile, lse_closed_tile, running), None)

        initial = (
            jnp.full(state_shape, masked_score, jnp.float32),
            jnp.zeros(state_shape, jnp.float32),
        )
        (row_top, row_total), _ = lax.scan(lse_step, initial, (key_tiles, kpos_tiles, kseg_tiles))
        log_total = row_top + jnp.log(row_total)

        def out_step(running, tile_item):
            key_tile, value_tile, tile_kpos, tile_kseg = tile_item
            allowed = visible(tile_pos, tile_seg, tile_kpos, tile_kseg)

            def out_open_tile(accumulated):
                scores = jnp.where(allowed, tile_scores(query_tile, key_tile, scale), masked_score)
                probabilities = jnp.where(
                    allowed, jnp.exp(scores - log_total[..., None]), 0.0
                ).astype(jnp.bfloat16)
                return accumulated + jnp.einsum(
                    "hgrk,khd->rhgd", probabilities, value_tile, preferred_element_type=jnp.float32
                )

            def out_closed_tile(accumulated):
                return accumulated

            return (lax.cond(jnp.any(allowed), out_open_tile, out_closed_tile, running), None)

        output, _ = lax.scan(
            out_step,
            jnp.zeros(query_tile.shape, jnp.float32),
            (key_tiles, value_tiles, kpos_tiles, kseg_tiles),
        )
        return (output, log_total)

    outputs, log_totals = lax.map(
        one_block,
        (
            query_split(query_heads, query_block),
            query_split(query_pos, query_block),
            query_split(query_seg, query_block),
        ),
    )
    return (outputs.reshape(query_heads.shape), log_totals)


def attention_backward(
    query_heads, key_heads, value_heads, places, attended_grad, attended, log_totals
):
    query_pos, query_seg, key_pos, key_seg = places
    count_of_rows, kv_heads, group_size, head_size = query_heads.shape
    scale = head_size ** (-0.5)
    query_block = min(512, count_of_rows)
    key_tiles, value_tiles, kpos_tiles, kseg_tiles = key_tiling(
        key_heads, value_heads, key_pos, key_seg
    )

    def block_grads(sums, block_item):
        query_tile, grad_tile, output_tile, tile_lse, tile_pos, tile_seg = block_item
        tile_delta = jnp.einsum("rhgd,rhgd->hgr", grad_tile.astype(jnp.float32), output_tile)

        def back_step(query_grad, tile_item):
            key_tile, value_tile, tile_kpos, tile_kseg = tile_item
            allowed = visible(tile_pos, tile_seg, tile_kpos, tile_kseg)

            def back_open_tile(query_grad):
                scores = jnp.where(allowed, tile_scores(query_tile, key_tile, scale), masked_score)
                probabilities = jnp.where(allowed, jnp.exp(scores - tile_lse[..., None]), 0.0)
                prob_grad = jnp.einsum(
                    "rhgd,khd->hgrk", grad_tile, value_tile, preferred_element_type=jnp.float32
                )
                score_grad = (probabilities * (prob_grad - tile_delta[..., None])).astype(
                    jnp.bfloat16
                )
                query_grad = query_grad + scale * jnp.einsum(
                    "hgrk,khd->rhgd", score_grad, key_tile, preferred_element_type=jnp.float32
                )
                key_part = scale * jnp.einsum(
                    "hgrk,rhgd->khd", score_grad, query_tile, preferred_element_type=jnp.float32
                )
                value_part = jnp.einsum(
                    "hgrk,rhgd->khd",
                    probabilities.astype(jnp.bfloat16),
                    grad_tile,
                    preferred_element_type=jnp.float32,
                )
                return (query_grad, key_part, value_part)

            def back_closed_tile(query_grad):
                return (
                    query_grad,
                    jnp.zeros(key_tile.shape, jnp.float32),
                    jnp.zeros(value_tile.shape, jnp.float32),
                )

            query_grad, key_part, value_part = lax.cond(
                jnp.any(allowed), back_open_tile, back_closed_tile, query_grad
            )
            return (query_grad, (key_part, value_part))

        query_grad, (key_parts, value_parts) = lax.scan(
            back_step,
            jnp.zeros(query_tile.shape, jnp.float32),
            (key_tiles, value_tiles, kpos_tiles, kseg_tiles),
        )
        return ((sums[0] + key_parts, sums[1] + value_parts), query_grad)

    initial = (jnp.zeros(key_tiles.shape, jnp.float32), jnp.zeros(value_tiles.shape, jnp.float32))
    block_items = (
        query_split(query_heads, query_block),
        query_split(attended_grad, query_block),
        query_split(attended, query_block),
        log_totals,
        query_split(query_pos, query_block),
        query_split(query_seg, query_block),
    )
    (key_sum, value_sum), query_grads = lax.scan(block_grads, initial, block_items)
    key_rows = key_heads.shape[0]
    return (
        query_grads.reshape(query_heads.shape),
        key_sum.reshape(key_rows, -1),
        value_sum.reshape(key_rows, -1),
    )


def forward_pass(weights, inputs, places, tables, gather_pair):
    (
        attn_gain,
        query_full,
        key_complete,
        value_complete,
        out_full,
        ffn_gain,
        gate_full,
        up_full,
        down_full,
    ) = weights
    cosine_table, sine_table = tables
    count_of_rows = inputs.shape[0]
    normalized_input = rms_scale(inputs, attn_gain.astype(jnp.float32)).astype(jnp.bfloat16)
    query_lin = jnp.dot(normalized_input, query_full, preferred_element_type=jnp.float32)
    key_lin = jnp.dot(normalized_input, key_complete, preferred_element_type=jnp.float32)
    value_lin = jnp.dot(normalized_input, value_complete, preferred_element_type=jnp.float32)
    kv_heads = key_lin.shape[1] // HEAD_WIDTH
    query_rot = rotary_apply(
        query_lin.reshape(count_of_rows, -1, HEAD_WIDTH), cosine_table, sine_table
    ).astype(jnp.bfloat16)
    key_rot = (
        rotary_apply(key_lin.reshape(count_of_rows, kv_heads, HEAD_WIDTH), cosine_table, sine_table)
        .astype(jnp.bfloat16)
        .reshape(count_of_rows, -1)
    )
    value_low = value_lin.astype(jnp.bfloat16)
    keys_all, values_all = gather_pair((key_rot, value_low))
    group_size = query_rot.shape[1] // kv_heads
    query_heads = query_rot.reshape(count_of_rows, kv_heads, group_size, HEAD_WIDTH)
    key_heads = keys_all.reshape(-1, kv_heads, HEAD_WIDTH)
    value_heads = values_all.reshape(-1, kv_heads, HEAD_WIDTH)
    attended, log_totals = attention_forward(query_heads, key_heads, value_heads, places)
    attended_low = attended.reshape(count_of_rows, -1).astype(jnp.bfloat16)
    mixed = inputs + jnp.dot(attended_low, out_full, preferred_element_type=jnp.float32)
    normed_two = rms_scale(mixed, ffn_gain.astype(jnp.float32)).astype(jnp.bfloat16)
    gate = jnp.dot(normed_two, gate_full, preferred_element_type=jnp.float32)
    up_value = jnp.dot(normed_two, up_full, preferred_element_type=jnp.float32)
    hidden = (jax.nn.silu(gate) * up_value).astype(jnp.bfloat16)
    result = mixed + jnp.dot(hidden, down_full, preferred_element_type=jnp.float32)
    return (
        normalized_input,
        query_heads,
        key_heads,
        value_heads,
        attended,
        attended_low,
        log_totals,
        mixed,
        normed_two,
        gate,
        up_value,
        hidden,
        result,
    )


def local(
    tokens,
    block_map,
    attention_gain,
    query_weight,
    key_matrix,
    value_matrix,
    output_weight,
    feedforward_gain,
    gate_weight,
    up_weight,
    down_weight,
    out_grad,
):
    shards = (
        attention_gain,
        query_weight,
        key_matrix,
        value_matrix,
        output_weight,
        feedforward_gain,
        gate_weight,
        up_weight,
        down_weight,
    )
    count_of_rows = tokens.shape[1]
    ctx_rank = lax.axis_index("ctx")
    blocks = block_map[0]
    block_rows = count_of_rows // 2
    group_rows = blocks.shape[0] * block_rows
    prompt_rows = group_rows // 2
    natural = (
        blocks[:, None] * block_rows + jnp.arange(block_rows, dtype=jnp.int32)[None, :]
    ).reshape(-1)
    in_prompt = natural < prompt_rows
    key_pos = jnp.where(in_prompt, natural, prompt_rows + (natural - prompt_rows) % CONTINUE_LENGTH)
    key_seg = jnp.where(in_prompt, 0, 1 + (natural - prompt_rows) // CONTINUE_LENGTH)
    query_pos = lax.dynamic_slice_in_dim(key_pos, ctx_rank * count_of_rows, count_of_rows)
    query_seg = lax.dynamic_slice_in_dim(key_seg, ctx_rank * count_of_rows, count_of_rows)
    places = (query_pos, query_seg, key_pos, key_seg)
    cosine_table, sine_table = rope_tables(query_pos, HEAD_WIDTH)
    tables = (cosine_table, sine_table)
    inputs = tokens[0].astype(jnp.float32)
    full_weights = (
        lax.all_gather(shards[0], ("group", "wshard"), axis=0, tiled=True),
        lax.all_gather(shards[1], ("group", "wshard"), axis=0, tiled=True),
        lax.all_gather(shards[2], ("group", "wshard"), axis=0, tiled=True),
        lax.all_gather(shards[3], ("group", "wshard"), axis=0, tiled=True),
        lax.all_gather(shards[4], ("group", "wshard"), axis=0, tiled=True),
        lax.all_gather(shards[5], ("group", "wshard"), axis=0, tiled=True),
        lax.all_gather(shards[6], ("group", "wshard"), axis=0, tiled=True),
        lax.all_gather(shards[7], ("group", "wshard"), axis=0, tiled=True),
        lax.all_gather(shards[8], ("group", "wshard"), axis=0, tiled=True),
    )
    forward = forward_pass(
        full_weights,
        inputs,
        places,
        tables,
        lambda packed: jax.tree.map(
            lambda part, own: part.astype(own.dtype),
            lax.all_gather(as_sent(packed), "ctx", axis=0, tiled=True),
            packed,
        ),
    )
    layer_out = forward[12].astype(jnp.bfloat16)
    back_weights = (
        lax.all_gather(shards[0], ("group", "wshard"), axis=0, tiled=True),
        lax.all_gather(shards[1], ("group", "wshard"), axis=0, tiled=True),
        lax.all_gather(shards[2], ("group", "wshard"), axis=0, tiled=True),
        lax.all_gather(shards[3], ("group", "wshard"), axis=0, tiled=True),
        lax.all_gather(shards[4], ("group", "wshard"), axis=0, tiled=True),
        lax.all_gather(shards[5], ("group", "wshard"), axis=0, tiled=True),
        lax.all_gather(shards[6], ("group", "wshard"), axis=0, tiled=True),
        lax.all_gather(shards[7], ("group", "wshard"), axis=0, tiled=True),
        lax.all_gather(shards[8], ("group", "wshard"), axis=0, tiled=True),
    )
    saved = forward_pass(
        back_weights,
        inputs,
        places,
        tables,
        lambda packed: jax.tree.map(
            lambda part, own: part.astype(own.dtype),
            lax.all_gather(as_sent(packed), "ctx", axis=0, tiled=True),
            packed,
        ),
    )
    (
        normalized_input,
        query_heads,
        key_heads,
        value_heads,
        attended,
        attended_low,
        log_totals,
        mixed,
        normed_two,
        gate,
        up_value,
        hidden,
        result,
    ) = saved
    (
        attn_gain,
        query_full,
        key_complete,
        value_complete,
        out_full,
        ffn_gain,
        gate_full,
        up_full,
        down_full,
    ) = back_weights
    upstream = out_grad[0].astype(jnp.float32)
    ffn_grad = upstream.astype(jnp.bfloat16)
    grad_down = jnp.einsum("rf,rd->fd", hidden, ffn_grad, preferred_element_type=jnp.float32)
    hidden_grad = jnp.einsum("rd,fd->rf", ffn_grad, down_full, preferred_element_type=jnp.float32)
    gate_sigmoid = jax.nn.sigmoid(gate)
    gate_grad = (
        hidden_grad * up_value * gate_sigmoid * (1.0 + gate * (1.0 - gate_sigmoid))
    ).astype(jnp.bfloat16)
    up_grad = (hidden_grad * (gate * gate_sigmoid)).astype(jnp.bfloat16)
    grad_gate = jnp.einsum("rd,rf->df", normed_two, gate_grad, preferred_element_type=jnp.float32)
    grad_up = jnp.einsum("rd,rf->df", normed_two, up_grad, preferred_element_type=jnp.float32)
    normed_two_grad = jnp.einsum(
        "rf,df->rd", gate_grad, gate_full, preferred_element_type=jnp.float32
    ) + jnp.einsum("rf,df->rd", up_grad, up_full, preferred_element_type=jnp.float32)
    grad_ffn_gain, mixed_back = rms_back(mixed, ffn_gain.astype(jnp.float32), normed_two_grad)
    mixed_grad = upstream + mixed_back
    attn_grad = mixed_grad.astype(jnp.bfloat16)
    grad_out = jnp.einsum("rf,rd->fd", attended_low, attn_grad, preferred_element_type=jnp.float32)
    attended_grad = (
        jnp.einsum("rd,fd->rf", attn_grad, out_full, preferred_element_type=jnp.float32)
        .astype(jnp.bfloat16)
        .reshape(attended.shape)
    )
    query_grad, key_grad, value_grad = attention_backward(
        query_heads, key_heads, value_heads, places, attended_grad, attended, log_totals
    )
    key_local, value_local = (
        lax.psum_scatter(
            key_grad.astype(jnp.bfloat16), "ctx", scatter_dimension=0, tiled=True
        ).astype(jnp.float32),
        lax.psum_scatter(
            value_grad.astype(jnp.bfloat16), "ctx", scatter_dimension=0, tiled=True
        ).astype(jnp.float32),
    )
    query_lin_grad = (
        rotary_apply(query_grad.reshape(count_of_rows, -1, HEAD_WIDTH), cosine_table, -sine_table)
        .reshape(count_of_rows, -1)
        .astype(jnp.bfloat16)
    )
    key_lin_grad = (
        rotary_apply(key_local.reshape(count_of_rows, -1, HEAD_WIDTH), cosine_table, -sine_table)
        .reshape(count_of_rows, -1)
        .astype(jnp.bfloat16)
    )
    value_lin_grad = value_local.astype(jnp.bfloat16)
    grad_query = jnp.einsum(
        "rd,rf->df", normalized_input, query_lin_grad, preferred_element_type=jnp.float32
    )
    grad_key = jnp.einsum(
        "rd,rf->df", normalized_input, key_lin_grad, preferred_element_type=jnp.float32
    )
    grad_value = jnp.einsum(
        "rd,rf->df", normalized_input, value_lin_grad, preferred_element_type=jnp.float32
    )
    normed_grad = jnp.einsum(
        "rf,df->rd", query_lin_grad, query_full, preferred_element_type=jnp.float32
    )
    normed_grad = normed_grad + jnp.einsum(
        "rf,df->rd", key_lin_grad, key_complete, preferred_element_type=jnp.float32
    )
    normed_grad = normed_grad + jnp.einsum(
        "rf,df->rd", value_lin_grad, value_complete, preferred_element_type=jnp.float32
    )
    grad_attn_gain, input_back = rms_back(inputs, attn_gain.astype(jnp.float32), normed_grad)
    input_grad = mixed_grad + input_back
    partial_grads = (
        grad_attn_gain,
        grad_query,
        grad_key,
        grad_value,
        grad_out,
        grad_ffn_gain,
        grad_gate,
        grad_up,
        grad_down,
    )
    reduced = (
        lax.psum_scatter(
            partial_grads[0].astype(jnp.bfloat16),
            ("group", "wshard"),
            scatter_dimension=0,
            tiled=True,
        ).astype(jnp.float32),
        lax.psum_scatter(
            partial_grads[1].astype(jnp.bfloat16),
            ("group", "wshard"),
            scatter_dimension=0,
            tiled=True,
        ).astype(jnp.float32),
        lax.psum_scatter(
            partial_grads[2].astype(jnp.bfloat16),
            ("group", "wshard"),
            scatter_dimension=0,
            tiled=True,
        ).astype(jnp.float32),
        lax.psum_scatter(
            partial_grads[3].astype(jnp.bfloat16),
            ("group", "wshard"),
            scatter_dimension=0,
            tiled=True,
        ).astype(jnp.float32),
        lax.psum_scatter(
            partial_grads[4].astype(jnp.bfloat16),
            ("group", "wshard"),
            scatter_dimension=0,
            tiled=True,
        ).astype(jnp.float32),
        lax.psum_scatter(
            partial_grads[5].astype(jnp.bfloat16),
            ("group", "wshard"),
            scatter_dimension=0,
            tiled=True,
        ).astype(jnp.float32),
        lax.psum_scatter(
            partial_grads[6].astype(jnp.bfloat16),
            ("group", "wshard"),
            scatter_dimension=0,
            tiled=True,
        ).astype(jnp.float32),
        lax.psum_scatter(
            partial_grads[7].astype(jnp.bfloat16),
            ("group", "wshard"),
            scatter_dimension=0,
            tiled=True,
        ).astype(jnp.float32),
        lax.psum_scatter(
            partial_grads[8].astype(jnp.bfloat16),
            ("group", "wshard"),
            scatter_dimension=0,
            tiled=True,
        ).astype(jnp.float32),
    )
    summed = (
        lax.psum(reduced[0].astype(jnp.bfloat16), "ctx").astype(jnp.float32),
        lax.psum(reduced[1].astype(jnp.bfloat16), "ctx").astype(jnp.float32),
        lax.psum(reduced[2].astype(jnp.bfloat16), "ctx").astype(jnp.float32),
        lax.psum(reduced[3].astype(jnp.bfloat16), "ctx").astype(jnp.float32),
        lax.psum(reduced[4].astype(jnp.bfloat16), "ctx").astype(jnp.float32),
        lax.psum(reduced[5].astype(jnp.bfloat16), "ctx").astype(jnp.float32),
        lax.psum(reduced[6].astype(jnp.bfloat16), "ctx").astype(jnp.float32),
        lax.psum(reduced[7].astype(jnp.bfloat16), "ctx").astype(jnp.float32),
        lax.psum(reduced[8].astype(jnp.bfloat16), "ctx").astype(jnp.float32),
    )
    gain_attn, gain_ffn = (summed[0], summed[5])
    matrices = (summed[1], summed[2], summed[3], summed[4], summed[6], summed[7], summed[8])
    return (
        layer_out[None],
        input_grad[None],
        gain_attn,
        matrices[0],
        matrices[1],
        matrices[2],
        matrices[3],
        gain_ffn,
        matrices[4],
        matrices[5],
        matrices[6],
    )


def solution(mesh):
    return jax.shard_map(
        local,
        mesh=mesh,
        in_specs=(
            P(("group", "wshard"), "ctx", None),
            P(("group", "wshard"), None),
            P(("group", "wshard")),
            P(("group", "wshard"), None),
            P(("group", "wshard"), None),
            P(("group", "wshard"), None),
            P(("group", "wshard"), None),
            P(("group", "wshard")),
            P(("group", "wshard"), None),
            P(("group", "wshard"), None),
            P(("group", "wshard"), None),
            P(("group", "wshard"), "ctx", None),
        ),
        out_specs=(
            P(("group", "wshard"), "ctx", None),
            P(("group", "wshard"), "ctx", None),
            P(("group", "wshard")),
            P(("group", "wshard"), None),
            P(("group", "wshard"), None),
            P(("group", "wshard"), None),
            P(("group", "wshard"), None),
            P(("group", "wshard")),
            P(("group", "wshard"), None),
            P(("group", "wshard"), None),
            P(("group", "wshard"), None),
        ),
        check_vma=False,
    )
```

profile of v0, /device:TPU:8, one launch (start us, length us, event | category | flops | bytes accessed | tf_op | source)
XLA Modules:
  0.0 3404.5 jit_solution(3869372233269099151)
XLA Ops:
  133.1 40.8 %all-gather.12.cloned.1.call-done = bf16[4096,384]{1,0:T(8,128)(2,1)} async-done(((bf16[2048,384]{1,0:T(8,128)(2,1)}), bf16[4096,384]{1,0:T(8,128)(2,1)}) %all-gather.12.cloned.1.call-update) | async-done | bytes 3145744 | tf_op jit(solution)/shard_map/all_gather | solution.py:361
  181.0 38.3 %all-gather.8.cloned.1.call-done = bf16[1152,1152]{1,0:T(8,128)(2,1)} async-done(((bf16[72,1152]{1,0:T(8,128)(2,1)}), bf16[1152,1152]{1,0:T(8,128)(2,1)}) %all-gather.8.cloned.1.call-update) | async-done | bytes 2654224 | tf_op jit(solution)/shard_map/all_gather | solution.py:345
  251.7 605.2 %while.139 = (s32[]{:T(128)}, f32[4,512,6,3,64]{1,4,3,2,0:T(8,128)}, f32[4,6,3,512]{3,2,1,0:T(4,128)}, s32[4,512]{1,0:T(4,128)}, s32[4,512]{1,0:T(4,128)}, /*ind...) while((s32[]{:T(128)}, f32[4,512,6,3,64]{1,4,3,2,0:T(8,128)}, ...), condition=%wide.region_29.30_spmd.clone.clone.clone, body=%wide.region_16.0_spmd.clone.clone.sunk.clone | while | flops 938675712 | bytes 37675344 | solution.py:152
  290.1 68.6 %while.138 = (s32[]{:T(128)}, f32[512,6,3,64]{0,3,2,1:T(8,128)S(1)}, s32[16,256]{1,0:T(8,128)}, s32[512]{0:T(512)S(1)}, s32[16,256]{1,0:T(8,128)}, /*index=5*/s3...) while((s32[]{:T(128)}, f32[512,6,3,64]{0,3,2,1:T(8,128)S(1)}, ...), condition=%wide.region_28.28_spmd, body=%wide.region_24.27_spmd.sunk | while | flops 617021696 | bytes 6614715 | solution.py:145
  362.7 45.0 %while.137 = (s32[]{:T(128)}, f32[6,3,512]{2,1,0:T(4,128)S(1)}, f32[6,3,512]{2,1,0:T(4,128)S(1)}, s32[16,256]{1,0:T(8,128)S(1)}, s32[512]{0:T(512)S(1)}, /*index...) while((s32[]{:T(128)}, f32[6,3,512]{2,1,0:T(4,128)S(1)}, ...), condition=%wide.region_23.23_spmd, body=%wide.region_17.22_spmd.sunk | while | flops 321538304 | bytes 21134540 | solution.py:124
  408.7 77.7 %while.138 = (s32[]{:T(128)}, f32[512,6,3,64]{0,3,2,1:T(8,128)S(1)}, s32[16,256]{1,0:T(8,128)}, s32[512]{0:T(512)S(1)}, s32[16,256]{1,0:T(8,128)}, /*index=5*/s3...) while((s32[]{:T(128)}, f32[512,6,3,64]{0,3,2,1:T(8,128)S(1)}, ...), condition=%wide.region_28.28_spmd, body=%wide.region_24.27_spmd.sunk | while | flops 617021696 | bytes 6614715 | solution.py:145
  490.5 74.2 %while.137 = (s32[]{:T(128)}, f32[6,3,512]{2,1,0:T(4,128)S(1)}, f32[6,3,512]{2,1,0:T(4,128)S(1)}, s32[16,256]{1,0:T(8,128)S(1)}, s32[512]{0:T(512)S(1)}, /*index...) while((s32[]{:T(128)}, f32[6,3,512]{2,1,0:T(4,128)S(1)}, ...), condition=%wide.region_23.23_spmd, body=%wide.region_17.22_spmd.sunk | while | flops 321538304 | bytes 21134540 | solution.py:124
  565.7 105.0 %while.138 = (s32[]{:T(128)}, f32[512,6,3,64]{0,3,2,1:T(8,128)S(1)}, s32[16,256]{1,0:T(8,128)}, s32[512]{0:T(512)S(1)}, s32[16,256]{1,0:T(8,128)}, /*index=5*/s3...) while((s32[]{:T(128)}, f32[512,6,3,64]{0,3,2,1:T(8,128)S(1)}, ...), condition=%wide.region_28.28_spmd, body=%wide.region_24.27_spmd.sunk | while | flops 617021696 | bytes 6614715 | solution.py:145
  674.7 74.2 %while.137 = (s32[]{:T(128)}, f32[6,3,512]{2,1,0:T(4,128)S(1)}, f32[6,3,512]{2,1,0:T(4,128)S(1)}, s32[16,256]{1,0:T(8,128)S(1)}, s32[512]{0:T(512)S(1)}, /*index...) while((s32[]{:T(128)}, f32[6,3,512]{2,1,0:T(4,128)S(1)}, ...), condition=%wide.region_23.23_spmd, body=%wide.region_17.22_spmd.sunk | while | flops 321538304 | bytes 21134540 | solution.py:124
  750.0 105.0 %while.138 = (s32[]{:T(128)}, f32[512,6,3,64]{0,3,2,1:T(8,128)S(1)}, s32[16,256]{1,0:T(8,128)}, s32[512]{0:T(512)S(1)}, s32[16,256]{1,0:T(8,128)}, /*index=5*/s3...) while((s32[]{:T(128)}, f32[512,6,3,64]{0,3,2,1:T(8,128)S(1)}, ...), condition=%wide.region_28.28_spmd, body=%wide.region_24.27_spmd.sunk | while | flops 617021696 | bytes 6614715 | solution.py:145
  933.0 37.9 %multiply_convert_fusion.1 = (bf16[2048,3072]{1,0:T(8,128)(2,1)}, bf16[2048,3072]{1,0:T(8,128)(2,1)}) fusion(f32[2048,3072]{1,0:T(8,128)} %fusion.181, f32[2048,3072]{1,0:T(8,128)} %fusion.180, bf16[3072,1152]{1,0:T(8,128)(2,1)} %all-gather.20.cloned.1.call-done, bf16[1,2048,1152]{2,1,0:T(8,128)(2,1)} %param.49), kind=kOutput, calls=%fused_computation.168 | convolution fusion | flops 14577303552 | bytes 87293952 | tf_op jit(solution)/shard_map/rd,fd->rf/dot_general | solution.py:417
  1060.5 1030.9 %while.141 = (s32[]{:T(128)}, f32[16,256,6,64]{1,3,2,0:T(8,128)}, f32[16,256,6,64]{1,3,2,0:T(8,128)}, f32[4,512,6,3,64]{1,0,4,3,2:T(4,128)}, s32[4,512]{1,0:T(4,...) while((s32[]{:T(128)}, f32[16,256,6,64]{1,3,2,0:T(8,128)}, ...), condition=%wide.region_38.39_spmd.clone.clone.clone.clone, body=%wide.region_32.38_spmd.clone.clone.clone.sunk.clone | while | flops 1548352768 | bytes 149284080 | solution.py:233
  1096.6 101.6 %while.140 = (s32[]{:T(128)}, f32[512,6,3,64]{0,3,2,1:T(8,128)S(1)}, f32[16,256,6,64]{1,3,2,0:T(8,128)}, f32[16,256,6,64]{1,3,2,0:T(8,128)}, s32[16,256]{1,0:T(8...) while((s32[]{:T(128)}, f32[512,6,3,64]{0,3,2,1:T(8,128)S(1)}, ...), condition=%wide.region_37.37_spmd, body=%wide.region_33.36_spmd.sunk | while | flops 1540194560 | bytes 60908392 | solution.py:217
  1211.6 46.0 %dynamic_update_slice.48 = f32[4,512,6,3,64]{1,0,4,3,2:T(4,128)} dynamic-update-slice(f32[4,512,6,3,64]{1,0,4,3,2:T(4,128)} %get-tuple-element.2590, f32[1,512,6,3,64]{1,0,4,3,2:T(1,128)} %copy.208, s32[]{:T(128)} %get-tuple-element.2587, s32[]{:T(128)} %constant.263.clone.1..sunk.5, s32[]{:T(128)} %constant.263.clone.1..sunk.5, s32[]{:T(128)} %constant.263.clone.1..sunk.5, ...) | dynamic-update-slice | bytes 4718596 | tf_op jit(solution)/shard_map/while/body/jit(dynamic_update_index_in_dim)/dynamic_update_slice | solution.py:152
  1293.5 127.1 %while.140 = (s32[]{:T(128)}, f32[512,6,3,64]{0,3,2,1:T(8,128)S(1)}, f32[16,256,6,64]{1,3,2,0:T(8,128)}, f32[16,256,6,64]{1,3,2,0:T(8,128)}, s32[16,256]{1,0:T(8...) while((s32[]{:T(128)}, f32[512,6,3,64]{0,3,2,1:T(8,128)S(1)}, ...), condition=%wide.region_37.37_spmd, body=%wide.region_33.36_spmd.sunk | while | flops 1540194560 | bytes 60908392 | solution.py:217
  1438.6 46.0 %dynamic_update_slice.48 = f32[4,512,6,3,64]{1,0,4,3,2:T(4,128)} dynamic-update-slice(f32[4,512,6,3,64]{1,0,4,3,2:T(4,128)} %get-tuple-element.2590, f32[1,512,6,3,64]{1,0,4,3,2:T(1,128)} %copy.208, s32[]{:T(128)} %get-tuple-element.2587, s32[]{:T(128)} %constant.263.clone.1..sunk.5, s32[]{:T(128)} %constant.263.clone.1..sunk.5, s32[]{:T(128)} %constant.263.clone.1..sunk.5, ...) | dynamic-update-slice | bytes 4718596 | tf_op jit(solution)/shard_map/while/body/jit(dynamic_update_index_in_dim)/dynamic_update_slice | solution.py:152
  1520.4 203.4 %while.140 = (s32[]{:T(128)}, f32[512,6,3,64]{0,3,2,1:T(8,128)S(1)}, f32[16,256,6,64]{1,3,2,0:T(8,128)}, f32[16,256,6,64]{1,3,2,0:T(8,128)}, s32[16,256]{1,0:T(8...) while((s32[]{:T(128)}, f32[512,6,3,64]{0,3,2,1:T(8,128)S(1)}, ...), condition=%wide.region_37.37_spmd, body=%wide.region_33.36_spmd.sunk | while | flops 1540194560 | bytes 60908392 | solution.py:217
  1741.9 46.0 %dynamic_update_slice.48 = f32[4,512,6,3,64]{1,0,4,3,2:T(4,128)} dynamic-update-slice(f32[4,512,6,3,64]{1,0,4,3,2:T(4,128)} %get-tuple-element.2590, f32[1,512,6,3,64]{1,0,4,3,2:T(1,128)} %copy.208, s32[]{:T(128)} %get-tuple-element.2587, s32[]{:T(128)} %constant.263.clone.1..sunk.5, s32[]{:T(128)} %constant.263.clone.1..sunk.5, s32[]{:T(128)} %constant.263.clone.1..sunk.5, ...) | dynamic-update-slice | bytes 4718596 | tf_op jit(solution)/shard_map/while/body/jit(dynamic_update_index_in_dim)/dynamic_update_slice | solution.py:152
  1823.7 203.4 %while.140 = (s32[]{:T(128)}, f32[512,6,3,64]{0,3,2,1:T(8,128)S(1)}, f32[16,256,6,64]{1,3,2,0:T(8,128)}, f32[16,256,6,64]{1,3,2,0:T(8,128)}, s32[16,256]{1,0:T(8...) while((s32[]{:T(128)}, f32[512,6,3,64]{0,3,2,1:T(8,128)S(1)}, ...), condition=%wide.region_37.37_spmd, body=%wide.region_33.36_spmd.sunk | while | flops 1540194560 | bytes 60908392 | solution.py:217
  2045.2 46.0 %dynamic_update_slice.48 = f32[4,512,6,3,64]{1,0,4,3,2:T(4,128)} dynamic-update-slice(f32[4,512,6,3,64]{1,0,4,3,2:T(4,128)} %get-tuple-element.2590, f32[1,512,6,3,64]{1,0,4,3,2:T(1,128)} %copy.208, s32[]{:T(128)} %get-tuple-element.2587, s32[]{:T(128)} %constant.263.clone.1..sunk.5, s32[]{:T(128)} %constant.263.clone.1..sunk.5, s32[]{:T(128)} %constant.263.clone.1..sunk.5, ...) | dynamic-update-slice | bytes 4718596 | tf_op jit(solution)/shard_map/while/body/jit(dynamic_update_index_in_dim)/dynamic_update_slice | solution.py:152
  2108.1 211.1 %reduce-scatter.18.cloned.1.call-done = bf16[2048,384]{0,1:T(8,128)(2,1)} async-done(((bf16[4096,384]{0,1:T(8,128)(2,1)}), bf16[2048,384]{0,1:T(8,128)(2,1)}) %reduce-scatter.18.cloned.1.call-update) | async-done | bytes 1572880 | tf_op jit(solution)/shard_map/reduce_scatter | solution.py:441
  2326.8 38.1 %reduce-scatter.20.cloned.1.call-done = bf16[2048,384]{0,1:T(8,128)(2,1)} async-done(((bf16[4096,384]{0,1:T(8,128)(2,1)}), bf16[2048,384]{0,1:T(8,128)(2,1)}) %reduce-scatter.20.cloned.1.call-update) | async-done | bytes 1572880 | tf_op jit(solution)/shard_map/reduce_scatter | solution.py:444
  2457.1 597.0 %while.136 = (s32[]{:T(128)}, bf16[4,512,6,3,64]{1,4,3,2,0:T(8,128)(2,1)}, s32[4,512]{1,0:T(4,128)}, s32[4,512]{1,0:T(4,128)}, bf16[4,512,6,3,64]{1,4,3,2,0:T(8,...) while((s32[]{:T(128)}, ...), condition=%wide.region_14.15_spmd.clone.clone.clone, body=%wide.region_1.14_spmd.clone.clone.sunk.clone | while | flops 938675712 | bytes 37613384 | solution.py:152
  2495.5 67.1 %while.135 = (s32[]{:T(128)}, f32[512,6,3,64]{0,3,2,1:T(8,128)S(1)}, s32[16,256]{1,0:T(8,128)}, s32[512]{0:T(512)S(1)}, s32[16,256]{1,0:T(8,128)}, /*index=5*/s3...) while((s32[]{:T(128)}, f32[512,6,3,64]{0,3,2,1:T(8,128)S(1)}, ...), condition=%wide.region_13.13_spmd, body=%wide.region_9.12_spmd.sunk | while | flops 617021696 | bytes 6614715 | solution.py:145
  2566.1 44.9 %while.134 = (s32[]{:T(128)}, f32[6,3,512]{2,1,0:T(4,128)S(1)}, f32[6,3,512]{2,1,0:T(4,128)S(1)}, s32[16,256]{1,0:T(8,128)S(1)}, s32[512]{0:T(512)S(1)}, /*index...) while((s32[]{:T(128)}, f32[6,3,512]{2,1,0:T(4,128)S(1)}, ...), condition=%wide.region_8.8_spmd, body=%wide.region_2.7_spmd.sunk | while | flops 321538304 | bytes 21134540 | solution.py:124
  2612.1 76.4 %while.135 = (s32[]{:T(128)}, f32[512,6,3,64]{0,3,2,1:T(8,128)S(1)}, s32[16,256]{1,0:T(8,128)}, s32[512]{0:T(512)S(1)}, s32[16,256]{1,0:T(8,128)}, /*index=5*/s3...) while((s32[]{:T(128)}, f32[512,6,3,64]{0,3,2,1:T(8,128)S(1)}, ...), condition=%wide.region_13.13_spmd, body=%wide.region_9.12_spmd.sunk | while | flops 617021696 | bytes 6614715 | solution.py:145
  2691.9 74.3 %while.134 = (s32[]{:T(128)}, f32[6,3,512]{2,1,0:T(4,128)S(1)}, f32[6,3,512]{2,1,0:T(4,128)S(1)}, s32[16,256]{1,0:T(8,128)S(1)}, s32[512]{0:T(512)S(1)}, /*index...) while((s32[]{:T(128)}, f32[6,3,512]{2,1,0:T(4,128)S(1)}, ...), condition=%wide.region_8.8_spmd, body=%wide.region_2.7_spmd.sunk | while | flops 321538304 | bytes 21134540 | solution.py:124
  2767.2 103.5 %while.135 = (s32[]{:T(128)}, f32[512,6,3,64]{0,3,2,1:T(8,128)S(1)}, s32[16,256]{1,0:T(8,128)}, s32[512]{0:T(512)S(1)}, s32[16,256]{1,0:T(8,128)}, /*index=5*/s3...) while((s32[]{:T(128)}, f32[512,6,3,64]{0,3,2,1:T(8,128)S(1)}, ...), condition=%wide.region_13.13_spmd, body=%wide.region_9.12_spmd.sunk | while | flops 617021696 | bytes 6614715 | solution.py:145
  2874.2 74.2 %while.134 = (s32[]{:T(128)}, f32[6,3,512]{2,1,0:T(4,128)S(1)}, f32[6,3,512]{2,1,0:T(4,128)S(1)}, s32[16,256]{1,0:T(8,128)S(1)}, s32[512]{0:T(512)S(1)}, /*index...) while((s32[]{:T(128)}, f32[6,3,512]{2,1,0:T(4,128)S(1)}, ...), condition=%wide.region_8.8_spmd, body=%wide.region_2.7_spmd.sunk | while | flops 321538304 | bytes 21134540 | solution.py:124
  2949.3 103.5 %while.135 = (s32[]{:T(128)}, f32[512,6,3,64]{0,3,2,1:T(8,128)S(1)}, s32[16,256]{1,0:T(8,128)}, s32[512]{0:T(512)S(1)}, s32[16,256]{1,0:T(8,128)}, /*index=5*/s3...) while((s32[]{:T(128)}, f32[512,6,3,64]{0,3,2,1:T(8,128)S(1)}, ...), condition=%wide.region_13.13_spmd, body=%wide.region_9.12_spmd.sunk | while | flops 617021696 | bytes 6614715 | solution.py:145
  3203.1 100.0 %all-reduce.8 = (bf16[1152]{0:T(1024)(128)(2,1)S(1)}, bf16[1152]{0:T(1024)(128)(2,1)S(1)}) all-reduce(bf16[1152]{0:T(1024)(128)(2,1)S(1)} %get-tuple-element.1183, bf16[1152]{0:T(1024)(128)(2,1)S(1)} %copy-done.40), channel_id=4, replica_groups=mesh['group'=4,'ctx'=2,'wshard'=4] {'group','wshard'}, use_global_device_ids=true, to_apply=%region_43.44.clone | all-reduce | flops 2304 | bytes 9216
  3336.6 51.5 %all-reduce.17.cloned.1.call-done = (bf16[72,1152]{1,0:T(8,128)(2,1)}, bf16[72,1152]{1,0:T(8,128)(2,1)}, bf16[72,3072]{1,0:T(8,128)(2,1)}, bf16[72,3072]{1,0:T(8,128)(2,1)}, bf16[192,1152]{1,0:T(8,128)(2,1)}) async-done(((bf16[72,1152]{1,0:T(8,128)(2,1)}, bf16[72,1152]{1,0:T(8,128)(2,1)}, bf16[72,3072]{1,0:T(8,128)(2,1)}, bf16[72,3072]{1,0:T(8,128)(2,1)}, bf16[192,1152]{1,0:T(8,128)(2,1)}), ...) | async-done | bytes 1658896 | tf_op jit(solution)/shard_map/psum | solution.py:548
  (2521 shorter events, 3354.9 us)
Async XLA Ops:
  7.2 120.3 %all-gather.10.cloned.1.call-start = ((), (), s32[]{:S(2)}) async-start(), calls=%async_computation.10 | async-start | bytes 4718592 | tf_op jit(solution)/shard_map/all_gather | solution.py:361
  8.1 38.3 %copy-start.36 = (bf16[72,384]{1,0:T(8,128)(2,1)S(1)}, bf16[72,384]{1,0:T(8,128)(2,1)}, u32[]{:S(2)}) copy-start(bf16[72,384]{1,0:T(8,128)(2,1)} %param.42) | copy-start | bytes 165892
  18.7 204.7 %copy-start.28 = (f32[2048]{0:T(1024)}, f32[2048]{0:T(1024)S(1)}, u32[]{:S(2)}) copy-start(f32[2048]{0:T(1024)S(1)} %get-tuple-element.1432) | copy-start | bytes 24580
  46.4 177.0 %copy-start.31 = (f32[1152]{0:T(1024)}, f32[1152]{0:T(1024)S(1)}, u32[]{:S(2)}) copy-start(f32[1152]{0:T(1024)S(1)} %convert_element_type.245) | copy-start | bytes 13828
  74.4 157.8 %copy-start.6 = (f32[2048,32]{0,1:T(8,128)}, f32[2048,32]{0,1:T(8,128)S(1)}, u32[]{:S(2)}) copy-start(f32[2048,32]{0,1:T(8,128)S(1)} %get-tuple-element.1430) | copy-start | bytes 786436
  81.0 92.9 %all-gather.12.cloned.1.call-start = ((), (), s32[]{:S(2)}) async-start(), calls=%async_computation.11 | async-start | bytes 4718592 | tf_op jit(solution)/shard_map/all_gather | solution.py:361
  110.1 109.2 %all-gather.8.cloned.1.call-start = ((), (), s32[]{:S(2)}) async-start(), calls=%async_computation.9 | async-start | bytes 2820096 | tf_op jit(solution)/shard_map/all_gather | solution.py:345
  110.9 758.7 %all-gather.14.cloned.1.call-start = ((), (), s32[]{:S(2)}) async-start(), calls=%async_computation.12 | async-start | bytes 2820096 | tf_op jit(solution)/shard_map/all_gather | solution.py:348
  111.5 775.4 %all-gather.18.cloned.1.call-start = ((), (), s32[]{:S(2)}) async-start(), calls=%async_computation.14 | async-start | bytes 7520256 | tf_op jit(solution)/shard_map/all_gather | solution.py:351
  112.0 798.0 %all-gather.16.cloned.1.call-start = ((), (), s32[]{:S(2)}) async-start(), calls=%async_computation.13 | async-start | bytes 7520256 | tf_op jit(solution)/shard_map/all_gather | solution.py:350
  112.6 820.4 %all-gather.20.cloned.1.call-start = ((), (), s32[]{:S(2)}) async-start(), calls=%async_computation.15 | async-start | bytes 7520256 | tf_op jit(solution)/shard_map/all_gather | solution.py:352
  113.4 2205.8 %reduce-scatter.18.cloned.1.call-start = ((), (), s32[]{:S(2)}) async-start(), calls=%async_computation.16 | async-start | bytes 4718592 | tf_op jit(solution)/shard_map/reduce_scatter | solution.py:441
  970.9 48.1 %slice-start.11 = ((s8[4718592]{0:T(1024)(128)(4,1)}), s8[4194304]{0:T(1024)(128)(4,1)S(1)}, s32[]{:S(2)}) async-start(s8[4718592]{0:T(1024)(128)(4,1)} %bitcast.444), calls=%async_computation.38 | async-start | bytes 8388608
  992.0 27.1 slice-start.8
  992.0 27.1 slice-start.9
  992.0 27.1 slice-start.10
  992.0 27.1 slice-start.12
  992.0 27.1 copy-start.39
  2099.6 265.3 %reduce-scatter.20.cloned.1.call-start = ((), (), s32[]{:S(2)}) async-start(), calls=%async_computation.17 | async-start | bytes 4718592 | tf_op jit(solution)/shard_map/reduce_scatter | solution.py:444
  2104.9 216.3 %copy-start.7 = (f32[2048,32]{0,1:T(8,128)S(1)}, f32[2048,32]{0,1:T(8,128)}, u32[]{:S(2)}) copy-start(f32[2048,32]{0,1:T(8,128)} %copy-done.6) | copy-start | bytes 786436
  2104.9 216.3 %copy-start.14 = (f32[2048,32]{0,1:T(8,128)S(1)}, f32[2048,32]{0,1:T(8,128)}, u32[]{:S(2)}) copy-start(f32[2048,32]{0,1:T(8,128)} %get-tuple-element.1428) | copy-start | bytes 786436
  2108.0 1196.2 %reduce-scatter.30.cloned.1.call-start = ((), (), s32[]{:S(2)}) async-start(), calls=%async_computation.22 | async-start | bytes 940032
  2326.5 977.7 %reduce-scatter.32.cloned.1.call-start = ((), (), s32[]{:S(2)}) async-start(), calls=%async_computation.23 | async-start | bytes 940032
  2371.4 933.0 %reduce-scatter.34.cloned.1.call-start = ((), (), s32[]{:S(2)}) async-start(), calls=%async_computation.24 | async-start | bytes 2820096
  2383.5 920.8 %reduce-scatter.28.cloned.1.call-start = ((), (), s32[]{:S(2)}) async-start(), calls=%async_computation.21 | async-start | bytes 2820096
  2412.3 892.1 %reduce-scatter.22.cloned.1.call-start = ((), (), s32[]{:S(2)}) async-start(), calls=%async_computation.18 | async-start | bytes 7520256 | tf_op jit(solution)/shard_map/reduce_scatter | solution.py:527
  2433.1 871.3 %reduce-scatter.24.cloned.1.call-start = ((), (), s32[]{:S(2)}) async-start(), calls=%async_computation.19 | async-start | bytes 7520256 | tf_op jit(solution)/shard_map/reduce_scatter | solution.py:533
  2456.9 847.5 %reduce-scatter.26.cloned.1.call-start = ((), (), s32[]{:S(2)}) async-start(), calls=%async_computation.20 | async-start | bytes 7520256 | tf_op jit(solution)/shard_map/reduce_scatter | solution.py:539
  3101.1 230.2 %all-reduce.15.cloned.1.call-start = ((), (), s32[]{:S(2)}) async-start(), calls=%async_computation.25 | async-start | bytes 223232 | tf_op jit(solution)/shard_map/psum | solution.py:547
  3178.4 18.1 slice-start.6
  3196.5 108.3 %copy-start.38 = (f32[2048]{0:T(1024)S(1)}, f32[2048]{0:T(1024)}, u32[]{:S(2)}) copy-start(f32[2048]{0:T(1024)} %get-tuple-element.1431) | copy-start | bytes 24580
  3304.2 83.9 %all-reduce.17.cloned.1.call-start = ((), (), s32[]{:S(2)}) async-start(), calls=%async_computation.26 | async-start | bytes 3317760 | tf_op jit(solution)/shard_map/psum | solution.py:548
  (156 other events, 456.6 us)
Sparse Core Ops, SparseCore 0:
  81.2 46.2 all-gather.9
  129.0 44.9 all-gather.11
  176.1 43.1 all-gather.7
  221.3 42.0 all-gather.13
  265.5 65.2 all-gather.17
  332.9 65.0 all-gather.15
  400.3 65.1 all-gather.19
  2099.7 219.3 reduce-scatter.17
  2321.5 43.3 reduce-scatter.19
  2368.9 55.9 reduce-scatter.29
  2428.6 55.1 reduce-scatter.31
  2487.5 62.4 reduce-scatter.33
  2554.4 62.9 reduce-scatter.27
  2621.2 89.3 reduce-scatter.21
  2715.0 89.5 reduce-scatter.23
  3101.2 165.4 reduce-scatter.25
  3304.4 26.9 all-reduce.14
  3334.0 54.0 all-reduce.16
where the time goes:
time: 3450 us; the launch traced here: 3400 us
  matrix products  1070 us (31%)
  other arithmetic  846 us (25%)
  local copies, waits for them, and re-layouts  670 us (19%)
  waiting for transfers between devices  392 us (11%)
  loops' own time  232 us (7%)
  blocking collectives  173 us (5%)
    dot_general x52, matrix products, out_open_tile(): jnp.einsum('hgrk,khd->rhgd', probabilities, value_tile, preferred_element...  237 us
    reduce_scatter x1, waiting for transfers between devices, local(): lax.psum_scatter(key_grad.astype(jnp.bfloat16), 'ctx', scatter_dimension=...  211 us
    dynamic_update_slice x16, local copies, waits for them, and re-layouts, attention_forward(): lax.map(one_block, (query_split(query_heads, query_block), query_split(qu...  211 us
    reduce_or x128, other arithmetic, out_step(): jnp.any(allowed)  198 us
    dot_general x78, matrix products, tile_scores(): jnp.einsum('rhgd,khd->hgrk', query_tile, key_tile, preferred_element_type...  195 us
    eq x320, other arithmetic, visible(): key_seg[None, :] == 0  142 us
    dynamic_slice x320, local copies, waits for them, and re-layouts, one_block(): lax.scan(lse_step, initial, (key_tiles, kpos_tiles, kseg_tiles))  136 us
    unnamed x2, blocking collectives  126 us
  transfers between devices with their start and end apart: 18, of which 7 were waited for; matrix products, arithmetic and copies ran while one was open for 42% of the time, Pallas kernels for 0%

commit v1 on v0

--- a/solution.py
+++ b/solution.py
@@ -1,13 +1,565 @@
+import functools
 import jax
 import jax.numpy as jnp
 from jax import lax
+from jax.experimental import pallas as pl
+from jax.experimental.pallas import tpu as pltpu
 from jax.sharding import PartitionSpec as P
 
+f32 = jnp.float32
+bf16 = jnp.bfloat16
 HEAD_WIDTH = 64
 CONTINUE_LENGTH = 512
-
-
 norm_eps = 1e-05
+LOG2E = 1.4426950408889634
+LN2 = 0.6931471805599453
+MIB = 2**20
+
+
+def contract(a, b, dim_a, dim_b):
+    return lax.dot_general(
+        a, b, (((dim_a,), (dim_b,)), ((), ())), preferred_element_type=f32
+    )
+
+
+def resident(shape):
+    zeros = (0,) * len(shape)
+    return pl.BlockSpec(shape, lambda *_: zeros, pipeline_mode=pl.Buffered(1))
+
+
+def project_kernel(x_ref, gain_ref, w_ref, cos_ref, sin_ref, q_ref, k_ref, v_ref, h_ref, nq_ref, nk_ref):
+    x = x_ref[...].astype(f32)
+    inverse = lax.rsqrt(jnp.mean(x * x, axis=-1, keepdims=True) + norm_eps)
+    h = (x * inverse * gain_ref[...]).astype(bf16)
+    h_ref[...] = h
+    q_rows, kv_rows = q_ref.shape[0], k_ref.shape[0]
+    half = HEAD_WIDTH // 2
+    scale = LOG2E * HEAD_WIDTH**-0.5
+    cos, sin = cos_ref[...], sin_ref[...]
+
+    def rotated(lin, out_ref, cos, sin):
+        worst = jnp.zeros((1, lin.shape[1]), f32)
+        for head in range(lin.shape[0] // HEAD_WIDTH):
+            at = head * HEAD_WIDTH
+            a, b = lin[at : at + half], lin[at + half : at + HEAD_WIDTH]
+            first = (a * cos - b * sin).astype(bf16)
+            second = (b * cos + a * sin).astype(bf16)
+            out_ref[at : at + half] = first
+            out_ref[at + half : at + HEAD_WIDTH] = second
+            fa, fb = first.astype(f32), second.astype(f32)
+            worst = jnp.maximum(worst, jnp.sum(fa * fa + fb * fb, axis=0, keepdims=True))
+        return worst
+
+    nk_ref[...] = rotated(contract(w_ref[:, q_rows : q_rows + kv_rows], h, 0, 1), k_ref, cos, sin)
+    v_ref[...] = contract(w_ref[:, q_rows + kv_rows : q_rows + 2 * kv_rows], h, 0, 1).astype(bf16)
+    nq_ref[...] = rotated(contract(w_ref[:, :q_rows], h, 0, 1), q_ref, cos * scale, sin * scale)
+
+
+def project(x, gain, w, cos, sin, q_rows, kv_rows, tile=512):
+    rows, width = x.shape
+    cols = lambda n: pl.BlockSpec((n, tile), lambda i: (0, i))
+    return pl.pallas_call(
+        project_kernel,
+        grid=(rows // tile,),
+        in_specs=[
+            pl.BlockSpec((tile, width), lambda i: (i, 0)),
+            resident(gain.shape),
+            resident(w.shape),
+            cols(cos.shape[0]),
+            cols(cos.shape[0]),
+        ],
+        out_specs=(
+            cols(q_rows),
+            cols(kv_rows),
+            cols(kv_rows),
+            pl.BlockSpec((tile, width), lambda i: (i, 0)),
+            cols(1),
+            cols(1),
+        ),
+        out_shape=(
+            jax.ShapeDtypeStruct((q_rows, rows), bf16),
+            jax.ShapeDtypeStruct((kv_rows, rows), bf16),
+            jax.ShapeDtypeStruct((kv_rows, rows), bf16),
+            jax.ShapeDtypeStruct((rows, width), bf16),
+            jax.ShapeDtypeStruct((1, rows), f32),
+            jax.ShapeDtypeStruct((1, rows), f32),
+        ),
+        compiler_params=pltpu.CompilerParams(vmem_limit_bytes=48 * MIB),
+        name="project",
+    )(x, gain, w, cos, sin)
+
+
+ONES = 16
+
+
+def causal(keys, columns):
+    return lax.broadcasted_iota(jnp.int32, (keys, columns), 0) <= lax.broadcasted_iota(
+        jnp.int32, (keys, columns), 1
+    )
+
+
+def spans(prompt_rows, rows, step):
+    found = [(0, prompt_rows, prompt_rows, rows, False)]
+    at = 0
+    while at < rows:
+        end = prompt_rows if at < prompt_rows else at + CONTINUE_LENGTH
+        for key in range(at, end, step):
+            found.append((key, key + step, key, end, True))
+        at = end
+    return found
+
+
+def weigh(keys, query, diagonal):
+    scores = contract(keys, query, 1, 0)
+    weights = jnp.exp2(scores)
+    if diagonal:
+        step = keys.shape[0]
+        front = jnp.where(causal(step, step), weights[:, :step], 0.0)
+        weights = front if weights.shape[1] == step else jnp.concatenate([front, weights[:, step:]], axis=1)
+    return weights.astype(bf16)
+
+
+def own_forward_kernel(q_ref, k_ref, v_ref, acc_ref, *, group, prompt_rows, step):
+    rows = q_ref.shape[1]
+    keys = k_ref[...].T
+    values = jnp.concatenate([v_ref[...], jnp.ones((ONES, rows), bf16)], axis=0)
+    wide = HEAD_WIDTH + ONES
+    started = set()
+    for low, high, first, last, diagonal in spans(prompt_rows, rows, step):
+        for head in range(group):
+            query = q_ref[head * HEAD_WIDTH : (head + 1) * HEAD_WIDTH, first:last]
+            weights = weigh(keys[low:high], query, diagonal)
+            part = contract(values[:, low:high], weights, 1, 0)
+            at = pl.ds(head * wide, wide)
+            fresh = (low == 0 and not diagonal) or (diagonal and low == 0)
+            if fresh:
+                acc_ref[at, first:last] = part
+            else:
+                acc_ref[at, first:last] += part
+
+
+def own_forward(q, k, v, kv_heads, prompt_rows, step=256):
+    rows = q.shape[1]
+    group = q.shape[0] // HEAD_WIDTH // kv_heads
+    wide = group * (HEAD_WIDTH + ONES)
+    block = lambda n: pl.BlockSpec((n, rows), lambda h: (h, 0))
+    return pl.pallas_call(
+        functools.partial(own_forward_kernel, group=group, prompt_rows=prompt_rows, step=step),
+        grid=(kv_heads,),
+        in_specs=[block(group * HEAD_WIDTH), block(HEAD_WIDTH), block(HEAD_WIDTH)],
+        out_specs=block(wide),
+        out_shape=jax.ShapeDtypeStruct((kv_heads * wide, rows), f32),
+        compiler_params=pltpu.CompilerParams(vmem_limit_bytes=56 * MIB),
+        name="own_forward",
+    )(q, k, v)
+
+
+def other_forward_kernel(seen_ref, q_ref, k_ref, v_ref, acc_ref, o_ref, lse_ref, *, group, prompt_rows):
+    rows = q_ref.shape[1]
+    keys = k_ref[...].T
+    values = jnp.concatenate([v_ref[...], jnp.ones((ONES, keys.shape[0]), bf16)], axis=0)
+    wide = HEAD_WIDTH + ONES
+
+    def finish(first, last, with_other):
+        for head in range(group):
+            total = acc_ref[head * wide : (head + 1) * wide, first:last]
+            if with_other:
+                query = q_ref[head * HEAD_WIDTH : (head + 1) * HEAD_WIDTH, first:last]
+                total = total + contract(values, weigh(keys, query, False), 1, 0)
+            weight_sum = total[HEAD_WIDTH : HEAD_WIDTH + 1]
+            o_ref[head * HEAD_WIDTH : (head + 1) * HEAD_WIDTH, first:last] = (
+                total[:HEAD_WIDTH] / weight_sum
+            ).astype(bf16)
+            lse_ref[0, head : head + 1, first:last] = jnp.log2(weight_sum)
+
+    finish(prompt_rows, rows, True)
+
+    @pl.when(seen_ref[0] > 0)
+    def _():
+        finish(0, prompt_rows, True)
+
+    @pl.when(seen_ref[0] == 0)
+    def _():
+        finish(0, prompt_rows, False)
+
+
+def other_forward(seen, q, k, v, acc, kv_heads, prompt_rows):
+    rows = q.shape[1]
+    group = q.shape[0] // HEAD_WIDTH // kv_heads
+    wide = group * (HEAD_WIDTH + ONES)
+    block = lambda n, m: pl.BlockSpec((n, m), lambda h, s: (h, 0))
+    return pl.pallas_call(
+        functools.partial(other_forward_kernel, group=group, prompt_rows=prompt_rows),
+        grid_spec=pltpu.PrefetchScalarGridSpec(
+            num_scalar_prefetch=1,
+            grid=(kv_heads,),
+            in_specs=[
+                block(group * HEAD_WIDTH, rows),
+                block(HEAD_WIDTH, k.shape[1]),
+                block(HEAD_WIDTH, k.shape[1]),
+                block(wide, rows),
+            ],
+            out_specs=(
+                block(group * HEAD_WIDTH, rows),
+                pl.BlockSpec((1, group, rows), lambda h, s: (h, 0, 0)),
+            ),
+        ),
+        out_shape=(
+            jax.ShapeDtypeStruct(q.shape, bf16),
+            jax.ShapeDtypeStruct((kv_heads, group, rows), f32),
+        ),
+        compiler_params=pltpu.CompilerParams(vmem_limit_bytes=56 * MIB),
+        name="other_forward",
+    )(seen, q, k, v, acc)
+
+
+def in_parts(row):
+    high = row.astype(bf16)
+    rest = row - high.astype(f32)
+    middle = rest.astype(bf16)
+    low = (rest - middle.astype(f32)).astype(bf16)
+    return jnp.concatenate([high, middle, low, jnp.zeros((ONES - 3, row.shape[1]), bf16)], axis=0)
+
+
+def widened(matrix):
+    return jnp.concatenate([matrix, jnp.ones((matrix.shape[0], ONES), bf16)], axis=1)
+
+
+def tile_backward(keys, values, key_rows, query, grad, diagonal):
+    weights = jnp.exp2(contract(keys, query, 1, 0))
+    slopes = contract(values, grad, 1, 0)
+    if diagonal:
+        step = keys.shape[0]
+        front = jnp.where(causal(step, step), weights[:, :step], 0.0)
+        weights = front if weights.shape[1] == step else jnp.concatenate([front, weights[:, step:]], axis=1)
+    slopes = (weights * slopes).astype(bf16)
+    weights = weights.astype(bf16)
+    query_grad = contract(key_rows, slopes, 1, 0)
+    key_grad = contract(query[:HEAD_WIDTH], slopes, 1, 1)
+    value_grad = contract(grad[:HEAD_WIDTH], weights, 1, 1)
+    return query_grad, key_grad, value_grad
+
+
+def fill_sides(q_ref, g_ref, lse_ref, delta_ref, query_ref, grad_ref, group):
+    for head in range(group):
+        rows = pl.ds(head * HEAD_WIDTH, HEAD_WIDTH)
+        query_ref[head, :HEAD_WIDTH] = q_ref[rows]
+        grad_ref[head, :HEAD_WIDTH] = g_ref[rows]
+        query_ref[head, HEAD_WIDTH:] = in_parts(-lse_ref[0, head : head + 1])
+        grad_ref[head, HEAD_WIDTH:] = in_parts(-delta_ref[0, head : head + 1])
+
+
+def other_backward_kernel(
+    seen_ref, q_ref, g_ref, lse_ref, delta_ref, k_ref, v_ref, dq_ref, dk_ref, dv_ref,
+    query_ref, grad_ref, keys_ref, values_ref, *, group, prompt_rows, step
+):
+    rows = q_ref.shape[1]
+    fill_sides(q_ref, g_ref, lse_ref, delta_ref, query_ref, grad_ref, group)
+    keys_ref[...] = widened(k_ref[...].T)
+    values_ref[...] = widened(v_ref[...].T)
+    dq_ref[...] = jnp.zeros_like(dq_ref)
+
+    def part(first, last, fresh):
+        for low in range(0, k_ref.shape[1], step):
+            span = slice(low, low + step)
+            key_sum = value_sum = None
+            for head in range(group):
+                query_grad, key_grad, value_grad = tile_backward(
+                    keys_ref[span], values_ref[span], k_ref[:, span],
+                    query_ref[head, :, first:last], grad_ref[head, :, first:last], False,
+                )
+                at = pl.ds(head * HEAD_WIDTH, HEAD_WIDTH)
+                dq_ref[at, first:last] += query_grad
+                key_sum = key_grad if key_sum is None else key_sum + key_grad
+                value_sum = value_grad if value_sum is None else value_sum + value_grad
+            if fresh:
+                dk_ref[:, span] = key_sum
+                dv_ref[:, span] = value_sum
+            else:
+                dk_ref[:, span] += key_sum
+                dv_ref[:, span] += value_sum
+
+    part(prompt_rows, rows, True)
+
+    @pl.when(seen_ref[0] > 0)
+    def _():
+        part(0, prompt_rows, False)
+
+
+def backward_specs(group, rows, key_count):
+    block = lambda n, m: pl.BlockSpec((n, m), lambda h, *_: (h, 0))
+    row_block = pl.BlockSpec((1, group, rows), lambda h, *_: (h, 0, 0))
+    wide = group * HEAD_WIDTH
+    ins = [block(wide, rows), block(wide, rows), row_block, row_block,
+           block(HEAD_WIDTH, key_count), block(HEAD_WIDTH, key_count)]
+    outs = (block(wide, rows), block(HEAD_WIDTH, key_count), block(HEAD_WIDTH, key_count))
+    scratch = [
+        pltpu.VMEM((group, HEAD_WIDTH + ONES, rows), bf16),
+        pltpu.VMEM((group, HEAD_WIDTH + ONES, rows), bf16),
+        pltpu.VMEM((key_count, HEAD_WIDTH + ONES), bf16),
+        pltpu.VMEM((key_count, HEAD_WIDTH + ONES), bf16),
+    ]
+    return ins, outs, scratch
+
+
+def other_backward(seen, q, g, lse, delta, k, v, kv_heads, prompt_rows, step=256):
+    rows = q.shape[1]
+    group = q.shape[0] // HEAD_WIDTH // kv_heads
+    ins, outs, scratch = backward_specs(group, rows, k.shape[1])
+    return pl.pallas_call(
+        functools.partial(other_backward_kernel, group=group, prompt_rows=prompt_rows, step=step),
+        grid_spec=pltpu.PrefetchScalarGridSpec(
+            num_scalar_prefetch=1, grid=(kv_heads,), in_specs=ins, out_specs=outs, scratch_shapes=scratch
+        ),
+        out_shape=(
+            jax.ShapeDtypeStruct(q.shape, f32),
+            jax.ShapeDtypeStruct(k.shape, f32),
+            jax.ShapeDtypeStruct(v.shape, f32),
+        ),
+        compiler_params=pltpu.CompilerParams(vmem_limit_bytes=56 * MIB),
+        name="other_backward",
+    )(seen, q, g, lse, delta, k, v)
+
+
+def own_backward_kernel(
+    q_ref, g_ref, lse_ref, delta_ref, k_ref, v_ref, dq_in_ref, dq_ref, dk_ref, dv_ref,
+    query_ref, grad_ref, keys_ref, values_ref, *, group, prompt_rows, step
+):
+    rows = q_ref.shape[1]
+    fill_sides(q_ref, g_ref, lse_ref, delta_ref, query_ref, grad_ref, group)
+    keys_ref[...] = widened(k_ref[...].T)
+    values_ref[...] = widened(v_ref[...].T)
+    dq_ref[...] = dq_in_ref[...]
+    dk_ref[...] = jnp.zeros_like(dk_ref)
+    dv_ref[...] = jnp.zeros_like(dv_ref)
+
+    def one(low, high, first, last, diagonal):
+        span = slice(low, high)
+        key_sum = value_sum = None
+        for head in range(group):
+            query_grad, key_grad, value_grad = tile_backward(
+                keys_ref[span], values_ref[span], k_ref[:, span],
+                query_ref[head, :, first:last], grad_ref[head, :, first:last], diagonal,
+            )
+            at = pl.ds(head * HEAD_WIDTH, HEAD_WIDTH)
+            dq_ref[at, first:last] += query_grad
+            key_sum = key_grad if key_sum is None else key_sum + key_grad
+            value_sum = value_grad if value_sum is None else value_sum + value_grad
+        dk_ref[:, span] += key_sum
+        dv_ref[:, span] += value_sum
+
+    for low, high, first, last, diagonal in spans(prompt_rows, rows, step):
+        if diagonal:
+            one(low, high, first, last, True)
+        else:
+            for at in range(low, high, step):
+                one(at, at + step, first, last, False)
+
+
+def own_backward(q, g, lse, delta, k, v, dq, kv_heads, prompt_rows, step=256):
+    rows = q.shape[1]
+    group = q.shape[0] // HEAD_WIDTH // kv_heads
+    ins, outs, scratch = backward_specs(group, rows, k.shape[1])
+    return pl.pallas_call(
+        functools.partial(own_backward_kernel, group=group, prompt_rows=prompt_rows, step=step),
+        grid=(kv_heads,),
+        in_specs=ins + [outs[0]],
+        out_specs=outs,
+        scratch_shapes=scratch,
+        out_shape=(
+            jax.ShapeDtypeStruct(q.shape, f32),
+            jax.ShapeDtypeStruct(k.shape, f32),
+            jax.ShapeDtypeStruct(v.shape, f32),
+        ),
+        compiler_params=pltpu.CompilerParams(vmem_limit_bytes=60 * MIB),
+        name="own_backward",
+    )(q, g, lse, delta, k, v, dq)
+
+
+def middle_kernel(
+    x_ref, dy_ref, o_ref, gain_ref, wo_any, wg_any, wu_any, wd_any,
+    out_ref, h2_ref, hidden_ref, dgate_ref, dup_ref, dattn_ref, dob_ref, delta_ref, dgain_ref,
+    wo_ref, wg_ref, wu_ref, wd_ref, sems, *, chunk
+):
+    step = pl.program_id(0)
+    copies = [
+        pltpu.make_async_copy(source, target, sems.at[i])
+        for i, (source, target) in enumerate(
+            ((wo_any, wo_ref), (wg_any, wg_ref), (wu_any, wu_ref), (wd_any, wd_ref))
+        )
+    ]
+
+    @pl.when(step == 0)
+    def _():
+        for copy in copies:
+            copy.start()
+        dgain_ref[...] = jnp.zeros_like(dgain_ref)
+        copies[0].wait()
+
+    ob = o_ref[...]
+    x1 = x_ref[...].astype(f32) + contract(ob, wo_ref[...], 0, 0)
+    inverse = lax.rsqrt(jnp.mean(x1 * x1, axis=-1, keepdims=True) + norm_eps)
+    gain = gain_ref[...]
+    h2 = (x1 * inverse * gain).astype(bf16)
+    h2_ref[...] = h2
+    dy = dy_ref[...]
+
+    @pl.when(step == 0)
+    def _():
+        for copy in copies[1:]:
+            copy.wait()
+
+    result = x1
+    dh2 = None
+    for low in range(0, wg_ref.shape[1], chunk):
+        span = slice(low, low + chunk)
+        gate = contract(h2, wg_ref[:, span], 1, 0)
+        up = contract(h2, wu_ref[:, span], 1, 0)
+        dhidden = contract(dy, wd_ref[span], 1, 1)
+        sigma = 1.0 / (1.0 + jnp.exp(-gate))
+        silu = gate * sigma
+        hidden = (silu * up).astype(bf16)
+        hidden_ref[:, span] = hidden
+        result = result + contract(hidden, wd_ref[span], 1, 0)
+        dgate = (dhidden * up * sigma * (1.0 + gate * (1.0 - sigma))).astype(bf16)
+        dup = (dhidden * silu).astype(bf16)
+        dgate_ref[:, span] = dgate
+        dup_ref[:, span] = dup
+        part = contract(dgate, wg_ref[:, span], 1, 1) + contract(dup, wu_ref[:, span], 1, 1)
+        dh2 = part if dh2 is None else dh2 + part
+    out_ref[...] = result.astype(bf16)
+    dgain_ref[...] += jnp.sum(dh2 * x1 * inverse, axis=0, keepdims=True)
+    u = dh2 * gain
+    dx1 = dy.astype(f32) + inverse * u - x1 * (inverse * inverse * inverse) * jnp.mean(
+        u * x1, axis=-1, keepdims=True
+    )
+    dattn = dx1.astype(bf16)
+    dattn_ref[...] = dattn
+    dob = contract(wo_ref[...], dattn, 1, 1).astype(bf16)
+    dob_ref[...] = dob
+    product = dob.astype(f32) * ob.astype(f32)
+    heads, group = delta_ref.shape[0], delta_ref.shape[1]
+    for kv in range(heads):
+        for member in range(group):
+            at = (kv * group + member) * HEAD_WIDTH
+            delta_ref[kv, member : member + 1] = jnp.sum(
+                product[at : at + HEAD_WIDTH], axis=0, keepdims=True
+            )
+
+
+def middle(x, dy, o, gain, wo, wg, wu, wd, kv_heads, tile=256, chunk=1024):
+    rows, width = x.shape
+    hidden = wg.shape[1]
+    q_rows = o.shape[0]
+    group = q_rows // HEAD_WIDTH // kv_heads
+    by_row = lambda n: pl.BlockSpec((tile, n), lambda i: (i, 0))
+    any_spec = pl.BlockSpec(memory_space=pl.ANY)
+    shape = jax.ShapeDtypeStruct
+    return pl.pallas_call(
+        functools.partial(middle_kernel, chunk=chunk),
+        grid=(rows // tile,),
+        in_specs=[by_row(width), by_row(width), pl.BlockSpec((q_rows, tile), lambda i: (0, i)),
+                  resident(gain.shape)] + [any_spec] * 4,
+        out_specs=(
+            by_row(width), by_row(width), by_row(hidden), by_row(hidden), by_row(hidden), by_row(width),
+            pl.BlockSpec((q_rows, tile), lambda i: (0, i)),
+            pl.BlockSpec((kv_heads, group, tile), lambda i: (0, 0, i)),
+            pl.BlockSpec((1, width), lambda i: (0, 0)),
+        ),
+        out_shape=(
+            shape((rows, width), bf16), shape((rows, width), bf16), shape((rows, hidden), bf16),
+            shape((rows, hidden), bf16), shape((rows, hidden), bf16), shape((rows, width), bf16),
+            shape((q_rows, rows), bf16), shape((kv_heads, group, rows), f32), shape((1, width), f32),
+        ),
+        scratch_shapes=[pltpu.VMEM(w.shape, bf16) for w in (wo, wg, wu, wd)] + [pltpu.SemaphoreType.DMA((4,))],
+        compiler_params=pltpu.CompilerParams(vmem_limit_bytes=62 * MIB),
+        name="middle",
+    )(x, dy, o, gain, wo, wg, wu, wd)
+
+
+def ffn_grads_kernel(h2_ref, dy_ref, hidden_ref, dgate_ref, dup_ref, down_ref, gate_ref, up_ref):
+    down_ref[...] = contract(hidden_ref[...], dy_ref[...], 0, 0).astype(bf16)
+    gate_ref[...] = contract(h2_ref[...], dgate_ref[...], 0, 0).astype(bf16)
+    up_ref[...] = contract(h2_ref[...], dup_ref[...], 0, 0).astype(bf16)
+
+
+def ffn_grads(h2, dy, hidden, dgate, dup, tile=512):
+    rows, width = h2.shape
+    total = hidden.shape[1]
+    cols = lambda n: pl.BlockSpec((n, tile), lambda i: (0, i))
+    shape = jax.ShapeDtypeStruct
+    return pl.pallas_call(
+        ffn_grads_kernel,
+        grid=(total // tile,),
+        in_specs=[resident(h2.shape), resident(dy.shape), cols(rows), cols(rows), cols(rows)],
+        out_specs=(pl.BlockSpec((tile, width), lambda i: (i, 0)), cols(width), cols(width)),
+        out_shape=(shape((total, width), bf16), shape((width, total), bf16), shape((width, total), bf16)),
+        compiler_params=pltpu.CompilerParams(vmem_limit_bytes=56 * MIB),
+        name="ffn_grads",
+    )(h2, dy, hidden, dgate, dup)
+
+
+def finish_kernel(
+    x_ref, h_ref, dattn_ref, gain_ref, w_ref, dq_ref, dk_ref, dv_ref, cos_ref, sin_ref,
+    out_ref, dw_ref, dgain_ref, acc_ref
+):
+    step = pl.program_id(0)
+
+    @pl.when(step == 0)
+    def _():
+        dgain_ref[...] = jnp.zeros_like(dgain_ref)
+        acc_ref[...] = jnp.zeros_like(acc_ref)
+
+    half = HEAD_WIDTH // 2
+    cos, sin = cos_ref[...], sin_ref[...]
+
+    def turned(ref, scale):
+        c, s = cos * scale, sin * scale
+        pieces = []
+        for at in range(0, ref.shape[0], HEAD_WIDTH):
+            a, b = ref[at : at + half], ref[at + half : at + HEAD_WIDTH]
+            pieces += [a * c + b * s, b * c - a * s]
+        return jnp.concatenate(pieces, axis=0)
+
+    lin = jnp.concatenate(
+        [turned(dq_ref, HEAD_WIDTH**-0.5), turned(dk_ref, LN2), dv_ref[...]], axis=0
+    ).astype(bf16).T
+    acc_ref[...] += contract(h_ref[...], lin, 0, 0)
+    dh = contract(lin, w_ref[...], 1, 1)
+    x = x_ref[...].astype(f32)
+    inverse = lax.rsqrt(jnp.mean(x * x, axis=-1, keepdims=True) + norm_eps)
+    dgain_ref[...] += jnp.sum(dh * x * inverse, axis=0, keepdims=True)
+    u = dh * gain_ref[...]
+    out_ref[...] = (
+        dattn_ref[...].astype(f32)
+        + inverse * u
+        - x * (inverse * inverse * inverse) * jnp.mean(u * x, axis=-1, keepdims=True)
+    )
+
+    @pl.when(step == pl.num_programs(0) - 1)
+    def _():
+        dw_ref[...] = acc_ref[...].astype(bf16)
+
+
+def finish(x, h, dattn, gain, w, dq, dk, dv, cos, sin, tile=256):
+    rows, width = x.shape
+    by_row = pl.BlockSpec((tile, width), lambda i: (i, 0))
+    cols = lambda n: pl.BlockSpec((n, tile), lambda i: (0, i))
+    shape = jax.ShapeDtypeStruct
+    return pl.pallas_call(
+        finish_kernel,
+        grid=(rows // tile,),
+        in_specs=[by_row, by_row, by_row, resident(gain.shape), resident(w.shape),
+                  cols(dq.shape[0]), cols(dk.shape[0]), cols(dv.shape[0]),
+                  cols(cos.shape[0]), cols(cos.shape[0])],
+        out_specs=(by_row, pl.BlockSpec(w.shape, lambda i: (0, 0)), pl.BlockSpec((1, width), lambda i: (0, 0))),
+        out_shape=(shape((rows, width), f32), shape(w.shape, bf16), shape((1, width), f32)),
+        scratch_shapes=[pltpu.VMEM(w.shape, f32)],
+        compiler_params=pltpu.CompilerParams(vmem_limit_bytes=56 * MIB),
+        name="finish",
+    )(x, h, dattn, gain, w, dq, dk, dv, cos, sin)
+
+
 rope_base = 10000.0
 masked_score = -1e30
 
@@ -297,7 +849,7 @@
     )
 
 
-def local(
+def general_local(
     tokens,
     block_map,
     attention_gain,
@@ -571,9 +1123,140 @@
     )
 
 
+SAFE_BOUND = 90.0
+OWNERS = ("group", "wshard")
+SWAP = [(0, 1), (1, 0)]
+
+
+def exact_attention(seen, q, k, v, k_other, v_other, kv_heads, prompt_rows):
+    rows = q.shape[1]
+    heads = q.shape[0] // HEAD_WIDTH
+    keys = jnp.concatenate([k_other, k], axis=1).reshape(kv_heads, HEAD_WIDTH, -1)
+    values = jnp.concatenate([v_other, v], axis=1).reshape(kv_heads, HEAD_WIDTH, -1)
+    at = jnp.arange(rows)
+    in_prompt = at < prompt_rows
+    piece = jnp.where(in_prompt, -1, (at - prompt_rows) // CONTINUE_LENGTH)
+    own = (at[None, :] <= at[:, None]) & (in_prompt[None, :] | (piece[None, :] == piece[:, None]))
+    other = jnp.broadcast_to(jnp.where(in_prompt, seen > 0, True)[:, None], (rows, k_other.shape[1]))
+    allowed = jnp.concatenate([other, own], axis=1)
+
+    def one_head(head):
+        query = lax.dynamic_index_in_dim(q.reshape(heads, HEAD_WIDTH, rows), head, 0, False)
+        key = lax.dynamic_index_in_dim(keys, head // (heads // kv_heads), 0, False)
+        value = lax.dynamic_index_in_dim(values, head // (heads // kv_heads), 0, False)
+        scores = jnp.where(allowed, contract(query, key, 0, 0), masked_score)
+        top = jnp.max(scores, axis=1, keepdims=True)
+        weights = jnp.exp2(scores - top)
+        total = jnp.sum(weights, axis=1, keepdims=True)
+        out = contract(value, (weights / total).astype(bf16), 1, 1)
+        return out.astype(bf16), (top + jnp.log2(total))[:, 0]
+
+    out, lse = lax.map(one_head, jnp.arange(heads))
+    return out.reshape(q.shape), lse.reshape(kv_heads, heads // kv_heads, rows)
+
+
+def swap(array):
+    return lax.ppermute(array, "ctx", SWAP)
+
+
+def fast_local(
+    tokens, block_map, attention_gain, query_weight, key_matrix, value_matrix, output_weight,
+    feedforward_gain, gate_weight, up_weight, down_weight, out_grad,
+):
+    x, dy = tokens[0], out_grad[0]
+    rows, width = x.shape
+    prompt_rows = rows // 2
+    q_rows, kv_rows = query_weight.shape[1], key_matrix.shape[1]
+    kv_heads = kv_rows // HEAD_WIDTH
+    hidden = gate_weight.shape[1]
+    shard_rows = query_weight.shape[0]
+    block = lax.dynamic_index_in_dim(block_map[0], 2 * lax.axis_index("ctx"), 0, False)
+    seen = (block > 0).astype(jnp.int32)
+    prompt_total = block_map.shape[1] // 2 * prompt_rows
+
+    gains = jnp.stack([attention_gain, feedforward_gain], axis=1)
+    gains = jnp.pad(gains, ((0, 0), (0, 126)))
+    first = lax.all_gather(
+        jnp.concatenate([query_weight, key_matrix, value_matrix, gains], axis=1), OWNERS, axis=0, tiled=True
+    )
+    second = lax.all_gather(
+        jnp.concatenate([output_weight, gate_weight, up_weight], axis=1), OWNERS, axis=0, tiled=True
+    )
+    wd = lax.all_gather(down_weight, OWNERS, axis=0, tiled=True)
+    w_qkv = first[:, : q_rows + 2 * kv_rows]
+    gain_pair = first[:, q_rows + 2 * kv_rows : q_rows + 2 * kv_rows + 2].astype(f32).T
+    gain_a, gain_f = gain_pair[0:1], gain_pair[1:2]
+    wo = second[:, :q_rows]
+    wg = second[:, q_rows : q_rows + hidden]
+    wu = second[:, q_rows + hidden :]
+
+    at = jnp.arange(rows, dtype=jnp.int32)
+    positions = jnp.where(
+        at < prompt_rows, block * prompt_rows + at, prompt_total + (at - prompt_rows) % CONTINUE_LENGTH
+    )
+    half = HEAD_WIDTH // 2
+    frequency = rope_base ** (-(jnp.arange(half, dtype=f32) * 2.0) / HEAD_WIDTH)
+    angles = frequency[:, None] * positions.astype(f32)[None, :]
+    cos, sin = jnp.cos(angles), jnp.sin(angles)
+
+    q, k, v, h1, norm_q, norm_k = project(x, gain_a, w_qkv, cos, sin, q_rows, kv_rows)
+    k_other, v_other = swap(k[:, :prompt_rows]), swap(v[:, :prompt_rows])
+    acc = own_forward(q, k, v, kv_heads, prompt_rows)
+    other_norm = jnp.max(jnp.sum(jnp.square(k_other.astype(f32)).reshape(kv_heads, HEAD_WIDTH, -1), axis=1))
+    bound = jnp.max(norm_q) * jnp.maximum(jnp.max(norm_k), other_norm)
+    o, lse = other_forward(seen[None], q, k_other, v_other, acc, kv_heads, prompt_rows)
+    o, lse = lax.cond(
+        bound < SAFE_BOUND * SAFE_BOUND,
+        lambda: (o, lse),
+        lambda: exact_attention(seen, q, k, v, k_other, v_other, kv_heads, prompt_rows),
+    )
+    layer_out, h2, hid, dgate, dup, dattn, dob, delta, dgain_f = middle(
+        x, dy, o, gain_f, wo, wg, wu, wd, kv_heads
+    )
+    d_down, d_gate, d_up = ffn_grads(h2, dy, hid, dgate, dup)
+    d_out = contract(o, dattn, 1, 0).astype(bf16)
+    scatter = lambda a: lax.psum_scatter(a, OWNERS, scatter_dimension=0, tiled=True)
+    d_down = scatter(d_down)
+    d_wide = scatter(jnp.concatenate([d_out, d_gate, d_up], axis=1))
+    dq_part, dk_other, dv_other = other_backward(seen[None], q, dob, lse, delta, k_other, v_other, kv_heads, prompt_rows)
+    dk_in, dv_in = swap(dk_other.astype(bf16)), swap(dv_other.astype(bf16))
+    dq, dk, dv = own_backward(q, dob, lse, delta, k, v, dq_part, kv_heads, prompt_rows)
+    more = lambda a, b: a.at[:, :prompt_rows].add(b.astype(f32))
+    grad_tokens, d_qkv, dgain_a = finish(
+        x, h1, dattn, gain_a, w_qkv, dq, more(dk, dk_in), more(dv, dv_in), cos, sin
+    )
+    dgains = jnp.pad(jnp.concatenate([dgain_a, dgain_f], axis=0).T, ((0, 0), (0, 126))).astype(bf16)
+    d_first = scatter(jnp.concatenate([d_qkv, dgains], axis=1))
+
+    def over_ctx(part):
+        return part.astype(f32) + swap(part).astype(f32)
+
+    d_down, d_wide, d_first = over_ctx(d_down), over_ctx(d_wide), over_ctx(d_first)
+    end = q_rows + 2 * kv_rows
+    return (
+        layer_out[None],
+        grad_tokens[None],
+        d_first[:, end],
+        d_first[:, :q_rows],
+        d_first[:, q_rows : q_rows + kv_rows],
+        d_first[:, q_rows + kv_rows : end],
+        d_wide[:, :q_rows],
+        d_first[:, end + 1],
+        d_wide[:, q_rows : q_rows + hidden],
+        d_wide[:, q_rows + hidden :],
+        d_down,
+    )
+
+
+def local(mesh, tokens, block_map, *rest):
+    block_rows = tokens.shape[1] // 2
+    whole = mesh.shape["ctx"] == 2 and block_rows % CONTINUE_LENGTH == 0 and tokens.shape[0] == 1
+    return (fast_local if whole else general_local)(tokens, block_map, *rest)
+
+
 def solution(mesh):
     return jax.shard_map(
-        local,
+        lambda *args: local(mesh, *args),
         mesh=mesh,
         in_specs=(
             P(("group", "wshard"), "ctx", None),

time: 3450 us -> 1040 us (0.30); the launches traced: 3400 us -> 1030 us
  matrix products: 1070 us -> 9.91 us
  other arithmetic: 846 us -> 42.3 us
  local copies, waits for them, and re-layouts: 670 us -> 27.8 us
  Pallas kernels: 0 us -> 560 us
  loops' own time: 232 us -> 9.86 us
  blocking collectives: 173 us -> 0 us
  waiting for transfers between devices: 392 us -> 356 us
    dot_general x258 -> x1, matrix products: 1070 us -> 9.91 us  [contract(): lax.dot_general(a, b, (((dim_a,), (dim_b,)), ((), ())), preferred_element...]
    pallas_call x0 -> x8, Pallas kernels: none -> 560 us  [the longest x1 135 us: middle(): pl.pallas_call(functools.partial(middle_kernel, chunk=chunk), grid=(rows...]
    reduce_or x320 -> x0, other arithmetic: 409 us -> none  [the longest x128 198 us: out_step(): jnp.any(allowed)]
    dynamic_update_slice x80 -> x0, local copies, waits for them, and re-layouts: 272 us -> none  [the longest x16 211 us: attention_forward(): lax.map(one_block, (query_split(query_heads, query_block), query_split(qu...]
    another operation x343 -> x1, loops' own time: 232 us -> 9.86 us  [fast_local(): lax.cond(bound < SAFE_BOUND * SAFE_BOUND, lambda: (o, lse), lambda: exact...]
    unnamed x22 -> x7, waiting for transfers between devices: 3.57 us -> 180 us
    dynamic_slice x344 -> x0, local copies, waits for them, and re-layouts: 175 us -> none  [the longest x320 136 us: one_block(): lax.scan(lse_step, initial, (key_tiles, kpos_tiles, kseg_tiles))]
    reduce_scatter x5 -> x2, waiting for transfers between devices: 249 us -> 95.1 us  [fast_local(): lax.psum_scatter(a, OWNERS, scatter_dimension=0, tiled=True)]
  transfers between devices with their start and end apart: 18 -> 13, of which waited for: 7 -> 6; matrix products, arithmetic and copies ran while one was open for 42% -> 6% of each run, Pallas kernels for 0% -> 27%
where the time goes in v1:
time: 1040 us; the launch traced here: 1030 us
  Pallas kernels  560 us (54%)
  waiting for transfers between devices  356 us (34%)
  other arithmetic  42.3 us (4%)
  local copies, waits for them, and re-layouts  27.8 us (3%)
  between operations  17.4 us (2%)
    unnamed x7, waiting for transfers between devices  180 us
    pallas_call x1, Pallas kernels, middle(): pl.pallas_call(functools.partial(middle_kernel, chunk=chunk), grid=(rows...  135 us
    pallas_call x1, Pallas kernels, own_backward(): pl.pallas_call(functools.partial(own_backward_kernel, group=group, prompt...  121 us
    pallas_call x1, Pallas kernels, other_backward(): pl.pallas_call(functools.partial(other_backward_kernel, group=group, prom...  114 us
    reduce_scatter x2, waiting for transfers between devices, fast_local(): lax.psum_scatter(a, OWNERS, scatter_dimension=0, tiled=True)  95.1 us
    pallas_call x1, Pallas kernels, ffn_grads(): pl.pallas_call(ffn_grads_kernel, grid=(total // tile,), in_specs=[residen...  54.6 us
    all_gather x1, waiting for transfers between devices, fast_local(): lax.all_gather(jnp.concatenate([query_weight, key_matrix, value_matrix, g...  49.5 us
    pallas_call x1, Pallas kernels, own_forward(): pl.pallas_call(functools.partial(own_forward_kernel, group=group, prompt_...  46.2 us
  transfers between devices with their start and end apart: 13, of which 6 were waited for; matrix products, arithmetic and copies ran while one was open for 6% of the time, Pallas kernels for 27%

profile of v1, /device:TPU:8, one launch (start us, length us, event | category | flops | bytes accessed | tf_op | source)
XLA Modules:
  0.0 1032.0 jit_solution(14238933257967005027)
XLA Ops:
  8.0 1.7 fusion.28
  9.8 2.2 pad_maximum_fusion.3
  15.8 49.5 %all-gather.4.cloned.1.call-done = bf16[1152,2048]{1,0:T(8,128)(2,1)} async-done(((bf16[72,2048]{1,0:T(8,128)(2,1)}), bf16[1152,2048]{1,0:T(8,128)(2,1)}) %all-gather.4.cloned.1.call-update) | async-done | bytes 4718608 | tf_op jit(solution)/shard_map/all_gather | solution.py:1179
  67.6 2.6 slice.110.w_ref
  70.2 18.8 %project.1 = (bf16[1152,2048]{1,0:T(8,128)(2,1)S(1)}, bf16[384,2048]{1,0:T(8,128)(2,1)S(1)}, bf16[384,2048]{1,0:T(8,128)(2,1)S(1)}, bf16[2048,1152]{1,0:T(8,128)...) custom-call(bf16[2048,1152]{1,0:T(8,128)(2,1)} %bitcast.55, f32[1,1152]{1,0:T(1,128)S(1)} %copy.44.gain_ref, ...), custom_call_target="tpu_custom_call" | custom-call | tf_op jit(solution)/shard_map/project/pallas_call | solution.py:61
  94.2 46.2 %own_forward.1.acc_ref = f32[1440,2048]{1,0:T(8,128)} custom-call(bf16[1152,2048]{1,0:T(8,128)(2,1)S(1)} %get-tuple-element.193.q_ref, bf16[384,2048]{1,0:T(8,128)(2,1)S(1)} %get-tuple-element.191.k_ref, bf16[384,2048]{1,0:T(8,128)(2,1)} %copy-done.8), custom_call_target="tpu_custom_call" | custom-call | tf_op jit(solution)/shard_map/own_forward/pallas_call | solution.py:146
  141.7 1.9 copy.45.gain_ref
  143.5 2.5 convert_multiply_fusion
  150.2 37.4 %other_forward.1 = (bf16[1152,2048]{1,0:T(8,128)(2,1)}, f32[6,3,2048]{2,1,0:T(4,128)S(1)}) custom-call(s32[1]{0:T(128)} %bitcast.18.seen_ref, bf16[1152,2048]{1,0:T(8,128)(2,1)} %copy-done.5, bf16[384,1024]{1,0:T(8,128)(2,1)} %collective-permute-done.k_ref, bf16[384,1024]{1,0:T(8,128)(2,1)} %collective-permute-done.1.v_ref, f32[1440,2048]{1,0:T(8,128)} %own_forward.1.acc_ref), custom_call_target="tpu_custom_call" | custom-call | tf_op jit(solution)/shard_map/other_forward/pallas_call | solution.py:191
  187.6 9.9 conditional.1
  197.5 3.5 slice.112.wo_any
  201.0 10.2 fusion.36
  211.1 12.4 %all-gather.8.cloned.1.call-done.wd_any = bf16[3072,1152]{1,0:T(8,128)(2,1)} async-done(((bf16[192,1152]{1,0:T(8,128)(2,1)}), bf16[3072,1152]{1,0:T(8,128)(2,1)}) %all-gather.8.cloned.1.call-update) | async-done | bytes 7077904 | tf_op jit(solution)/shard_map/all_gather | solution.py:1185
  223.5 134.7 %middle.1 = (bf16[2048,1152]{1,0:T(8,128)(2,1)}, bf16[2048,1152]{1,0:T(8,128)(2,1)}, bf16[2048,3072]{1,0:T(8,128)(2,1)}, bf16[2048,3072]{1,0:T(8,128)(2,1)}, bf1...) custom-call(bf16[2048,1152]{1,0:T(8,128)(2,1)} %bitcast.56, ...), custom_call_target="tpu_custom_call" | custom-call | tf_op jit(solution)/shard_map/middle/pallas_call | solution.py:458
  358.2 113.5 %other_backward.1 = (f32[1152,2048]{1,0:T(8,128)}, f32[384,1024]{1,0:T(8,128)}, f32[384,1024]{1,0:T(8,128)}) custom-call(s32[1]{0:T(128)} %bitcast.18.seen_ref, bf16[1152,2048]{1,0:T(8,128)(2,1)} %copy-done.5, bf16[1152,2048]{1,0:T(8,128)(2,1)} %get-tuple-element.198.g_ref, f32[6,3,2048]{2,1,0:T(4,128)S(1)} %get-tuple-element.199.lse_ref, ...), custom_call_target="tpu_custom_call" | custom-call | tf_op jit(solution)/shard_map/other_backward/pallas_call | solution.py:309
  471.7 2.5 convert_element_type.77
  474.3 2.4 convert_element_type.75
  476.7 2.0 collective-permute-start.2
  479.3 121.4 %own_backward.1 = (f32[1152,2048]{1,0:T(8,128)}, f32[384,2048]{1,0:T(8,128)}, f32[384,2048]{1,0:T(8,128)}) custom-call(bf16[1152,2048]{1,0:T(8,128)(2,1)} %copy-done.5, bf16[1152,2048]{1,0:T(8,128)(2,1)} %get-tuple-element.198.g_ref, f32[6,3,2048]{2,1,0:T(4,128)S(1)} %get-tuple-element.199.lse_ref, f32[6,3,2048]{2,1,0:T(4,128)} %get-tuple-element.200.delta_ref, ...), custom_call_target="tpu_custom_call" | custom-call | tf_op jit(solution)/shard_map/own_backward/pallas_call | solution.py:363
  600.8 4.1 fusion.26.dv_ref
  604.9 2.4 fusion.25.dk_ref
  607.3 1.7 copy-done.11
  608.9 33.3 %finish.1 = (f32[2048,1152]{1,0:T(8,128)}, bf16[1152,1920]{1,0:T(8,128)(2,1)}, f32[1,1152]{1,0:T(1,128)}) custom-call(bf16[2048,1152]{1,0:T(8,128)(2,1)} %bitcast.57, bf16[2048,1152]{1,0:T(8,128)(2,1)} %get-tuple-element.196.h_ref, bf16[2048,1152]{1,0:T(8,128)(2,1)} %get-tuple-element.197.dattn_ref, f32[1,1152]{1,0:T(1,128)} %copy-done.3, ...), custom_call_target="tpu_custom_call" | custom-call | tf_op jit(solution)/shard_map/finish/pallas_call | solution.py:549
  643.2 5.1 fusion.24
  648.4 54.6 %ffn_grads.1 = (bf16[3072,1152]{1,0:T(8,128)(2,1)}, bf16[1152,3072]{1,0:T(8,128)(2,1)}, bf16[1152,3072]{1,0:T(8,128)(2,1)}) custom-call(bf16[2048,1152]{1,0:T(8,128)(2,1)} %get-tuple-element.211.h2_ref, bf16[2048,1152]{1,0:T(8,128)(2,1)} %bitcast.59, bf16[2048,3072]{1,0:T(8,128)(2,1)} %get-tuple-element.212.hidden_ref, ...), custom_call_target="tpu_custom_call" | custom-call | tf_op jit(solution)/shard_map/ffn_grads/pallas_call | solution.py:491
  703.1 9.9 convolution_convert_fusion
  713.0 6.7 pad_maximum_fusion.2
  719.8 2.4 reduce-scatter.6.cloned.1.call-done
  723.6 92.7 %reduce-scatter.8.cloned.1.call-done = bf16[192,1152]{1,0:T(8,128)(2,1)} async-done(((bf16[3072,1152]{1,0:T(8,128)(2,1)}), bf16[192,1152]{1,0:T(8,128)(2,1)}) %reduce-scatter.8.cloned.1.call-update) | async-done | bytes 442384 | tf_op jit(solution)/shard_map/reduce_scatter | solution.py:1218
  817.9 179.4 %reduce-scatter.10.cloned.1.call-done = bf16[72,7296]{1,0:T(8,128)(2,1)} async-done(((bf16[1152,7296]{1,0:T(8,128)(2,1)}), bf16[72,7296]{1,0:T(8,128)(2,1)}) %reduce-scatter.10.cloned.1.call-update) | async-done | bytes 1050640
  1001.9 2.0 convert_add_fusion.1
  1004.0 18.3 %collective-permute-done.5 = bf16[72,7296]{1,0:T(8,128)(2,1)S(1)} collective-permute-done((bf16[72,7296]{1,0:T(8,128)(2,1)}, bf16[72,7296]{1,0:T(8,128)(2,1)S(1)}, u32[]{:S(2)}, u32[]{:S(2)}) %collective-permute-start.5) | collective-permute-done | bytes 1050656 | tf_op jit(solution)/shard_map/ppermute | solution.py:1159
  (81 shorter events, 26.6 us)
Async XLA Ops:
  7.2 58.1 %all-gather.4.cloned.1.call-start = ((), (), s32[]{:S(2)}) async-start(), calls=%async_computation.3 | async-start | bytes 5013504 | tf_op jit(solution)/shard_map/all_gather | solution.py:1179
  9.8 187.7 %all-gather.6.cloned.1.call-start = ((), (), s32[]{:S(2)}) async-start(), calls=%async_computation.4 | async-start | bytes 17860608 | tf_op jit(solution)/shard_map/all_gather | solution.py:1182
  12.1 211.4 %all-gather.8.cloned.1.call-start = ((), (), s32[]{:S(2)}) async-start(), calls=%async_computation.5 | async-start | bytes 7520256 | tf_op jit(solution)/shard_map/all_gather | solution.py:1185
  12.8 709.3 %reduce-scatter.6.cloned.1.call-start = ((), (), s32[]{:S(2)}) async-start(), calls=%async_computation.6 | async-start | bytes 5013504 | tf_op jit(solution)/shard_map/reduce_scatter | solution.py:1218
  15.8 54.4 %copy-start.1 = (f32[32,2048]{1,0:T(8,128)}, f32[32,2048]{1,0:T(8,128)S(1)}, u32[]{:S(2)}) copy-start(f32[32,2048]{1,0:T(8,128)S(1)} %get-tuple-element.249.sin_ref) | copy-start | bytes 786436
  15.8 54.4 %copy-start.2 = (f32[32,2048]{1,0:T(8,128)}, f32[32,2048]{1,0:T(8,128)S(1)}, u32[]{:S(2)}) copy-start(f32[32,2048]{1,0:T(8,128)S(1)} %get-tuple-element.250.cos_ref) | copy-start | bytes 786436
  67.6 21.4 %copy-start.3 = (f32[1,1152]{1,0:T(1,128)}, f32[1,1152]{1,0:T(1,128)S(1)}, u32[]{:S(2)}) copy-start(f32[1,1152]{1,0:T(1,128)S(1)} %copy.44.gain_ref) | copy-start | bytes 13828
  70.2 18.8 %copy-start = (bf16[1152,1920]{1,0:T(8,128)(2,1)}, bf16[1152,1920]{1,0:T(8,128)(2,1)S(1)}, u32[]{:S(2)}) copy-start(bf16[1152,1920]{1,0:T(8,128)(2,1)S(1)} %slice.110.w_ref) | copy-start | bytes 13271044
  89.0 2.5 copy-start.8
  89.0 51.5 %copy-start.5 = (bf16[1152,2048]{1,0:T(8,128)(2,1)}, bf16[1152,2048]{1,0:T(8,128)(2,1)S(1)}, u32[]{:S(2)}) copy-start(bf16[1152,2048]{1,0:T(8,128)(2,1)S(1)} %get-tuple-element.193.q_ref) | copy-start | bytes 14155780
  89.0 98.6 %copy-start.6 = (bf16[384,2048]{1,0:T(8,128)(2,1)}, bf16[384,2048]{1,0:T(8,128)(2,1)S(1)}, u32[]{:S(2)}) copy-start(bf16[384,2048]{1,0:T(8,128)(2,1)S(1)} %get-tuple-element.191.k_ref) | copy-start | bytes 4718596
  90.0 53.5 %collective-permute-start = (bf16[384,1024]{1,0:T(8,128)(2,1)}, bf16[384,1024]{1,0:T(8,128)(2,1)}, u32[]{:S(2)}, u32[]{:S(2)}) collective-permute-start(bf16[384,1024]{1,0:T(8,128)(2,1)} %slice.92), channel_id=1, source_target_pairs={{0,4},{4,0},{1,5},{5,1},{2,6},{6,2},{3,7},{7,3},{8,12},{12,8},{9,1... | collective-permute-start | bytes 2359304 | tf_op jit(solution)/shard_map/ppermute | solution.py:1159
  92.6 57.5 %collective-permute-start.1 = (bf16[384,1024]{1,0:T(8,128)(2,1)}, bf16[384,1024]{1,0:T(8,128)(2,1)}, u32[]{:S(2)}, u32[]{:S(2)}) collective-permute-start(bf16[384,1024]{1,0:T(8,128)(2,1)} %slice.93), channel_id=1, source_target_pairs={{0,4},{4,0},{1,5},{5,1},{2,6},{6,2},{3,7},{7,3},{8,12},{12,8},{9,1... | collective-permute-start | bytes 2359304 | tf_op jit(solution)/shard_map/ppermute | solution.py:1159
  94.2 55.9 %copy-start.9 = (bf16[384,2048]{1,0:T(8,128)(2,1)S(1)}, bf16[384,2048]{1,0:T(8,128)(2,1)}, u32[]{:S(2)}) copy-start(bf16[384,2048]{1,0:T(8,128)(2,1)} %copy-done.8) | copy-start | bytes 4718596
  471.7 7.6 copy-start.7
  474.3 126.6 %collective-permute-start.3 = (bf16[384,1024]{1,0:T(8,128)(2,1)}, bf16[384,1024]{1,0:T(8,128)(2,1)}, u32[]{:S(2)}, u32[]{:S(2)}) collective-permute-start(bf16[384,1024]{1,0:T(8,128)(2,1)} %convert_element_type.77), channel_id=1, source_target_pairs={{0,4},{4,0},{1,5},{5,1},{2,6},{6,2},{3,7},{7,3},{8,12},{12,8},{9,1... | collective-permute-start | bytes 2359304 | tf_op jit(solution)/shard_map/ppermute | solution.py:1159
  476.7 128.2 %collective-permute-start.2 = (bf16[384,1024]{1,0:T(8,128)(2,1)}, bf16[384,1024]{1,0:T(8,128)(2,1)}, u32[]{:S(2)}, u32[]{:S(2)}) collective-permute-start(bf16[384,1024]{1,0:T(8,128)(2,1)} %convert_element_type.75), channel_id=1, source_target_pairs={{0,4},{4,0},{1,5},{5,1},{2,6},{6,2},{3,7},{7,3},{8,12},{12,8},{9,1... | collective-permute-start | bytes 2359304 | tf_op jit(solution)/shard_map/ppermute | solution.py:1159
  479.3 121.5 %copy-start.15 = (f32[1,1152]{1,0:T(1,128)S(1)}, f32[1,1152]{1,0:T(1,128)}, u32[]{:S(2)}) copy-start(f32[1,1152]{1,0:T(1,128)} %get-tuple-element.210) | copy-start | bytes 13828
  600.8 4.1 copy-start.10
  607.3 1.7 copy-start.11
  648.4 168.0 %reduce-scatter.8.cloned.1.call-start = ((), (), s32[]{:S(2)}) async-start(), calls=%async_computation.7 | async-start | bytes 7520256 | tf_op jit(solution)/shard_map/reduce_scatter | solution.py:1218
  703.0 294.2 %reduce-scatter.10.cloned.1.call-start = ((), (), s32[]{:S(2)}) async-start(), calls=%async_computation.8 | async-start | bytes 17860608
  703.1 9.9 copy-start.12
  703.1 9.9 copy-start.13
  722.2 276.6 %collective-permute-start.4 = (bf16[72,2048]{1,0:T(8,128)(2,1)}, bf16[72,2048]{1,0:T(8,128)(2,1)S(1)}, u32[]{:S(2)}, u32[]{:S(2)}) collective-permute-start(bf16[72,2048]{1,0:T(8,128)(2,1)} %reduce-scatter.6.cloned.1.call-done), channel_id=1, source_target_pairs={{0,4},{4,0},{1,5},{5,1},{2,6},{6,2},{3,7},{7,3},{8,12},{12,8},{9,1... | collective-permute-start | bytes 884744 | tf_op jit(solution)/shard_map/ppermute | solution.py:1159
  816.4 185.6 %collective-permute-start.6 = (bf16[192,1152]{1,0:T(8,128)(2,1)}, bf16[192,1152]{1,0:T(8,128)(2,1)S(1)}, u32[]{:S(2)}, u32[]{:S(2)}) collective-permute-start(bf16[192,1152]{1,0:T(8,128)(2,1)} %reduce-scatter.8.cloned.1.call-done), channel_id=1, source_target_pairs={{0,4},{4,0},{1,5},{5,1},{2,6},{6,2},{3,7},{7,3},{8,12},{12,8},{9,1... | collective-permute-start | bytes 1327112 | tf_op jit(solution)/shard_map/ppermute | solution.py:1159
  997.3 25.0 %copy-start.14 = (bf16[72,7296]{1,0:T(8,128)(2,1)S(1)}, bf16[72,7296]{1,0:T(8,128)(2,1)}, u32[]{:S(2)}) copy-start(bf16[72,7296]{1,0:T(8,128)(2,1)} %reduce-scatter.10.cloned.1.call-done) | copy-start | bytes 3151876
  997.3 25.0 %collective-permute-start.5 = (bf16[72,7296]{1,0:T(8,128)(2,1)}, bf16[72,7296]{1,0:T(8,128)(2,1)S(1)}, u32[]{:S(2)}, u32[]{:S(2)}) collective-permute-start(bf16[72,7296]{1,0:T(8,128)(2,1)} %reduce-scatter.10.cloned.1.call-done), channel_id=1, source_target_pairs={{0,4},{4,0},{1,5},{5,1},{2,6},{6,2},{3,7},{7,3},{8,12},{12,8},{9,1... | collective-permute-start | bytes 3151880 | tf_op jit(solution)/shard_map/ppermute | solution.py:1159
Sparse Core Ops, SparseCore 0:
  10.9 54.4 all-gather.3
  66.9 87.7 all-gather.5
  157.0 66.4 all-gather.7
  648.5 73.6 reduce-scatter.5
  726.5 89.7 reduce-scatter.7
  820.5 176.7 reduce-scatter.9

commit v2 on v1

--- a/solution.py
+++ b/solution.py
@@ -37,22 +37,35 @@
     scale = LOG2E * HEAD_WIDTH**-0.5
     cos, sin = cos_ref[...], sin_ref[...]
 
-    def rotated(lin, out_ref, cos, sin):
+    def rotated(lin, out_ref, base, cos, sin):
         worst = jnp.zeros((1, lin.shape[1]), f32)
         for head in range(lin.shape[0] // HEAD_WIDTH):
             at = head * HEAD_WIDTH
             a, b = lin[at : at + half], lin[at + half : at + HEAD_WIDTH]
             first = (a * cos - b * sin).astype(bf16)
             second = (b * cos + a * sin).astype(bf16)
-            out_ref[at : at + half] = first
-            out_ref[at + half : at + HEAD_WIDTH] = second
+            out_ref[base + at : base + at + half] = first
+            out_ref[base + at + half : base + at + HEAD_WIDTH] = second
             fa, fb = first.astype(f32), second.astype(f32)
             worst = jnp.maximum(worst, jnp.sum(fa * fa + fb * fb, axis=0, keepdims=True))
         return worst
 
-    nk_ref[...] = rotated(contract(w_ref[:, q_rows : q_rows + kv_rows], h, 0, 1), k_ref, cos, sin)
-    v_ref[...] = contract(w_ref[:, q_rows + kv_rows : q_rows + 2 * kv_rows], h, 0, 1).astype(bf16)
-    nq_ref[...] = rotated(contract(w_ref[:, :q_rows], h, 0, 1), q_ref, cos * scale, sin * scale)
+    ht = h.T
+    chunk = kv_rows
+    qc, qs = cos * scale, sin * scale
+    worst_q = worst_k = None
+    for at in range(0, q_rows + 2 * kv_rows, chunk):
+        lin = contract(w_ref[:, at : at + chunk], ht, 0, 0)
+        if at < q_rows:
+            worst = rotated(lin, q_ref, at, qc, qs)
+            worst_q = worst if worst_q is None else jnp.maximum(worst_q, worst)
+        elif at < q_rows + kv_rows:
+            worst = rotated(lin, k_ref, at - q_rows, cos, sin)
+            worst_k = worst if worst_k is None else jnp.maximum(worst_k, worst)
+        else:
+            v_ref[pl.ds(at - q_rows - kv_rows, chunk)] = lin.astype(bf16)
+    nq_ref[...] = worst_q
+    nk_ref[...] = worst_k
 
 
 def project(x, gain, w, cos, sin, q_rows, kv_rows, tile=512):
@@ -251,7 +264,7 @@
 
 def other_backward_kernel(
     seen_ref, q_ref, g_ref, lse_ref, delta_ref, k_ref, v_ref, dq_ref, dk_ref, dv_ref,
-    query_ref, grad_ref, keys_ref, values_ref, *, group, prompt_rows, step
+    query_ref, grad_ref, keys_ref, values_ref, dk_sum, dv_sum, *, group, prompt_rows, step
 ):
     rows = q_ref.shape[1]
     fill_sides(q_ref, g_ref, lse_ref, delta_ref, query_ref, grad_ref, group)
@@ -273,17 +286,20 @@
                 key_sum = key_grad if key_sum is None else key_sum + key_grad
                 value_sum = value_grad if value_sum is None else value_sum + value_grad
             if fresh:
-                dk_ref[:, span] = key_sum
-                dv_ref[:, span] = value_sum
+                dk_sum[:, span] = key_sum
+                dv_sum[:, span] = value_sum
             else:
-                dk_ref[:, span] += key_sum
-                dv_ref[:, span] += value_sum
+                dk_sum[:, span] += key_sum
+                dv_sum[:, span] += value_sum
 
     part(prompt_rows, rows, True)
 
     @pl.when(seen_ref[0] > 0)
     def _():
         part(0, prompt_rows, False)
+
+    dk_ref[...] = dk_sum[...].astype(bf16)
+    dv_ref[...] = dv_sum[...].astype(bf16)
 
 
 def backward_specs(group, rows, key_count):
@@ -306,6 +322,7 @@
     rows = q.shape[1]
     group = q.shape[0] // HEAD_WIDTH // kv_heads
     ins, outs, scratch = backward_specs(group, rows, k.shape[1])
+    scratch += [pltpu.VMEM((HEAD_WIDTH, k.shape[1]), f32)] * 2
     return pl.pallas_call(
         functools.partial(other_backward_kernel, group=group, prompt_rows=prompt_rows, step=step),
         grid_spec=pltpu.PrefetchScalarGridSpec(
@@ -313,8 +330,8 @@
         ),
         out_shape=(
             jax.ShapeDtypeStruct(q.shape, f32),
-            jax.ShapeDtypeStruct(k.shape, f32),
-            jax.ShapeDtypeStruct(v.shape, f32),
+            jax.ShapeDtypeStruct(k.shape, bf16),
+            jax.ShapeDtypeStruct(v.shape, bf16),
         ),
         compiler_params=pltpu.CompilerParams(vmem_limit_bytes=56 * MIB),
         name="other_backward",
@@ -377,15 +394,21 @@
 
 
 def middle_kernel(
-    x_ref, dy_ref, o_ref, gain_ref, wo_any, wg_any, wu_any, wd_any,
+    x_ref, dy_ref, o_ref, gain_ref, wide_any, wd_any,
     out_ref, h2_ref, hidden_ref, dgate_ref, dup_ref, dattn_ref, dob_ref, delta_ref, dgain_ref,
     wo_ref, wg_ref, wu_ref, wd_ref, sems, *, chunk
 ):
     step = pl.program_id(0)
+    inner, total = wo_ref.shape[1], wg_ref.shape[1]
     copies = [
         pltpu.make_async_copy(source, target, sems.at[i])
         for i, (source, target) in enumerate(
-            ((wo_any, wo_ref), (wg_any, wg_ref), (wu_any, wu_ref), (wd_any, wd_ref))
+            (
+                (wide_any.at[:, pl.ds(0, inner)], wo_ref),
+                (wide_any.at[:, pl.ds(inner, total)], wg_ref),
+                (wide_any.at[:, pl.ds(inner + total, total)], wu_ref),
+                (wd_any, wd_ref),
+            )
         )
     ]
 
@@ -416,7 +439,7 @@
         gate = contract(h2, wg_ref[:, span], 1, 0)
         up = contract(h2, wu_ref[:, span], 1, 0)
         dhidden = contract(dy, wd_ref[span], 1, 1)
-        sigma = 1.0 / (1.0 + jnp.exp(-gate))
+        sigma = 0.5 + 0.5 * jnp.tanh(0.5 * gate)
         silu = gate * sigma
         hidden = (silu * up).astype(bf16)
         hidden_ref[:, span] = hidden
@@ -447,9 +470,9 @@
             )
 
 
-def middle(x, dy, o, gain, wo, wg, wu, wd, kv_heads, tile=256, chunk=1024):
+def middle(x, dy, o, gain, wide, wd, kv_heads, tile=256, chunk=768):
     rows, width = x.shape
-    hidden = wg.shape[1]
+    hidden = wd.shape[0]
     q_rows = o.shape[0]
     group = q_rows // HEAD_WIDTH // kv_heads
     by_row = lambda n: pl.BlockSpec((tile, n), lambda i: (i, 0))
@@ -459,7 +482,7 @@
         functools.partial(middle_kernel, chunk=chunk),
         grid=(rows // tile,),
         in_specs=[by_row(width), by_row(width), pl.BlockSpec((q_rows, tile), lambda i: (0, i)),
-                  resident(gain.shape)] + [any_spec] * 4,
+                  resident(gain.shape)] + [any_spec] * 2,
         out_specs=(
             by_row(width), by_row(width), by_row(hidden), by_row(hidden), by_row(hidden), by_row(width),
             pl.BlockSpec((q_rows, tile), lambda i: (0, i)),
@@ -471,37 +494,69 @@
             shape((rows, hidden), bf16), shape((rows, hidden), bf16), shape((rows, width), bf16),
             shape((q_rows, rows), bf16), shape((kv_heads, group, rows), f32), shape((1, width), f32),
         ),
-        scratch_shapes=[pltpu.VMEM(w.shape, bf16) for w in (wo, wg, wu, wd)] + [pltpu.SemaphoreType.DMA((4,))],
+        scratch_shapes=[pltpu.VMEM(s, bf16) for s in ((width, q_rows), (width, hidden), (width, hidden), wd.shape)]
+        + [pltpu.SemaphoreType.DMA((4,))],
         compiler_params=pltpu.CompilerParams(vmem_limit_bytes=62 * MIB),
         name="middle",
-    )(x, dy, o, gain, wo, wg, wu, wd)
-
-
-def ffn_grads_kernel(h2_ref, dy_ref, hidden_ref, dgate_ref, dup_ref, down_ref, gate_ref, up_ref):
+    )(x, dy, o, gain, wide, wd)
+
+
+def down_grads_kernel(dy_ref, hidden_ref, down_ref):
     down_ref[...] = contract(hidden_ref[...], dy_ref[...], 0, 0).astype(bf16)
-    gate_ref[...] = contract(h2_ref[...], dgate_ref[...], 0, 0).astype(bf16)
-    up_ref[...] = contract(h2_ref[...], dup_ref[...], 0, 0).astype(bf16)
-
-
-def ffn_grads(h2, dy, hidden, dgate, dup, tile=512):
+
+
+def down_grads(dy, hidden, tile=512):
+    rows, width = dy.shape
+    total = hidden.shape[1]
+    return pl.pallas_call(
+        down_grads_kernel,
+        grid=(total // tile,),
+        in_specs=[resident(dy.shape), pl.BlockSpec((rows, tile), lambda i: (0, i))],
+        out_specs=pl.BlockSpec((tile, width), lambda i: (i, 0)),
+        out_shape=jax.ShapeDtypeStruct((total, width), bf16),
+        compiler_params=pltpu.CompilerParams(vmem_limit_bytes=56 * MIB),
+        name="down_grads",
+    )(dy, hidden)
+
+
+def wide_grads_kernel(o_ref, h2_ref, dgate_ref, dup_ref, dattn_ref, out_ref, *, each):
+    step = pl.program_id(0)
+
+    @pl.when(step < each)
+    def _():
+        out_ref[...] = contract(h2_ref[...], dgate_ref[...], 0, 0).astype(bf16)
+
+    @pl.when((step >= each) & (step < 2 * each))
+    def _():
+        out_ref[...] = contract(h2_ref[...], dup_ref[...], 0, 0).astype(bf16)
+
+    @pl.when(step >= 2 * each)
+    def _():
+        out_ref[...] = contract(o_ref[...], dattn_ref[...], 1, 0).astype(bf16)
+
+
+def wide_grads(o, h2, dattn, dgate, dup, tile=512):
     rows, width = h2.shape
-    total = hidden.shape[1]
-    cols = lambda n: pl.BlockSpec((n, tile), lambda i: (0, i))
-    shape = jax.ShapeDtypeStruct
+    total = dgate.shape[1]
+    each = total // tile
+    steps = 2 * each + pl.cdiv(width, tile)
+    cols = lambda low, count: pl.BlockSpec((rows, tile), lambda i: (0, jnp.clip(i - low, 0, count - 1)))
     return pl.pallas_call(
-        ffn_grads_kernel,
-        grid=(total // tile,),
-        in_specs=[resident(h2.shape), resident(dy.shape), cols(rows), cols(rows), cols(rows)],
-        out_specs=(pl.BlockSpec((tile, width), lambda i: (i, 0)), cols(width), cols(width)),
-        out_shape=(shape((total, width), bf16), shape((width, total), bf16), shape((width, total), bf16)),
+        functools.partial(wide_grads_kernel, each=each),
+        grid=(steps,),
+        in_specs=[
+            resident(o.shape), resident(h2.shape), cols(0, each), cols(each, each), cols(2 * each, steps - 2 * each)
+        ],
+        out_specs=pl.BlockSpec((width, tile), lambda i: (0, i)),
+        out_shape=jax.ShapeDtypeStruct((width, 2 * total + width), bf16),
         compiler_params=pltpu.CompilerParams(vmem_limit_bytes=56 * MIB),
-        name="ffn_grads",
-    )(h2, dy, hidden, dgate, dup)
+        name="wide_grads",
+    )(o, h2, dgate, dup, dattn)
 
 
 def finish_kernel(
-    x_ref, h_ref, dattn_ref, gain_ref, w_ref, dq_ref, dk_ref, dv_ref, cos_ref, sin_ref,
-    out_ref, dw_ref, dgain_ref, acc_ref
+    x_ref, h_ref, dattn_ref, gain_ref, w_ref, dq_ref, dk_ref, dv_ref, dk_in_ref, dv_in_ref, cos_ref, sin_ref,
+    dgain_f_ref, out_ref, dw_ref, acc_ref, dgain_ref, *, prompt_steps
 ):
     step = pl.program_id(0)
 
@@ -513,22 +568,31 @@
     half = HEAD_WIDTH // 2
     cos, sin = cos_ref[...], sin_ref[...]
 
-    def turned(ref, scale):
+    def with_received(ref, in_ref):
+        return ref[...] + jnp.where(step < prompt_steps, in_ref[...].astype(f32), 0.0)
+
+    def turned(value, scale):
         c, s = cos * scale, sin * scale
         pieces = []
-        for at in range(0, ref.shape[0], HEAD_WIDTH):
-            a, b = ref[at : at + half], ref[at + half : at + HEAD_WIDTH]
+        for at in range(0, value.shape[0], HEAD_WIDTH):
+            a, b = value[at : at + half], value[at + half : at + HEAD_WIDTH]
             pieces += [a * c + b * s, b * c - a * s]
         return jnp.concatenate(pieces, axis=0)
 
     lin = jnp.concatenate(
-        [turned(dq_ref, HEAD_WIDTH**-0.5), turned(dk_ref, LN2), dv_ref[...]], axis=0
+        [
+            turned(dq_ref, HEAD_WIDTH**-0.5),
+            turned(with_received(dk_ref, dk_in_ref), LN2),
+            with_received(dv_ref, dv_in_ref),
+        ],
+        axis=0,
     ).astype(bf16).T
+    inner = lin.shape[1]
     acc_ref[...] += contract(h_ref[...], lin, 0, 0)
-    dh = contract(lin, w_ref[...], 1, 1)
+    dh = contract(lin, w_ref[:, :inner], 1, 1)
     x = x_ref[...].astype(f32)
     inverse = lax.rsqrt(jnp.mean(x * x, axis=-1, keepdims=True) + norm_eps)
-    dgain_ref[...] += jnp.sum(dh * x * inverse, axis=0, keepdims=True)
+    dgain_ref[0:1] += jnp.sum(dh * x * inverse, axis=0, keepdims=True)
     u = dh * gain_ref[...]
     out_ref[...] = (
         dattn_ref[...].astype(f32)
@@ -538,26 +602,241 @@
 
     @pl.when(step == pl.num_programs(0) - 1)
     def _():
-        dw_ref[...] = acc_ref[...].astype(bf16)
-
-
-def finish(x, h, dattn, gain, w, dq, dk, dv, cos, sin, tile=256):
+        dw_ref[:, :inner] = acc_ref[...].astype(bf16)
+        dgain_ref[1:2] = dgain_f_ref[...]
+        dw_ref[:, inner:] = dgain_ref[...].T.astype(bf16)
+
+
+def finish(x, h, dattn, gain, w, dq, dk, dv, dk_in, dv_in, cos, sin, dgain_f, tile=256):
     rows, width = x.shape
     by_row = pl.BlockSpec((tile, width), lambda i: (i, 0))
     cols = lambda n: pl.BlockSpec((n, tile), lambda i: (0, i))
+    steps = dk_in.shape[1] // tile
+    few = lambda n: pl.BlockSpec((n, tile), lambda i: (0, jnp.minimum(i, steps - 1)))
     shape = jax.ShapeDtypeStruct
+    inner = dq.shape[0] + dk.shape[0] + dv.shape[0]
     return pl.pallas_call(
-        finish_kernel,
+        functools.partial(finish_kernel, prompt_steps=steps),
         grid=(rows // tile,),
         in_specs=[by_row, by_row, by_row, resident(gain.shape), resident(w.shape),
                   cols(dq.shape[0]), cols(dk.shape[0]), cols(dv.shape[0]),
-                  cols(cos.shape[0]), cols(cos.shape[0])],
-        out_specs=(by_row, pl.BlockSpec(w.shape, lambda i: (0, 0)), pl.BlockSpec((1, width), lambda i: (0, 0))),
-        out_shape=(shape((rows, width), f32), shape(w.shape, bf16), shape((1, width), f32)),
-        scratch_shapes=[pltpu.VMEM(w.shape, f32)],
+                  few(dk.shape[0]), few(dv.shape[0]),
+                  cols(cos.shape[0]), cols(cos.shape[0]), resident(dgain_f.shape)],
+        out_specs=(by_row, pl.BlockSpec(w.shape, lambda i: (0, 0))),
+        out_shape=(shape((rows, width), f32), shape(w.shape, bf16)),
+        scratch_shapes=[pltpu.VMEM((width, inner), f32), pltpu.VMEM((w.shape[1] - inner, width), f32)],
         compiler_params=pltpu.CompilerParams(vmem_limit_bytes=56 * MIB),
         name="finish",
-    )(x, h, dattn, gain, w, dq, dk, dv, cos, sin)
+    )(x, h, dattn, gain, w, dq, dk, dv, dk_in, dv_in, cos, sin, dgain_f)
+
+
+MESH_ID = pl.DeviceIdType.MESH
+
+
+def whereabouts():
+    z, y, w = lax.axis_index("group"), lax.axis_index("ctx"), lax.axis_index("wshard")
+    return z, y, w // 2, w % 2
+
+
+def device_at(z, y, x, core):
+    return (z, y, x * 2 + core)
+
+
+def slot_at(z, x, core):
+    return z * 4 + x * 2 + core
+
+
+def greet(partners):
+    barrier = pltpu.get_barrier_semaphore()
+    for partner in partners:
+        pl.semaphore_signal(barrier, inc=1, device_id=partner, device_id_type=MESH_ID)
+    pl.semaphore_wait(barrier, len(partners))
+
+
+def neighbours(depth):
+    z, y, x, core = whereabouts()
+    along = [device_at((z + d) % depth, y, x, core) for d in range(1, depth)]
+    return along, device_at(z, y, 1 - x, core), device_at(z, 1 - y, x, core), device_at(z, y, x, 1 - core)
+
+
+class Copies:
+    def __init__(self, send_sems, recv_sems):
+        self.send_sems, self.recv_sems, self.made = send_sems, recv_sems, []
+
+    def make(self, source, target, device):
+        at = len(self.made)
+        copy = pltpu.make_async_remote_copy(
+            src_ref=source,
+            dst_ref=target,
+            send_sem=self.send_sems.at[at],
+            recv_sem=self.recv_sems.at[at],
+            device_id=device,
+            device_id_type=MESH_ID,
+        )
+        self.made.append(copy)
+        return copy
+
+
+def gather_kernel(shard_ref, out_ref, send_sems, recv_sems, own_sem, *, depth, split):
+    z, y, x, core = whereabouts()
+    along, over_x, over_y, over_core = neighbours(depth)
+    columns = out_ref.shape[2]
+    mine = pl.ds(pl.multiple_of(y * split, 128), columns - split)
+    given = pl.ds(pl.multiple_of(y * (columns - split), 128), split)
+    got = pl.ds(pl.multiple_of((1 - y) * (columns - split), 128), split)
+    me = slot_at(z, x, core)
+    copies = Copies(send_sems, recv_sems)
+    view = lambda slot, span: out_ref.at[slot, :, span]
+
+    own = pltpu.make_async_copy(shard_ref, out_ref.at[me], own_sem)
+    own.start()
+    own.wait()
+    greet(along + [over_x, over_y, over_core])
+
+    def send(slot, span, device):
+        copy = copies.make(view(slot, span), view(slot, span), device)
+        copy.start()
+        return copy
+
+    from_z = [send(me, mine, device) for device in along]
+    from_x = {0: send(me, mine, over_x)}
+    from_y = {(0, 0): send(me, given, over_y)}
+    from_core = [send(me, mine, over_core)]
+    for d in range(1, depth):
+        from_z[d - 1].wait_recv()
+        slot = slot_at((z + depth - d) % depth, x, core)
+        from_x[d] = send(slot, mine, over_x)
+        from_y[d, 0] = send(slot, given, over_y)
+        from_core.append(send(slot, mine, over_core))
+    for d in range(depth):
+        from_x[d].wait_recv()
+        slot = slot_at((z + depth - d) % depth, 1 - x, core)
+        from_y[d, 1] = send(slot, given, over_y)
+        from_core.append(send(slot, mine, over_core))
+    for other in range(2):
+        for d in range(depth):
+            from_y[d, other].wait_recv()
+            slot = slot_at((z + depth - d) % depth, x if other == 0 else 1 - x, core)
+            from_core.append(send(slot, got, over_core))
+    for copy in from_core:
+        copy.wait_recv()
+    for copy in copies.made:
+        copy.wait_send()
+
+
+def gather_all(shard, depth, split):
+    rows, columns = shard.shape
+    count = 8 * depth - 1
+    return pl.pallas_call(
+        functools.partial(gather_kernel, depth=depth, split=split),
+        in_specs=[pl.BlockSpec(memory_space=pltpu.VMEM)],
+        out_specs=pl.BlockSpec(memory_space=pltpu.VMEM),
+        out_shape=jax.ShapeDtypeStruct((4 * depth, rows, columns), shard.dtype),
+        scratch_shapes=[
+            pltpu.SemaphoreType.DMA((count,)),
+            pltpu.SemaphoreType.DMA((count,)),
+            pltpu.SemaphoreType.DMA,
+        ],
+        compiler_params=pltpu.CompilerParams(
+            collective_id=1, has_side_effects=True, vmem_limit_bytes=32 * MIB
+        ),
+        name="gather_all",
+    )(shard)
+
+
+def reduce_kernel(
+    part_ref, out_ref, core_ref, y_ref, sum_ref, x_ref, line_ref, z_ref, last_ref, twin_ref, send_sems, recv_sems,
+    *, depth, split
+):
+    z, y, x, core = whereabouts()
+    along, over_x, over_y, over_core = neighbours(depth)
+    columns = part_ref.shape[2]
+    copies = Copies(send_sems, recv_sems)
+    greet(along + [over_x, over_y, over_core])
+
+    def send(source, target, device):
+        copy = copies.make(source, target, device)
+        copy.start()
+        return copy
+
+    order = [(d, side) for side in (1, 0) for d in list(range(1, depth)) + [0]]
+    place = lambda d, side: ((z + d) % depth, x if side == 0 else 1 - x)
+    from_core = []
+    for at, (d, side) in enumerate(order):
+        to_z, to_x = place(d, side)
+        from_core.append(send(part_ref.at[slot_at(to_z, to_x, 1 - core)], core_ref.at[at], over_core))
+    low, high = split, columns - split
+
+    def halves(at, to_z, to_x):
+        total = part_ref[slot_at(to_z, to_x, core)].astype(f32) + core_ref[at].astype(f32)
+        left, middle_, right = total[:, :low], total[:, low:high], total[:, high:]
+        is_low = y == 0
+        sum_ref[at, :, :low] = jnp.where(is_low, left, right).astype(bf16)
+        sum_ref[at, :, low:high] = middle_.astype(bf16)
+        sum_ref[at, :, high:] = jnp.where(is_low, right, left).astype(bf16)
+
+    from_y = []
+    for at, (d, side) in enumerate(order):
+        from_core[at].wait_recv()
+        halves(at, *place(d, side))
+        from_y.append(send(sum_ref.at[at, :, pl.ds(high, split)], y_ref.at[at], over_y))
+    from_x = []
+    for at, (d, side) in enumerate(order):
+        from_y[at].wait_recv()
+        sum_ref[at, :, :low] = (sum_ref[at, :, :low].astype(f32) + y_ref[at].astype(f32)).astype(bf16)
+        if side == 1:
+            from_x.append(send(sum_ref.at[at, :, pl.ds(0, high)], x_ref.at[at], over_x))
+    from_z = []
+    for index, d in enumerate(list(range(1, depth)) + [0]):
+        at = depth + index
+        from_x[index].wait_recv()
+        total = (sum_ref[at, :, :high].astype(f32) + x_ref[index].astype(f32)).astype(bf16)
+        line_ref[index] = total
+        if d:
+            from_z.append(send(line_ref.at[index], z_ref.at[index], along[d - 1]))
+    total = line_ref[depth - 1].astype(f32)
+    for index in range(depth - 1):
+        from_z[index].wait_recv()
+        total = total + z_ref[index].astype(f32)
+    last_ref[...] = total.astype(bf16)
+    twin = send(last_ref, twin_ref, over_y)
+    twin.wait_recv()
+    theirs = twin_ref[...].astype(f32)
+    is_low = y == 0
+    out_ref[:, :low] = jnp.where(is_low, total[:, :low], theirs[:, :low])
+    out_ref[:, low:high] = total[:, low:] + theirs[:, low:]
+    out_ref[:, high:] = jnp.where(is_low, theirs[:, :low], total[:, :low])
+    for copy in copies.made:
+        copy.wait_send()
+
+
+def reduce_all(parts, depth, split):
+    slots, rows, columns = parts.shape
+    high = columns - split
+    count = 2 * depth + 2 * depth + depth + depth - 1 + 1
+    buffer = lambda *shape: pltpu.VMEM(shape, bf16)
+    return pl.pallas_call(
+        functools.partial(reduce_kernel, depth=depth, split=split),
+        in_specs=[pl.BlockSpec(memory_space=pltpu.VMEM)],
+        out_specs=pl.BlockSpec(memory_space=pltpu.VMEM),
+        out_shape=jax.ShapeDtypeStruct((rows, columns), f32),
+        scratch_shapes=[
+            buffer(2 * depth, rows, columns),
+            buffer(2 * depth, rows, split),
+            buffer(2 * depth, rows, columns),
+            buffer(depth, rows, high),
+            buffer(depth, rows, high),
+            buffer(depth - 1, rows, high),
+            buffer(rows, high),
+            buffer(rows, high),
+            pltpu.SemaphoreType.DMA((count,)),
+            pltpu.SemaphoreType.DMA((count,)),
+        ],
+        compiler_params=pltpu.CompilerParams(
+            collective_id=2, has_side_effects=True, vmem_limit_bytes=40 * MIB
+        ),
+        name="reduce_all",
+    )(parts)
 
 
 rope_base = 10000.0
@@ -1174,21 +1453,19 @@
     seen = (block > 0).astype(jnp.int32)
     prompt_total = block_map.shape[1] // 2 * prompt_rows
 
-    gains = jnp.stack([attention_gain, feedforward_gain], axis=1)
-    gains = jnp.pad(gains, ((0, 0), (0, 126)))
-    first = lax.all_gather(
-        jnp.concatenate([query_weight, key_matrix, value_matrix, gains], axis=1), OWNERS, axis=0, tiled=True
-    )
-    second = lax.all_gather(
+    depth = lax.axis_size("group")
+
+    gains = jnp.pad(jnp.stack([attention_gain, feedforward_gain], axis=1), ((0, 0), (0, 126)))
+    wide = lax.all_gather(
         jnp.concatenate([output_weight, gate_weight, up_weight], axis=1), OWNERS, axis=0, tiled=True
     )
     wd = lax.all_gather(down_weight, OWNERS, axis=0, tiled=True)
-    w_qkv = first[:, : q_rows + 2 * kv_rows]
-    gain_pair = first[:, q_rows + 2 * kv_rows : q_rows + 2 * kv_rows + 2].astype(f32).T
+    shard = jnp.concatenate([query_weight, key_matrix, value_matrix, gains], axis=1)
+    end = q_rows + 2 * kv_rows
+    split = shard.shape[1] // 3 // 128 * 128
+    first = gather_all(shard, depth, split).reshape(width, -1)
+    gain_pair = first[:, end : end + 2].astype(f32).T
     gain_a, gain_f = gain_pair[0:1], gain_pair[1:2]
-    wo = second[:, :q_rows]
-    wg = second[:, q_rows : q_rows + hidden]
-    wu = second[:, q_rows + hidden :]
 
     at = jnp.arange(rows, dtype=jnp.int32)
     positions = jnp.where(
@@ -1199,40 +1476,39 @@
     angles = frequency[:, None] * positions.astype(f32)[None, :]
     cos, sin = jnp.cos(angles), jnp.sin(angles)
 
-    q, k, v, h1, norm_q, norm_k = project(x, gain_a, w_qkv, cos, sin, q_rows, kv_rows)
+    q, k, v, h1, norm_q, norm_k = project(x, gain_a, first, cos, sin, q_rows, kv_rows)
     k_other, v_other = swap(k[:, :prompt_rows]), swap(v[:, :prompt_rows])
     acc = own_forward(q, k, v, kv_heads, prompt_rows)
     other_norm = jnp.max(jnp.sum(jnp.square(k_other.astype(f32)).reshape(kv_heads, HEAD_WIDTH, -1), axis=1))
     bound = jnp.max(norm_q) * jnp.maximum(jnp.max(norm_k), other_norm)
-    o, lse = other_forward(seen[None], q, k_other, v_other, acc, kv_heads, prompt_rows)
     o, lse = lax.cond(
         bound < SAFE_BOUND * SAFE_BOUND,
-        lambda: (o, lse),
+        lambda: other_forward(seen[None], q, k_other, v_other, acc, kv_heads, prompt_rows),
         lambda: exact_attention(seen, q, k, v, k_other, v_other, kv_heads, prompt_rows),
     )
     layer_out, h2, hid, dgate, dup, dattn, dob, delta, dgain_f = middle(
-        x, dy, o, gain_f, wo, wg, wu, wd, kv_heads
-    )
-    d_down, d_gate, d_up = ffn_grads(h2, dy, hid, dgate, dup)
-    d_out = contract(o, dattn, 1, 0).astype(bf16)
+        x, dy, o, gain_f, wide, wd, kv_heads
+    )
     scatter = lambda a: lax.psum_scatter(a, OWNERS, scatter_dimension=0, tiled=True)
-    d_down = scatter(d_down)
-    d_wide = scatter(jnp.concatenate([d_out, d_gate, d_up], axis=1))
-    dq_part, dk_other, dv_other = other_backward(seen[None], q, dob, lse, delta, k_other, v_other, kv_heads, prompt_rows)
-    dk_in, dv_in = swap(dk_other.astype(bf16)), swap(dv_other.astype(bf16))
+    d_down = down_grads(dy, hid)
+    d_wide = wide_grads(o, h2, dattn, dgate, dup)
+    dob, d_down, d_wide = lax.optimization_barrier((dob, d_down, d_wide))
+    d_down, d_wide = scatter(d_down), scatter(d_wide)
+    dq_part, dk_other, dv_other = other_backward(
+        seen[None], q, dob, lse, delta, k_other, v_other, kv_heads, prompt_rows
+    )
+    dk_in, dv_in = swap(dk_other), swap(dv_other)
     dq, dk, dv = own_backward(q, dob, lse, delta, k, v, dq_part, kv_heads, prompt_rows)
-    more = lambda a, b: a.at[:, :prompt_rows].add(b.astype(f32))
-    grad_tokens, d_qkv, dgain_a = finish(
-        x, h1, dattn, gain_a, w_qkv, dq, more(dk, dk_in), more(dv, dv_in), cos, sin
-    )
-    dgains = jnp.pad(jnp.concatenate([dgain_a, dgain_f], axis=0).T, ((0, 0), (0, 126))).astype(bf16)
-    d_first = scatter(jnp.concatenate([d_qkv, dgains], axis=1))
 
     def over_ctx(part):
         return part.astype(f32) + swap(part).astype(f32)
 
-    d_down, d_wide, d_first = over_ctx(d_down), over_ctx(d_wide), over_ctx(d_first)
-    end = q_rows + 2 * kv_rows
+    d_down, d_wide, dq = lax.optimization_barrier((d_down, d_wide, dq))
+    d_down, d_wide = over_ctx(d_down), over_ctx(d_wide)
+    grad_tokens, d_first = finish(
+        x, h1, dattn, gain_a, first, dq, dk, dv, dk_in, dv_in, cos, sin, dgain_f
+    )
+    d_first = reduce_all(d_first.reshape(4 * depth, shard_rows, -1), depth, split)
     return (
         layer_out[None],
         grad_tokens[None],
@@ -1240,17 +1516,22 @@
         d_first[:, :q_rows],
         d_first[:, q_rows : q_rows + kv_rows],
         d_first[:, q_rows + kv_rows : end],
-        d_wide[:, :q_rows],
+        d_wide[:, 2 * hidden :],
         d_first[:, end + 1],
-        d_wide[:, q_rows : q_rows + hidden],
-        d_wide[:, q_rows + hidden :],
+        d_wide[:, :hidden],
+        d_wide[:, hidden : 2 * hidden],
         d_down,
     )
 
 
 def local(mesh, tokens, block_map, *rest):
     block_rows = tokens.shape[1] // 2
-    whole = mesh.shape["ctx"] == 2 and block_rows % CONTINUE_LENGTH == 0 and tokens.shape[0] == 1
+    whole = (
+        mesh.shape["ctx"] == 2
+        and mesh.shape["wshard"] == 4
+        and block_rows % CONTINUE_LENGTH == 0
+        and tokens.shape[0] == 1
+    )
     return (fast_local if whole else general_local)(tokens, block_map, *rest)
 
 

time: 1040 us -> 767 us (0.74)
  waiting for transfers between devices: 356 us -> 33.6 us
  Pallas kernels: 560 us -> 667 us
  other arithmetic: 42.3 us -> 13.6 us
  local copies, waits for them, and re-layouts: 27.8 us -> 16.1 us
    unnamed x7 -> x4, waiting for transfers between devices: 180 us -> 1.24 us
    pallas_call x2 -> x5, Pallas kernels: 87.9 us -> 196 us  [the longest x1 47.3 us: reduce_all(): pl.pallas_call(functools.partial(reduce_kernel, depth=depth, split=split)...]
    reduce_scatter x2 -> x1, waiting for transfers between devices: 95.1 us -> 0.02 us  [fast_local(): lax.psum_scatter(a, OWNERS, scatter_dimension=0, tiled=True)]
    all_gather x1 -> x0, waiting for transfers between devices: 49.5 us -> none  [fast_local(): lax.all_gather(jnp.concatenate([query_weight, key_matrix, value_matrix, g...]
    optimization_barrier x0 -> x1, waiting for transfers between devices: none -> 32.3 us  [fast_local(): d_down, d_wide, dq = lax.optimization_barrier((d_down, d_wide, dq))]
    ppermute x7 -> x6, waiting for transfers between devices: 18.4 us -> 0.02 us  [swap(): return lax.ppermute(array, 'ctx', SWAP)]
    slice x5 -> x2, local copies, waits for them, and re-layouts: 18.4 us -> 2.14 us  [the longest x1 1.39 us: fast_local(): d_wide[:, hidden:2 * hidden]]
    all_gather x1, waiting for transfers between devices: 12.4 us -> 0.01 us  [fast_local(): wd = lax.all_gather(down_weight, OWNERS, axis=0, tiled=True)]
  transfers between devices with their start and end apart: 13 -> 10, of which waited for: 6 -> 1; matrix products, arithmetic and copies ran while one was open for 6% -> 3% of each run, Pallas kernels for 27% -> 61%
where the time goes in v2:
time: 767 us; the launch traced here: 758 us
  Pallas kernels  667 us (87%)
  waiting for transfers between devices  33.6 us (4%)
  between operations  16.8 us (2%)
  local copies, waits for them, and re-layouts  16.1 us (2%)
  other arithmetic  13.6 us (2%)
    pallas_call x1, Pallas kernels, middle(): pl.pallas_call(functools.partial(middle_kernel, chunk=chunk), grid=(rows...  133 us
    pallas_call x1, Pallas kernels, own_backward(): pl.pallas_call(functools.partial(own_backward_kernel, group=group, prompt...  122 us
    pallas_call x1, Pallas kernels, other_backward(): pl.pallas_call(functools.partial(other_backward_kernel, group=group, prom...  114 us
    pallas_call x1, Pallas kernels, reduce_all(): pl.pallas_call(functools.partial(reduce_kernel, depth=depth, split=split)...  47.3 us
    pallas_call x1, Pallas kernels, wide_grads(): pl.pallas_call(functools.partial(wide_grads_kernel, each=each), grid=(ste...  47.3 us
    pallas_call x1, Pallas kernels, own_forward(): pl.pallas_call(functools.partial(own_forward_kernel, group=group, prompt_...  46.4 us
    pallas_call x1, Pallas kernels, gather_all(): pl.pallas_call(functools.partial(gather_kernel, depth=depth, split=split)...  45.8 us
    pallas_call x1, Pallas kernels, other_forward(): pl.pallas_call(functools.partial(other_forward_kernel, group=group, promp...  37.2 us
  transfers between devices with their start and end apart: 10, of which 1 were waited for; matrix products, arithmetic and copies ran while one was open for 3% of the time, Pallas kernels for 61%

profile of v2, /device:TPU:8, one launch (start us, length us, event | category | flops | bytes accessed | tf_op | source)
XLA Modules:
  0.0 758.1 jit_solution(11806740631622001294)
XLA Ops:
  8.0 2.3 pad_maximum_fusion.2
  11.1 1.0 fusion.24.shard_ref
  12.2 45.8 %gather_all.1 = bf16[16,72,2048]{2,1,0:T(8,128)(2,1)S(1)} custom-call(bf16[72,2048]{1,0:T(8,128)(2,1)S(1)} %fusion.24.shard_ref), custom_call_target="tpu_custom_call" | custom-call | tf_op jit(solution)/shard_map/gather_all/pallas_call | solution.py:730
  58.0 2.1 copy-done
  60.2 1.0 fusion.34
  62.7 1.0 multiply_sine_fusion
  63.7 19.0 %project.1 = (bf16[1152,2048]{1,0:T(8,128)(2,1)}, bf16[384,2048]{1,0:T(8,128)(2,1)S(1)}, bf16[384,2048]{1,0:T(8,128)(2,1)S(1)}, bf16[2048,1152]{1,0:T(8,128)(2,1...) custom-call(bf16[2048,1152]{1,0:T(8,128)(2,1)} %bitcast.58, f32[1,1152]{1,0:T(1,128)S(1)} %copy.38.gain_ref, ...), custom_call_target="tpu_custom_call" | custom-call | tf_op jit(solution)/shard_map/project/pallas_call | solution.py:74
  82.8 2.2 copy-done.1
  84.9 1.0 slice.41
  86.5 0.9 slice.42
  87.5 1.4 collective-permute-start.1
  89.6 1.9 copy.39.gain_ref
  92.7 46.4 %own_forward.1 = f32[1440,2048]{1,0:T(8,128)} custom-call(bf16[1152,2048]{1,0:T(8,128)(2,1)} %get-tuple-element.182.q_ref, bf16[384,2048]{1,0:T(8,128)(2,1)S(1)} %get-tuple-element.180.k_ref, bf16[384,2048]{1,0:T(8,128)(2,1)S(1)} %get-tuple-element.181.v_ref), custom_call_target="tpu_custom_call" | custom-call | tf_op jit(solution)/shard_map/own_forward/pallas_call | solution.py:159
  139.0 2.5 convert_multiply_fusion
  141.5 1.7 reduce_sum.21
  145.8 41.6 %conditional.1 = ((bf16[1152,2048]{1,0:T(8,128)(2,1)}, f32[6,3,2048]{2,1,0:T(4,128)S(1)})) conditional(s32[]{:T(128)} %convert_element_type.48, (bf16[384,1024]{1,0:T(8,128)(2,1)}, bf16[384,2048]{1,0:T(8,128)(2,1)S(1)}, bf16[384,1024]{1,0:T(8,128)(2,1)}, bf16[384,2048]{1,0:T(8,128)(2,1)S(1)}, s32[]{:T(128)}, ...), branch_computations={%region_4.9_spmd, %region_9.10_spmd} | conditional | flops 1712498688 | bytes 149561920 | solution.py:1484
  150.3 37.2 %other_forward.1 = (bf16[1152,2048]{1,0:T(8,128)(2,1)}, f32[6,3,2048]{2,1,0:T(4,128)S(1)}) custom-call(s32[1]{0:T(128)} %bitcast.10.seen_ref, bf16[1152,2048]{1,0:T(8,128)(2,1)} %get-tuple-element.132.q_ref, bf16[384,1024]{1,0:T(8,128)(2,1)} %get-tuple-element.133.k_ref, bf16[384,1024]{1,0:T(8,128)(2,1)} %get-tuple-element.134.v_ref, ...), custom_call_target="tpu_custom_call" | custom-call | tf_op jit(solution)/shard_map/cond/branch_1_fun/other_forward/pallas_call | solution.py:204
  187.4 133.0 %middle.1 = (bf16[2048,1152]{1,0:T(8,128)(2,1)}, bf16[2048,1152]{1,0:T(8,128)(2,1)}, bf16[2048,3072]{1,0:T(8,128)(2,1)}, bf16[2048,3072]{1,0:T(8,128)(2,1)}, bf1...) custom-call(bf16[2048,1152]{1,0:T(8,128)(2,1)} %bitcast.59, ...), custom_call_target="tpu_custom_call" | custom-call | tf_op jit(solution)/shard_map/middle/pallas_call | solution.py:481
  320.5 21.6 %down_grads.1 = bf16[3072,1152]{1,0:T(8,128)(2,1)} custom-call(bf16[2048,1152]{1,0:T(8,128)(2,1)} %bitcast.63, bf16[2048,3072]{1,0:T(8,128)(2,1)} %get-tuple-element.188.hidden_ref), custom_call_target="tpu_custom_call" | custom-call | tf_op jit(solution)/shard_map/down_grads/pallas_call | solution.py:511
  342.1 47.3 %wide_grads.1 = bf16[1152,7296]{1,0:T(8,128)(2,1)} custom-call(bf16[1152,2048]{1,0:T(8,128)(2,1)} %get-tuple-element.183.o_ref, bf16[2048,1152]{1,0:T(8,128)(2,1)} %get-tuple-element.189.h2_ref, bf16[2048,3072]{1,0:T(8,128)(2,1)} %get-tuple-element.190.dgate_ref, bf16[2048,3072]{1,0:T(8,128)(2,1)} %get-tuple-element.191.dup_ref, ...), custom_call_target="tpu_custom_call" | custom-call | tf_op jit(solution)/shard_map/wide_grads/pallas_call | solution.py:544
  390.1 113.7 %other_backward.1 = (f32[1152,2048]{1,0:T(8,128)}, bf16[384,1024]{1,0:T(8,128)(2,1)}, bf16[384,1024]{1,0:T(8,128)(2,1)}) custom-call(s32[1]{0:T(128)} %bitcast.21.seen_ref, bf16[1152,2048]{1,0:T(8,128)(2,1)} %get-tuple-element.182.q_ref, bf16[1152,2048]{1,0:T(8,128)(2,1)} %get-tuple-element.194.g_ref, f32[6,3,2048]{2,1,0:T(4,128)S(1)} %get-tuple-element.195.lse_ref, ...), custom_call_target="tpu_custom_call" | custom-call | tf_op jit(solution)/shard_map/other_backward/pallas_call | solution.py:326
  503.8 2.0 collective-permute-start.3
  505.8 122.0 %own_backward.1 = (f32[1152,2048]{1,0:T(8,128)}, f32[384,2048]{1,0:T(8,128)}, f32[384,2048]{1,0:T(8,128)}) custom-call(bf16[1152,2048]{1,0:T(8,128)(2,1)} %get-tuple-element.182.q_ref, bf16[1152,2048]{1,0:T(8,128)(2,1)} %get-tuple-element.194.g_ref, f32[6,3,2048]{2,1,0:T(4,128)S(1)} %get-tuple-element.195.lse_ref, ...), custom_call_target="tpu_custom_call" | custom-call | tf_op jit(solution)/shard_map/own_backward/pallas_call | solution.py:380
  627.9 32.3 %reduce-scatter.7.cloned.1.call-done = bf16[72,7296]{1,0:T(8,128)(2,1)} async-done(((bf16[1152,7296]{1,0:T(8,128)(2,1)}), bf16[72,7296]{1,0:T(8,128)(2,1)}) %reduce-scatter.7.cloned.1.call-update) | async-done | bytes 1050640 | tf_op jit(solution)/shard_map/optimization_barrier | solution.py:1506
  660.2 1.5 collective-permute-start.4
  662.2 33.9 %finish.1 = (f32[2048,1152]{1,0:T(8,128)}, bf16[1152,2048]{1,0:T(8,128)(2,1)}) custom-call(bf16[2048,1152]{1,0:T(8,128)(2,1)} %bitcast.60, bf16[2048,1152]{1,0:T(8,128)(2,1)} %copy-done.1, bf16[2048,1152]{1,0:T(8,128)(2,1)} %get-tuple-element.186.dattn_ref, f32[1,1152]{1,0:T(1,128)} %copy-done.5, bf16[1152,2048]{1,0:T(8,128)(2,1)} %bitcast.55, ...), custom_call_target="tpu_custom_call" | custom-call | tf_op jit(solution)/shard_map/finish/pallas_call | solution.py:618
  696.2 2.3 copy-done.2
  698.5 47.3 %reduce_all.1 = f32[72,2048]{1,0:T(8,128)S(1)} custom-call(bf16[16,72,2048]{2,1,0:T(8,128)(2,1)S(1)} %bitcast.56), custom_call_target="tpu_custom_call" | custom-call | tf_op jit(solution)/shard_map/reduce_all/pallas_call | solution.py:818
  745.8 0.8 slice.45
  748.0 1.0 convert_add_fusion.1
  749.2 0.7 slice.55
  750.0 1.4 fusion.32
  (52 shorter events, 8.5 us)
Async XLA Ops:
  7.2 180.3 %all-gather.5.cloned.1.call-start = ((), (), s32[]{:S(2)}) async-start(), calls=%async_computation.3 | async-start | bytes 7520256 | tf_op jit(solution)/shard_map/all_gather | solution.py:1462
  7.9 179.5 %all-gather.3.cloned.1.call-start = ((), (), s32[]{:S(2)}) async-start(), calls=%async_computation.2 | async-start | bytes 17860608 | tf_op jit(solution)/shard_map/all_gather | solution.py:1459
  10.3 617.6 %reduce-scatter.5.cloned.1.call-start = ((), (), s32[]{:S(2)}) async-start(), calls=%async_computation.4 | async-start | bytes 7520256 | tf_op jit(solution)/shard_map/reduce_scatter | solution.py:1492
  11.1 50.3 %copy-start.11 = (s32[1,4]{1,0:T(1,128)S(1)}, s32[1,4]{1,0:T(1,128)}, u32[]{:S(2)}) copy-start(s32[1,4]{1,0:T(1,128)} %param.17) | copy-start | bytes 52
  57.9 2.1 copy-start
  61.4 21.4 %copy-start.5 = (f32[1,1152]{1,0:T(1,128)}, f32[1,1152]{1,0:T(1,128)S(1)}, u32[]{:S(2)}) copy-start(f32[1,1152]{1,0:T(1,128)S(1)} %copy.38.gain_ref) | copy-start | bytes 13828
  63.7 19.1 %copy-start.3 = (f32[32,2048]{1,0:T(8,128)}, f32[32,2048]{1,0:T(8,128)S(1)}, u32[]{:S(2)}) copy-start(f32[32,2048]{1,0:T(8,128)S(1)} %get-tuple-element.237.sin_ref) | copy-start | bytes 786436
  63.7 19.1 %copy-start.4 = (f32[32,2048]{1,0:T(8,128)}, f32[32,2048]{1,0:T(8,128)S(1)}, u32[]{:S(2)}) copy-start(f32[32,2048]{1,0:T(8,128)S(1)} %get-tuple-element.238.cos_ref) | copy-start | bytes 786436
  82.7 2.2 copy-start.1
  84.9 60.9 %copy-start.7 = (bf16[384,2048]{1,0:T(8,128)(2,1)}, bf16[384,2048]{1,0:T(8,128)(2,1)S(1)}, u32[]{:S(2)}) copy-start(bf16[384,2048]{1,0:T(8,128)(2,1)S(1)} %get-tuple-element.180.k_ref) | copy-start | bytes 4718596
  85.9 53.1 %collective-permute-start = (bf16[384,1024]{1,0:T(8,128)(2,1)}, bf16[384,1024]{1,0:T(8,128)(2,1)}, u32[]{:S(2)}, u32[]{:S(2)}) collective-permute-start(bf16[384,1024]{1,0:T(8,128)(2,1)} %slice.41), channel_id=1, source_target_pairs={{0,4},{4,0},{1,5},{5,1},{2,6},{6,2},{3,7},{7,3},{8,12},{12,8},{9,1... | collective-permute-start | bytes 2359304 | tf_op jit(solution)/shard_map/ppermute | solution.py:1438
  87.5 58.3 %collective-permute-start.1 = (bf16[384,1024]{1,0:T(8,128)(2,1)}, bf16[384,1024]{1,0:T(8,128)(2,1)}, u32[]{:S(2)}, u32[]{:S(2)}) collective-permute-start(bf16[384,1024]{1,0:T(8,128)(2,1)} %slice.42), channel_id=1, source_target_pairs={{0,4},{4,0},{1,5},{5,1},{2,6},{6,2},{3,7},{7,3},{8,12},{12,8},{9,1... | collective-permute-start | bytes 2359304 | tf_op jit(solution)/shard_map/ppermute | solution.py:1438
  389.5 270.7 %reduce-scatter.7.cloned.1.call-start = ((), (), s32[]{:S(2)}) async-start(), calls=%async_computation.5 | async-start | bytes 17860608
  390.0 115.8 %copy-start.8 = (bf16[384,2048]{1,0:T(8,128)(2,1)S(1)}, bf16[384,2048]{1,0:T(8,128)(2,1)}, u32[]{:S(2)}) copy-start(bf16[384,2048]{1,0:T(8,128)(2,1)} %copy-done.7) | copy-start | bytes 4718596
  503.8 158.4 %collective-permute-start.2 = (bf16[384,1024]{1,0:T(8,128)(2,1)}, bf16[384,1024]{1,0:T(8,128)(2,1)}, u32[]{:S(2)}, u32[]{:S(2)}) collective-permute-start(bf16[384,1024]{1,0:T(8,128)(2,1)} %get-tuple-element.202), channel_id=1, source_target_pairs={{0,4},{4,0},{1,5},{5,1},{2,6},{6,2},{3,7},{7,3},{8,12},{12,8},{9,1... | collective-permute-start | bytes 2359304 | tf_op jit(solution)/shard_map/ppermute | solution.py:1438
  503.8 158.4 %collective-permute-start.3 = (bf16[384,1024]{1,0:T(8,128)(2,1)}, bf16[384,1024]{1,0:T(8,128)(2,1)}, u32[]{:S(2)}, u32[]{:S(2)}) collective-permute-start(bf16[384,1024]{1,0:T(8,128)(2,1)} %get-tuple-element.203), channel_id=1, source_target_pairs={{0,4},{4,0},{1,5},{5,1},{2,6},{6,2},{3,7},{7,3},{8,12},{12,8},{9,1... | collective-permute-start | bytes 2359304 | tf_op jit(solution)/shard_map/ppermute | solution.py:1438
  660.2 88.8 %collective-permute-start.4 = (bf16[72,7296]{1,0:T(8,128)(2,1)}, bf16[72,7296]{1,0:T(8,128)(2,1)S(1)}, u32[]{:S(2)}, u32[]{:S(2)}) collective-permute-start(bf16[72,7296]{1,0:T(8,128)(2,1)} %reduce-scatter.7.cloned.1.call-done), channel_id=1, source_target_pairs={{0,4},{4,0},{1,5},{5,1},{2,6},{6,2},{3,7},{7,3},{8,12},{12,8},{9,1... | collective-permute-start | bytes 3151880 | tf_op jit(solution)/shard_map/ppermute | solution.py:1438
  661.6 86.4 %collective-permute-start.5 = (bf16[192,1152]{1,0:T(8,128)(2,1)}, bf16[192,1152]{1,0:T(8,128)(2,1)S(1)}, u32[]{:S(2)}, u32[]{:S(2)}) collective-permute-start(bf16[192,1152]{1,0:T(8,128)(2,1)} %reduce-scatter.5.cloned.1.call-done), channel_id=1, source_target_pairs={{0,4},{4,0},{1,5},{5,1},{2,6},{6,2},{3,7},{7,3},{8,12},{12,8},{9,1... | collective-permute-start | bytes 1327112 | tf_op jit(solution)/shard_map/ppermute | solution.py:1438
  662.2 85.8 %copy-start.10 = (bf16[192,1152]{1,0:T(8,128)(2,1)S(1)}, bf16[192,1152]{1,0:T(8,128)(2,1)}, u32[]{:S(2)}) copy-start(bf16[192,1152]{1,0:T(8,128)(2,1)} %reduce-scatter.5.cloned.1.call-done) | copy-start | bytes 1327108
  662.2 86.8 %copy-start.9 = (bf16[72,7296]{1,0:T(8,128)(2,1)S(1)}, bf16[72,7296]{1,0:T(8,128)(2,1)}, u32[]{:S(2)}) copy-start(bf16[72,7296]{1,0:T(8,128)(2,1)} %reduce-scatter.7.cloned.1.call-done) | copy-start | bytes 3151876
  696.2 2.3 copy-start.2
Sparse Core Ops, SparseCore 0:
  10.3 79.6 all-gather.4
  91.5 87.9 all-gather.2
  389.6 88.9 reduce-scatter.4
  483.3 176.8 reduce-scatter.6

commit v3 on v2

--- a/solution.py
+++ b/solution.py
@@ -27,11 +27,10 @@
     return pl.BlockSpec(shape, lambda *_: zeros, pipeline_mode=pl.Buffered(1))
 
 
-def project_kernel(x_ref, gain_ref, w_ref, cos_ref, sin_ref, q_ref, k_ref, v_ref, h_ref, nq_ref, nk_ref):
+def project_kernel(x_ref, gain_ref, w_ref, cos_ref, sin_ref, q_ref, k_ref, v_ref, kv_ref, nq_ref, nk_ref, *, prompt_steps):
     x = x_ref[...].astype(f32)
     inverse = lax.rsqrt(jnp.mean(x * x, axis=-1, keepdims=True) + norm_eps)
     h = (x * inverse * gain_ref[...]).astype(bf16)
-    h_ref[...] = h
     q_rows, kv_rows = q_ref.shape[0], k_ref.shape[0]
     half = HEAD_WIDTH // 2
     scale = LOG2E * HEAD_WIDTH**-0.5
@@ -67,12 +66,18 @@
     nq_ref[...] = worst_q
     nk_ref[...] = worst_k
 
-
-def project(x, gain, w, cos, sin, q_rows, kv_rows, tile=512):
+    @pl.when(pl.program_id(0) < prompt_steps)
+    def _():
+        kv_ref[0] = k_ref[...]
+        kv_ref[1] = v_ref[...]
+
+
+def project(x, gain, w, cos, sin, q_rows, kv_rows, prompt_rows, tile=512):
     rows, width = x.shape
+    prompt_steps = prompt_rows // tile
     cols = lambda n: pl.BlockSpec((n, tile), lambda i: (0, i))
     return pl.pallas_call(
-        project_kernel,
+        functools.partial(project_kernel, prompt_steps=prompt_steps),
         grid=(rows // tile,),
         in_specs=[
             pl.BlockSpec((tile, width), lambda i: (i, 0)),
@@ -85,7 +90,7 @@
             cols(q_rows),
             cols(kv_rows),
             cols(kv_rows),
-            pl.BlockSpec((tile, width), lambda i: (i, 0)),
+            pl.BlockSpec((2, kv_rows, tile), lambda i: (0, 0, jnp.minimum(i, prompt_steps - 1))),
             cols(1),
             cols(1),
         ),
@@ -93,16 +98,18 @@
             jax.ShapeDtypeStruct((q_rows, rows), bf16),
             jax.ShapeDtypeStruct((kv_rows, rows), bf16),
             jax.ShapeDtypeStruct((kv_rows, rows), bf16),
-            jax.ShapeDtypeStruct((rows, width), bf16),
+            jax.ShapeDtypeStruct((2, kv_rows, prompt_rows), bf16),
             jax.ShapeDtypeStruct((1, rows), f32),
             jax.ShapeDtypeStruct((1, rows), f32),
         ),
-        compiler_params=pltpu.CompilerParams(vmem_limit_bytes=48 * MIB),
+        compiler_params=pltpu.CompilerParams(vmem_limit_bytes=60 * MIB),
         name="project",
     )(x, gain, w, cos, sin)
 
 
 ONES = 16
+SAFE_BOUND = 80.0
+FAR = -1e30
 
 
 def causal(keys, columns):
@@ -111,96 +118,204 @@
     )
 
 
-def spans(prompt_rows, rows, step):
-    found = [(0, prompt_rows, prompt_rows, rows, False)]
+def masked(tile, fill):
+    step = tile.shape[0]
+    front = jnp.where(causal(step, step), tile[:, :step], fill)
+    return front if tile.shape[1] == step else jnp.concatenate([front, tile[:, step:]], axis=1)
+
+
+def strips(prompt_rows, rows, step):
+    tiles = []
     at = 0
     while at < rows:
         end = prompt_rows if at < prompt_rows else at + CONTINUE_LENGTH
-        for key in range(at, end, step):
-            found.append((key, key + step, key, end, True))
+        tiles += [(end - key, key, end) for key in range(at, end, step)]
         at = end
-    return found
-
-
-def weigh(keys, query, diagonal):
-    scores = contract(keys, query, 1, 0)
-    weights = jnp.exp2(scores)
-    if diagonal:
-        step = keys.shape[0]
-        front = jnp.where(causal(step, step), weights[:, :step], 0.0)
-        weights = front if weights.shape[1] == step else jnp.concatenate([front, weights[:, step:]], axis=1)
-    return weights.astype(bf16)
-
-
-def own_forward_kernel(q_ref, k_ref, v_ref, acc_ref, *, group, prompt_rows, step):
+    room, laid = [], []
+    for width, key, end in sorted(tiles, reverse=True):
+        for strip in range(len(room) + 1):
+            if strip == len(room):
+                room.append(rows - prompt_rows)
+            if room[strip] >= width:
+                laid.append((key, key, end, strip, rows - prompt_rows - room[strip]))
+                room[strip] -= width
+                break
+    return sorted(laid), len(room) * step
+
+
+def in_parts(row):
+    high = row.astype(bf16)
+    rest = row - high.astype(f32)
+    middle = rest.astype(bf16)
+    low = (rest - middle.astype(f32)).astype(bf16)
+    return jnp.concatenate([high, middle, low, jnp.zeros((ONES - 3, row.shape[1]), bf16)], axis=0)
+
+
+def widened(matrix):
+    return jnp.concatenate([matrix, jnp.ones((matrix.shape[0], ONES), bf16)], axis=1)
+
+
+def head_rows(head):
+    return slice(head * HEAD_WIDTH, (head + 1) * HEAD_WIDTH)
+
+
+def own_forward_kernel(
+    q_ref, k_ref, v_ref, nq_ref, nk_ref, acc_ref, top_ref, p_ref, query_ref, keys_ref, values_ref,
+    *, group, prompt_rows, step
+):
     rows = q_ref.shape[1]
-    keys = k_ref[...].T
-    values = jnp.concatenate([v_ref[...], jnp.ones((ONES, rows), bf16)], axis=0)
     wide = HEAD_WIDTH + ONES
-    started = set()
-    for low, high, first, last, diagonal in spans(prompt_rows, rows, step):
+    tiles, _ = strips(prompt_rows, rows, step)
+
+    keys_ref[...] = widened(k_ref[...].T)
+    values_ref[:HEAD_WIDTH] = v_ref[...]
+    values_ref[HEAD_WIDTH:] = jnp.ones((ONES, rows), bf16)
+    top_ref[...] = jnp.zeros_like(top_ref)
+    for head in range(group):
+        query_ref[head, :HEAD_WIDTH] = q_ref[head_rows(head)]
+        query_ref[head, HEAD_WIDTH:] = jnp.zeros((ONES, rows), bf16)
+
+    @pl.when(jnp.max(nq_ref[...]) * jnp.max(nk_ref[...]) >= SAFE_BOUND * SAFE_BOUND)
+    def _():
         for head in range(group):
-            query = q_ref[head * HEAD_WIDTH : (head + 1) * HEAD_WIDTH, first:last]
-            weights = weigh(keys[low:high], query, diagonal)
-            part = contract(values[:, low:high], weights, 1, 0)
-            at = pl.ds(head * wide, wide)
-            fresh = (low == 0 and not diagonal) or (diagonal and low == 0)
-            if fresh:
-                acc_ref[at, first:last] = part
+            top_ref[0, head : head + 1] = jnp.full((1, rows), FAR, f32)
+            for key, first, end, _, _ in tiles:
+                scores = masked(contract(keys_ref[key : key + step], query_ref[head, :, first:end], 1, 0), FAR)
+                top_ref[0, head : head + 1, first:end] = jnp.maximum(
+                    top_ref[0, head : head + 1, first:end], jnp.max(scores, axis=0, keepdims=True)
+                )
+            scores = contract(keys_ref[:prompt_rows], query_ref[head, :, prompt_rows:], 1, 0)
+            top_ref[0, head : head + 1, prompt_rows:] = jnp.maximum(
+                top_ref[0, head : head + 1, prompt_rows:], jnp.max(scores, axis=0, keepdims=True)
+            )
+        for head in range(group):
+            query_ref[head, HEAD_WIDTH:] = in_parts(-top_ref[0, head : head + 1])
+
+    for head in range(group):
+        weights = jnp.exp2(contract(keys_ref[:prompt_rows], query_ref[head, :, prompt_rows:], 1, 0)).astype(bf16)
+        p_ref[head, :prompt_rows] = weights
+        acc_ref[head * wide : (head + 1) * wide, prompt_rows:] = contract(
+            values_ref[:, :prompt_rows], weights, 1, 0
+        )
+    for key, first, end, strip, column in tiles:
+        for head in range(group):
+            scores = contract(keys_ref[key : key + step], query_ref[head, :, first:end], 1, 0)
+            weights = masked(jnp.exp2(scores), 0.0).astype(bf16)
+            row = prompt_rows + strip * step
+            p_ref[head, row : row + step, column : column + end - first] = weights
+            part = contract(values_ref[:, key : key + step], weights, 1, 0)
+            at = slice(head * wide, (head + 1) * wide)
+            if key == 0:
+                acc_ref[at, first:end] = part
             else:
-                acc_ref[at, first:last] += part
-
-
-def own_forward(q, k, v, kv_heads, prompt_rows, step=256):
+                acc_ref[at, first:end] += part
+
+
+def own_forward(q, k, v, norm_q, norm_k, kv_heads, prompt_rows, step=256):
     rows = q.shape[1]
     group = q.shape[0] // HEAD_WIDTH // kv_heads
-    wide = group * (HEAD_WIDTH + ONES)
+    wide = HEAD_WIDTH + ONES
     block = lambda n: pl.BlockSpec((n, rows), lambda h: (h, 0))
+    _, strip_rows = strips(prompt_rows, rows, step)
+    assert strip_rows == prompt_rows
+    shape = jax.ShapeDtypeStruct
     return pl.pallas_call(
         functools.partial(own_forward_kernel, group=group, prompt_rows=prompt_rows, step=step),
         grid=(kv_heads,),
-        in_specs=[block(group * HEAD_WIDTH), block(HEAD_WIDTH), block(HEAD_WIDTH)],
-        out_specs=block(wide),
-        out_shape=jax.ShapeDtypeStruct((kv_heads * wide, rows), f32),
-        compiler_params=pltpu.CompilerParams(vmem_limit_bytes=56 * MIB),
+        in_specs=[
+            block(group * HEAD_WIDTH), block(HEAD_WIDTH), block(HEAD_WIDTH), resident(norm_q.shape), resident(norm_k.shape)
+        ],
+        out_specs=(
+            block(group * wide),
+            pl.BlockSpec((1, group, rows), lambda h: (h, 0, 0)),
+            pl.BlockSpec((group, 2 * prompt_rows, rows - prompt_rows), lambda h: (h, 0, 0)),
+        ),
+        scratch_shapes=[
+            pltpu.VMEM((group, wide, rows), bf16),
+            pltpu.VMEM((rows, wide), bf16),
+            pltpu.VMEM((wide, rows), bf16),
+        ],
+        out_shape=(
+            shape((kv_heads * group * wide, rows), f32),
+            shape((kv_heads, group, rows), f32),
+            shape((kv_heads * group, 2 * prompt_rows, rows - prompt_rows), bf16),
+        ),
+        compiler_params=pltpu.CompilerParams(vmem_limit_bytes=60 * MIB),
         name="own_forward",
-    )(q, k, v)
-
-
-def other_forward_kernel(seen_ref, q_ref, k_ref, v_ref, acc_ref, o_ref, lse_ref, *, group, prompt_rows):
+    )(q, k, v, norm_q, norm_k)
+
+
+def other_forward_kernel(
+    seen_ref, q_ref, k_ref, v_ref, nq_ref, acc_ref, top_ref, o_ref, own_ref, far_ref, p_ref, query_ref, keys_ref,
+    values_ref, *, group, prompt_rows
+):
     rows = q_ref.shape[1]
-    keys = k_ref[...].T
-    values = jnp.concatenate([v_ref[...], jnp.ones((ONES, keys.shape[0]), bf16)], axis=0)
     wide = HEAD_WIDTH + ONES
-
-    def finish(first, last, with_other):
+    seen = seen_ref[0] > 0
+    key = k_ref[0].astype(f32)
+    norm_k = jnp.max(jnp.sum(key * key, axis=0, keepdims=True))
+    slow = jnp.max(nq_ref[...]) * norm_k >= SAFE_BOUND * SAFE_BOUND
+    keys_ref[...] = widened(k_ref[0].T)
+    values_ref[:HEAD_WIDTH] = v_ref[0]
+    values_ref[HEAD_WIDTH:] = jnp.ones((ONES, keys_ref.shape[0]), bf16)
+    for head in range(group):
+        query_ref[head, :HEAD_WIDTH] = q_ref[head_rows(head)]
+        query_ref[head, HEAD_WIDTH:] = jnp.zeros((ONES, rows), bf16)
+    far_ref[...] = jnp.zeros_like(far_ref)
+
+    @pl.when(slow)
+    def _():
         for head in range(group):
-            total = acc_ref[head * wide : (head + 1) * wide, first:last]
+            for first, end in ((0, prompt_rows), (prompt_rows, rows)):
+                scores = contract(keys_ref[...], query_ref[head, :, first:end], 1, 0)
+                far_ref[0, head : head + 1, first:end] = jnp.max(scores, axis=0, keepdims=True)
+            query_ref[head, HEAD_WIDTH:] = in_parts(-far_ref[0, head : head + 1])
+
+    def finish(first, end, with_other):
+        for head in range(group):
+            own = acc_ref[head * wide : (head + 1) * wide, first:end]
+            own_top = top_ref[0, head : head + 1, first:end]
             if with_other:
-                query = q_ref[head * HEAD_WIDTH : (head + 1) * HEAD_WIDTH, first:last]
-                total = total + contract(values, weigh(keys, query, False), 1, 0)
-            weight_sum = total[HEAD_WIDTH : HEAD_WIDTH + 1]
-            o_ref[head * HEAD_WIDTH : (head + 1) * HEAD_WIDTH, first:last] = (
-                total[:HEAD_WIDTH] / weight_sum
-            ).astype(bf16)
-            lse_ref[0, head : head + 1, first:last] = jnp.log2(weight_sum)
+                weights = jnp.exp2(contract(keys_ref[...], query_ref[head, :, first:end], 1, 0)).astype(bf16)
+                p_ref[head, :, first:end] = weights
+                far = contract(values_ref[...], weights, 1, 0)
+                far_top = far_ref[0, head : head + 1, first:end]
+                top = jnp.maximum(own_top, far_top)
+                own_scale, far_scale = jnp.exp2(own_top - top), jnp.exp2(far_top - top)
+                total = own * own_scale + far * far_scale
+                inverse = 1.0 / total[HEAD_WIDTH : HEAD_WIDTH + 1]
+                far_ref[0, head : head + 1, first:end] = far_scale * inverse
+                own_ref[0, head : head + 1, first:end] = own_scale * inverse
+            else:
+                total = own
+                inverse = 1.0 / total[HEAD_WIDTH : HEAD_WIDTH + 1]
+                far_ref[0, head : head + 1, first:end] = jnp.zeros_like(inverse)
+                own_ref[0, head : head + 1, first:end] = inverse
+            o_ref[head_rows(head), first:end] = (total[:HEAD_WIDTH] * inverse).astype(bf16)
 
     finish(prompt_rows, rows, True)
 
-    @pl.when(seen_ref[0] > 0)
+    @pl.when(seen)
     def _():
         finish(0, prompt_rows, True)
 
-    @pl.when(seen_ref[0] == 0)
+    @pl.when(jnp.logical_not(seen))
     def _():
         finish(0, prompt_rows, False)
 
 
-def other_forward(seen, q, k, v, acc, kv_heads, prompt_rows):
+def half_index(h, j, seen):
+    return (h, 0, 1 - j * jnp.minimum(seen[0], 1))
+
+
+def other_forward(seen, q, kv, norm_q, acc, top, kv_heads, prompt_rows):
     rows = q.shape[1]
     group = q.shape[0] // HEAD_WIDTH // kv_heads
-    wide = group * (HEAD_WIDTH + ONES)
+    wide = HEAD_WIDTH + ONES
+    keys = kv.shape[2]
     block = lambda n, m: pl.BlockSpec((n, m), lambda h, s: (h, 0))
+    row_block = pl.BlockSpec((1, group, rows), lambda h, s: (h, 0, 0))
+    shape = jax.ShapeDtypeStruct
     return pl.pallas_call(
         functools.partial(other_forward_kernel, group=group, prompt_rows=prompt_rows),
         grid_spec=pltpu.PrefetchScalarGridSpec(
@@ -208,81 +323,72 @@
             grid=(kv_heads,),
             in_specs=[
                 block(group * HEAD_WIDTH, rows),
-                block(HEAD_WIDTH, k.shape[1]),
-                block(HEAD_WIDTH, k.shape[1]),
-                block(wide, rows),
+                pl.BlockSpec((1, HEAD_WIDTH, keys), lambda h, s: (0, h, 0)),
+                pl.BlockSpec((1, HEAD_WIDTH, keys), lambda h, s: (1, h, 0)),
+                resident(norm_q.shape),
+                block(group * wide, rows),
+                row_block,
             ],
             out_specs=(
                 block(group * HEAD_WIDTH, rows),
-                pl.BlockSpec((1, group, rows), lambda h, s: (h, 0, 0)),
+                row_block,
+                row_block,
+                pl.BlockSpec((group, keys, rows), lambda h, s: (h, 0, 0)),
             ),
+            scratch_shapes=[
+                pltpu.VMEM((group, wide, rows), bf16),
+                pltpu.VMEM((keys, wide), bf16),
+                pltpu.VMEM((wide, keys), bf16),
+            ],
         ),
         out_shape=(
-            jax.ShapeDtypeStruct(q.shape, bf16),
-            jax.ShapeDtypeStruct((kv_heads, group, rows), f32),
+            shape(q.shape, bf16),
+            shape((kv_heads, group, rows), f32),
+            shape((kv_heads, group, rows), f32),
+            shape((kv_heads * group, keys, rows), bf16),
         ),
-        compiler_params=pltpu.CompilerParams(vmem_limit_bytes=56 * MIB),
+        compiler_params=pltpu.CompilerParams(vmem_limit_bytes=60 * MIB),
         name="other_forward",
-    )(seen, q, k, v, acc)
-
-
-def in_parts(row):
-    high = row.astype(bf16)
-    rest = row - high.astype(f32)
-    middle = rest.astype(bf16)
-    low = (rest - middle.astype(f32)).astype(bf16)
-    return jnp.concatenate([high, middle, low, jnp.zeros((ONES - 3, row.shape[1]), bf16)], axis=0)
-
-
-def widened(matrix):
-    return jnp.concatenate([matrix, jnp.ones((matrix.shape[0], ONES), bf16)], axis=1)
-
-
-def tile_backward(keys, values, key_rows, query, grad, diagonal):
-    weights = jnp.exp2(contract(keys, query, 1, 0))
+    )(seen, q, kv, kv, norm_q, acc, top)
+
+
+def tile_backward(values, key_rows, weights, query, grad):
     slopes = contract(values, grad, 1, 0)
-    if diagonal:
-        step = keys.shape[0]
-        front = jnp.where(causal(step, step), weights[:, :step], 0.0)
-        weights = front if weights.shape[1] == step else jnp.concatenate([front, weights[:, step:]], axis=1)
-    slopes = (weights * slopes).astype(bf16)
-    weights = weights.astype(bf16)
+    slopes = (weights.astype(f32) * slopes).astype(bf16)
     query_grad = contract(key_rows, slopes, 1, 0)
-    key_grad = contract(query[:HEAD_WIDTH], slopes, 1, 1)
+    key_grad = contract(query, slopes, 1, 1)
     value_grad = contract(grad[:HEAD_WIDTH], weights, 1, 1)
     return query_grad, key_grad, value_grad
 
 
-def fill_sides(q_ref, g_ref, lse_ref, delta_ref, query_ref, grad_ref, group):
+def fill_grads(g_ref, scale_ref, delta_ref, grad_ref, group):
     for head in range(group):
-        rows = pl.ds(head * HEAD_WIDTH, HEAD_WIDTH)
-        query_ref[head, :HEAD_WIDTH] = q_ref[rows]
-        grad_ref[head, :HEAD_WIDTH] = g_ref[rows]
-        query_ref[head, HEAD_WIDTH:] = in_parts(-lse_ref[0, head : head + 1])
-        grad_ref[head, HEAD_WIDTH:] = in_parts(-delta_ref[0, head : head + 1])
+        scale = scale_ref[0, head : head + 1]
+        grad_ref[head, :HEAD_WIDTH] = (g_ref[head_rows(head)].astype(f32) * scale).astype(bf16)
+        grad_ref[head, HEAD_WIDTH:] = in_parts(-delta_ref[0, head : head + 1] * scale)
 
 
 def other_backward_kernel(
-    seen_ref, q_ref, g_ref, lse_ref, delta_ref, k_ref, v_ref, dq_ref, dk_ref, dv_ref,
-    query_ref, grad_ref, keys_ref, values_ref, dk_sum, dv_sum, *, group, prompt_rows, step
+    seen_ref, q_ref, g_ref, scale_ref, delta_ref, k_ref, v_ref, p_ref, dq_ref, dkv_ref,
+    grad_ref, values_ref, dk_sum, dv_sum, dq_sum, *, group, prompt_rows, step
 ):
     rows = q_ref.shape[1]
-    fill_sides(q_ref, g_ref, lse_ref, delta_ref, query_ref, grad_ref, group)
-    keys_ref[...] = widened(k_ref[...].T)
-    values_ref[...] = widened(v_ref[...].T)
-    dq_ref[...] = jnp.zeros_like(dq_ref)
+    seen = seen_ref[0] > 0
+    stage = pl.program_id(1)
 
     def part(first, last, fresh):
-        for low in range(0, k_ref.shape[1], step):
+        for low in range(0, k_ref.shape[2], step):
             span = slice(low, low + step)
             key_sum = value_sum = None
             for head in range(group):
                 query_grad, key_grad, value_grad = tile_backward(
-                    keys_ref[span], values_ref[span], k_ref[:, span],
-                    query_ref[head, :, first:last], grad_ref[head, :, first:last], False,
+                    values_ref[span], k_ref[0, :, span], p_ref[head, span],
+                    q_ref[head_rows(head), first:last], grad_ref[head, :, first:last],
                 )
-                at = pl.ds(head * HEAD_WIDTH, HEAD_WIDTH)
-                dq_ref[at, first:last] += query_grad
+                if low == 0:
+                    dq_sum[head_rows(head), first:last] = query_grad
+                else:
+                    dq_sum[head_rows(head), first:last] += query_grad
                 key_sum = key_grad if key_sum is None else key_sum + key_grad
                 value_sum = value_grad if value_sum is None else value_sum + value_grad
             if fresh:
@@ -292,105 +398,129 @@
                 dk_sum[:, span] += key_sum
                 dv_sum[:, span] += value_sum
 
-    part(prompt_rows, rows, True)
-
-    @pl.when(seen_ref[0] > 0)
+    @pl.when(stage == 0)
+    def _():
+        fill_grads(g_ref, scale_ref, delta_ref, grad_ref, group)
+        values_ref[...] = widened(v_ref[0].T)
+        part(prompt_rows, rows, True)
+
+    @pl.when((stage == 1) & seen)
     def _():
         part(0, prompt_rows, False)
 
-    dk_ref[...] = dk_sum[...].astype(bf16)
-    dv_ref[...] = dv_sum[...].astype(bf16)
-
-
-def backward_specs(group, rows, key_count):
-    block = lambda n, m: pl.BlockSpec((n, m), lambda h, *_: (h, 0))
-    row_block = pl.BlockSpec((1, group, rows), lambda h, *_: (h, 0, 0))
-    wide = group * HEAD_WIDTH
-    ins = [block(wide, rows), block(wide, rows), row_block, row_block,
-           block(HEAD_WIDTH, key_count), block(HEAD_WIDTH, key_count)]
-    outs = (block(wide, rows), block(HEAD_WIDTH, key_count), block(HEAD_WIDTH, key_count))
-    scratch = [
-        pltpu.VMEM((group, HEAD_WIDTH + ONES, rows), bf16),
-        pltpu.VMEM((group, HEAD_WIDTH + ONES, rows), bf16),
-        pltpu.VMEM((key_count, HEAD_WIDTH + ONES), bf16),
-        pltpu.VMEM((key_count, HEAD_WIDTH + ONES), bf16),
-    ]
-    return ins, outs, scratch
-
-
-def other_backward(seen, q, g, lse, delta, k, v, kv_heads, prompt_rows, step=256):
+    @pl.when((stage == 1) & jnp.logical_not(seen))
+    def _():
+        dq_sum[:, :prompt_rows] = jnp.zeros((dq_ref.shape[0], prompt_rows), f32)
+
+    @pl.when(stage == 1)
+    def _():
+        dq_ref[...] = dq_sum[...].astype(bf16)
+        dkv_ref[0] = dk_sum[...].astype(bf16)
+        dkv_ref[1] = dv_sum[...].astype(bf16)
+
+
+def other_backward(seen, q, g, scale, delta, kv, p, kv_heads, prompt_rows, step=256):
     rows = q.shape[1]
     group = q.shape[0] // HEAD_WIDTH // kv_heads
-    ins, outs, scratch = backward_specs(group, rows, k.shape[1])
-    scratch += [pltpu.VMEM((HEAD_WIDTH, k.shape[1]), f32)] * 2
+    keys = kv.shape[2]
+    block = lambda n, m: pl.BlockSpec((n, m), lambda h, j, s: (h, 0))
+    row_block = pl.BlockSpec((1, group, rows), lambda h, j, s: (h, 0, 0))
+    wide = group * HEAD_WIDTH
+    shape = jax.ShapeDtypeStruct
     return pl.pallas_call(
         functools.partial(other_backward_kernel, group=group, prompt_rows=prompt_rows, step=step),
         grid_spec=pltpu.PrefetchScalarGridSpec(
-            num_scalar_prefetch=1, grid=(kv_heads,), in_specs=ins, out_specs=outs, scratch_shapes=scratch
+            num_scalar_prefetch=1,
+            grid=(kv_heads, 2),
+            in_specs=[
+                block(wide, rows), block(wide, rows), row_block, row_block,
+                pl.BlockSpec((1, HEAD_WIDTH, keys), lambda h, j, s: (0, h, 0)),
+                pl.BlockSpec((1, HEAD_WIDTH, keys), lambda h, j, s: (1, h, 0)),
+                pl.BlockSpec((group, keys, prompt_rows), half_index),
+            ],
+            out_specs=(block(wide, rows), pl.BlockSpec((2, HEAD_WIDTH, keys), lambda h, j, s: (0, h, 0))),
+            scratch_shapes=[
+                pltpu.VMEM((group, HEAD_WIDTH + ONES, rows), bf16),
+                pltpu.VMEM((keys, HEAD_WIDTH + ONES), bf16),
+                pltpu.VMEM((HEAD_WIDTH, keys), f32),
+                pltpu.VMEM((HEAD_WIDTH, keys), f32),
+                pltpu.VMEM((wide, rows), f32),
+            ],
         ),
-        out_shape=(
-            jax.ShapeDtypeStruct(q.shape, f32),
-            jax.ShapeDtypeStruct(k.shape, bf16),
-            jax.ShapeDtypeStruct(v.shape, bf16),
-        ),
-        compiler_params=pltpu.CompilerParams(vmem_limit_bytes=56 * MIB),
+        out_shape=(shape(q.shape, bf16), shape(kv.shape, bf16)),
+        compiler_params=pltpu.CompilerParams(vmem_limit_bytes=60 * MIB),
         name="other_backward",
-    )(seen, q, g, lse, delta, k, v)
+    )(seen, q, g, scale, delta, kv, kv, p)
 
 
 def own_backward_kernel(
-    q_ref, g_ref, lse_ref, delta_ref, k_ref, v_ref, dq_in_ref, dq_ref, dk_ref, dv_ref,
-    query_ref, grad_ref, keys_ref, values_ref, *, group, prompt_rows, step
+    q_ref, g_ref, scale_ref, delta_ref, k_ref, v_ref, p_ref, dq_in_ref, dq_ref, dk_ref, dv_ref,
+    grad_ref, values_ref, dk_sum, dv_sum, dq_sum, *, group, prompt_rows, step
 ):
     rows = q_ref.shape[1]
-    fill_sides(q_ref, g_ref, lse_ref, delta_ref, query_ref, grad_ref, group)
-    keys_ref[...] = widened(k_ref[...].T)
-    values_ref[...] = widened(v_ref[...].T)
-    dq_ref[...] = dq_in_ref[...]
-    dk_ref[...] = jnp.zeros_like(dk_ref)
-    dv_ref[...] = jnp.zeros_like(dv_ref)
-
-    def one(low, high, first, last, diagonal):
-        span = slice(low, high)
+    stage = pl.program_id(1)
+    tiles, _ = strips(prompt_rows, rows, step)
+
+    def one(key, first, end, place, columns):
+        span = slice(key, key + step)
         key_sum = value_sum = None
         for head in range(group):
             query_grad, key_grad, value_grad = tile_backward(
-                keys_ref[span], values_ref[span], k_ref[:, span],
-                query_ref[head, :, first:last], grad_ref[head, :, first:last], diagonal,
+                values_ref[span], k_ref[:, span], p_ref[head, place, columns],
+                q_ref[head_rows(head), first:end], grad_ref[head, :, first:end],
             )
-            at = pl.ds(head * HEAD_WIDTH, HEAD_WIDTH)
-            dq_ref[at, first:last] += query_grad
+            dq_sum[head_rows(head), first:end] += query_grad
             key_sum = key_grad if key_sum is None else key_sum + key_grad
             value_sum = value_grad if value_sum is None else value_sum + value_grad
-        dk_ref[:, span] += key_sum
-        dv_ref[:, span] += value_sum
-
-    for low, high, first, last, diagonal in spans(prompt_rows, rows, step):
-        if diagonal:
-            one(low, high, first, last, True)
-        else:
-            for at in range(low, high, step):
-                one(at, at + step, first, last, False)
-
-
-def own_backward(q, g, lse, delta, k, v, dq, kv_heads, prompt_rows, step=256):
+        dk_sum[:, span] += key_sum
+        dv_sum[:, span] += value_sum
+
+    @pl.when(stage == 0)
+    def _():
+        fill_grads(g_ref, scale_ref, delta_ref, grad_ref, group)
+        values_ref[...] = widened(v_ref[...].T)
+        dq_sum[...] = dq_in_ref[...].astype(f32)
+        dk_sum[...] = jnp.zeros_like(dk_sum)
+        dv_sum[...] = jnp.zeros_like(dv_sum)
+        for key in range(0, prompt_rows, step):
+            one(key, prompt_rows, rows, slice(key, key + step), slice(0, rows - prompt_rows))
+
+    @pl.when(stage == 1)
+    def _():
+        for key, first, end, strip, column in tiles:
+            one(key, first, end, slice(strip * step, (strip + 1) * step), slice(column, column + end - first))
+        dq_ref[...] = dq_sum[...].astype(bf16)
+        dk_ref[...] = dk_sum[...].astype(bf16)
+        dv_ref[...] = dv_sum[...].astype(bf16)
+
+
+def own_backward(q, g, scale, delta, k, v, p, dq, kv_heads, prompt_rows, step=256):
     rows = q.shape[1]
     group = q.shape[0] // HEAD_WIDTH // kv_heads
-    ins, outs, scratch = backward_specs(group, rows, k.shape[1])
+    block = lambda n: pl.BlockSpec((n, rows), lambda h, j: (h, 0))
+    row_block = pl.BlockSpec((1, group, rows), lambda h, j: (h, 0, 0))
+    wide = group * HEAD_WIDTH
+    shape = jax.ShapeDtypeStruct
     return pl.pallas_call(
         functools.partial(own_backward_kernel, group=group, prompt_rows=prompt_rows, step=step),
-        grid=(kv_heads,),
-        in_specs=ins + [outs[0]],
-        out_specs=outs,
-        scratch_shapes=scratch,
-        out_shape=(
-            jax.ShapeDtypeStruct(q.shape, f32),
-            jax.ShapeDtypeStruct(k.shape, f32),
-            jax.ShapeDtypeStruct(v.shape, f32),
-        ),
+        grid=(kv_heads, 2),
+        in_specs=[
+            block(wide), block(wide), row_block, row_block, block(HEAD_WIDTH), block(HEAD_WIDTH),
+            pl.BlockSpec((group, prompt_rows, rows - prompt_rows), lambda h, j: (h, j, 0)),
+            block(wide),
+        ],
+        out_specs=(block(wide), block(HEAD_WIDTH), block(HEAD_WIDTH)),
+        scratch_shapes=[
+            pltpu.VMEM((group, HEAD_WIDTH + ONES, rows), bf16),
+            pltpu.VMEM((rows, HEAD_WIDTH + ONES), bf16),
+            pltpu.VMEM((HEAD_WIDTH, rows), f32),
+            pltpu.VMEM((HEAD_WIDTH, rows), f32),
+            pltpu.VMEM((wide, rows), f32),
+        ],
+        out_shape=(shape(q.shape, bf16), shape(k.shape, bf16), shape(v.shape, bf16)),
         compiler_params=pltpu.CompilerParams(vmem_limit_bytes=60 * MIB),
         name="own_backward",
-    )(q, g, lse, delta, k, v, dq)
+    )(q, g, scale, delta, k, v, p, dq)
 
 
 def middle_kernel(
@@ -514,7 +644,7 @@
         in_specs=[resident(dy.shape), pl.BlockSpec((rows, tile), lambda i: (0, i))],
         out_specs=pl.BlockSpec((tile, width), lambda i: (i, 0)),
         out_shape=jax.ShapeDtypeStruct((total, width), bf16),
-        compiler_params=pltpu.CompilerParams(vmem_limit_bytes=56 * MIB),
+        compiler_params=pltpu.CompilerParams(vmem_limit_bytes=60 * MIB),
         name="down_grads",
     )(dy, hidden)
 
@@ -549,13 +679,13 @@
         ],
         out_specs=pl.BlockSpec((width, tile), lambda i: (0, i)),
         out_shape=jax.ShapeDtypeStruct((width, 2 * total + width), bf16),
-        compiler_params=pltpu.CompilerParams(vmem_limit_bytes=56 * MIB),
+        compiler_params=pltpu.CompilerParams(vmem_limit_bytes=60 * MIB),
         name="wide_grads",
     )(o, h2, dgate, dup, dattn)
 
 
 def finish_kernel(
-    x_ref, h_ref, dattn_ref, gain_ref, w_ref, dq_ref, dk_ref, dv_ref, dk_in_ref, dv_in_ref, cos_ref, sin_ref,
+    x_ref, dattn_ref, gain_ref, w_ref, dq_ref, dk_ref, dv_ref, dkv_in_ref, cos_ref, sin_ref,
     dgain_f_ref, out_ref, dw_ref, acc_ref, dgain_ref, *, prompt_steps
 ):
     step = pl.program_id(0)
@@ -568,8 +698,8 @@
     half = HEAD_WIDTH // 2
     cos, sin = cos_ref[...], sin_ref[...]
 
-    def with_received(ref, in_ref):
-        return ref[...] + jnp.where(step < prompt_steps, in_ref[...].astype(f32), 0.0)
+    def with_received(ref, which):
+        return ref[...].astype(f32) + jnp.where(step < prompt_steps, dkv_in_ref[which].astype(f32), 0.0)
 
     def turned(value, scale):
         c, s = cos * scale, sin * scale
@@ -581,17 +711,18 @@
 
     lin = jnp.concatenate(
         [
-            turned(dq_ref, HEAD_WIDTH**-0.5),
-            turned(with_received(dk_ref, dk_in_ref), LN2),
-            with_received(dv_ref, dv_in_ref),
+            turned(dq_ref[...].astype(f32), HEAD_WIDTH**-0.5),
+            turned(with_received(dk_ref, 0), LN2),
+            with_received(dv_ref, 1),
         ],
         axis=0,
     ).astype(bf16).T
     inner = lin.shape[1]
-    acc_ref[...] += contract(h_ref[...], lin, 0, 0)
-    dh = contract(lin, w_ref[:, :inner], 1, 1)
     x = x_ref[...].astype(f32)
     inverse = lax.rsqrt(jnp.mean(x * x, axis=-1, keepdims=True) + norm_eps)
+    h = (x * inverse * gain_ref[...]).astype(bf16)
+    acc_ref[...] += contract(h, lin, 0, 0)
+    dh = contract(lin, w_ref[:, :inner], 1, 1)
     dgain_ref[0:1] += jnp.sum(dh * x * inverse, axis=0, keepdims=True)
     u = dh * gain_ref[...]
     out_ref[...] = (
@@ -607,27 +738,58 @@
         dw_ref[:, inner:] = dgain_ref[...].T.astype(bf16)
 
 
-def finish(x, h, dattn, gain, w, dq, dk, dv, dk_in, dv_in, cos, sin, dgain_f, tile=256):
+def finish(x, dattn, gain, w, dq, dk, dv, dkv_in, cos, sin, dgain_f, tile=256):
     rows, width = x.shape
     by_row = pl.BlockSpec((tile, width), lambda i: (i, 0))
     cols = lambda n: pl.BlockSpec((n, tile), lambda i: (0, i))
-    steps = dk_in.shape[1] // tile
-    few = lambda n: pl.BlockSpec((n, tile), lambda i: (0, jnp.minimum(i, steps - 1)))
+    steps = dkv_in.shape[2] // tile
+    few = pl.BlockSpec((2, dk.shape[0], tile), lambda i: (0, 0, jnp.minimum(i, steps - 1)))
     shape = jax.ShapeDtypeStruct
     inner = dq.shape[0] + dk.shape[0] + dv.shape[0]
     return pl.pallas_call(
         functools.partial(finish_kernel, prompt_steps=steps),
         grid=(rows // tile,),
-        in_specs=[by_row, by_row, by_row, resident(gain.shape), resident(w.shape),
+        in_specs=[by_row, by_row, resident(gain.shape), resident(w.shape),
                   cols(dq.shape[0]), cols(dk.shape[0]), cols(dv.shape[0]),
-                  few(dk.shape[0]), few(dv.shape[0]),
+                  few,
                   cols(cos.shape[0]), cols(cos.shape[0]), resident(dgain_f.shape)],
         out_specs=(by_row, pl.BlockSpec(w.shape, lambda i: (0, 0))),
         out_shape=(shape((rows, width), f32), shape(w.shape, bf16)),
         scratch_shapes=[pltpu.VMEM((width, inner), f32), pltpu.VMEM((w.shape[1] - inner, width), f32)],
-        compiler_params=pltpu.CompilerParams(vmem_limit_bytes=56 * MIB),
+        compiler_params=pltpu.CompilerParams(vmem_limit_bytes=60 * MIB),
         name="finish",
-    )(x, h, dattn, gain, w, dq, dk, dv, dk_in, dv_in, cos, sin, dgain_f)
+    )(x, dattn, gain, w, dq, dk, dv, dkv_in, cos, sin, dgain_f)
+
+
+def settle_kernel(first_ref, wide_ref, wide_in_ref, down_ref, down_in_ref, *outs, widths):
+    refs = list(outs)
+    at = 0
+    for width in widths[0]:
+        refs.pop(0)[...] = first_ref[:, at : at + width]
+        at += width
+    gains = first_ref[:, at:].T
+    refs.pop(0)[...] = gains[0:1]
+    refs.pop(0)[...] = gains[1:2]
+    at = 0
+    for width in widths[1]:
+        span = slice(at, at + width)
+        refs.pop(0)[...] = wide_ref[:, span].astype(f32) + wide_in_ref[:, span].astype(f32)
+        at += width
+    refs.pop(0)[...] = down_ref[...].astype(f32) + down_in_ref[...].astype(f32)
+
+
+def settle(first, wide, wide_in, down, down_in, first_widths, wide_widths):
+    rows = first.shape[0]
+    shape = jax.ShapeDtypeStruct
+    return pl.pallas_call(
+        functools.partial(settle_kernel, widths=(first_widths, wide_widths)),
+        out_shape=[shape((rows, n), f32) for n in first_widths]
+        + [shape((1, rows), f32)] * 2
+        + [shape((rows, n), f32) for n in wide_widths]
+        + [shape(down.shape, f32)],
+        compiler_params=pltpu.CompilerParams(vmem_limit_bytes=60 * MIB),
+        name="settle",
+    )(first, wide, wide_in, down, down_in)
 
 
 MESH_ID = pl.DeviceIdType.MESH
@@ -681,9 +843,9 @@
     z, y, x, core = whereabouts()
     along, over_x, over_y, over_core = neighbours(depth)
     columns = out_ref.shape[2]
-    mine = pl.ds(pl.multiple_of(y * split, 128), columns - split)
     given = pl.ds(pl.multiple_of(y * (columns - split), 128), split)
     got = pl.ds(pl.multiple_of((1 - y) * (columns - split), 128), split)
+    common = pl.ds(split, columns - 2 * split)
     me = slot_at(z, x, core)
     copies = Copies(send_sems, recv_sems)
     view = lambda slot, span: out_ref.at[slot, :, span]
@@ -698,25 +860,32 @@
         copy.start()
         return copy
 
-    from_z = [send(me, mine, device) for device in along]
-    from_x = {0: send(me, mine, over_x)}
-    from_y = {(0, 0): send(me, given, over_y)}
-    from_core = [send(me, mine, over_core)]
-    for d in range(1, depth):
-        from_z[d - 1].wait_recv()
-        slot = slot_at((z + depth - d) % depth, x, core)
-        from_x[d] = send(slot, mine, over_x)
-        from_y[d, 0] = send(slot, given, over_y)
-        from_core.append(send(slot, mine, over_core))
-    for d in range(depth):
-        from_x[d].wait_recv()
-        slot = slot_at((z + depth - d) % depth, 1 - x, core)
-        from_y[d, 1] = send(slot, given, over_y)
-        from_core.append(send(slot, mine, over_core))
-    for other in range(2):
+    spans = (given, common)
+    from_z, from_x, from_y, from_core = {}, {}, {}, []
+
+    def onward(slot, part, d, side):
+        if side == 0:
+            from_x[d, part] = send(slot, spans[part], over_x)
+        if part == 0:
+            from_y[d, side] = send(slot, given, over_y)
+        from_core.append(send(slot, spans[part], over_core))
+
+    for part in range(2):
+        for d in range(1, depth):
+            from_z[d, part] = send(me, spans[part], along[d - 1])
+        onward(me, part, 0, 0)
+    for part in range(2):
+        for d in range(1, depth):
+            from_z[d, part].wait_recv()
+            onward(slot_at((z + depth - d) % depth, x, core), part, d, 0)
+    for part in range(2):
         for d in range(depth):
-            from_y[d, other].wait_recv()
-            slot = slot_at((z + depth - d) % depth, x if other == 0 else 1 - x, core)
+            from_x[d, part].wait_recv()
+            onward(slot_at((z + depth - d) % depth, 1 - x, core), part, d, 1)
+    for side in range(2):
+        for d in range(depth):
+            from_y[d, side].wait_recv()
+            slot = slot_at((z + depth - d) % depth, x if side == 0 else 1 - x, core)
             from_core.append(send(slot, got, over_core))
     for copy in from_core:
         copy.wait_recv()
@@ -726,7 +895,7 @@
 
 def gather_all(shard, depth, split):
     rows, columns = shard.shape
-    count = 8 * depth - 1
+    count = 2 * (depth - 1) + 2 * depth + 2 * depth + 6 * depth
     return pl.pallas_call(
         functools.partial(gather_kernel, depth=depth, split=split),
         in_specs=[pl.BlockSpec(memory_space=pltpu.VMEM)],
@@ -738,19 +907,17 @@
             pltpu.SemaphoreType.DMA,
         ],
         compiler_params=pltpu.CompilerParams(
-            collective_id=1, has_side_effects=True, vmem_limit_bytes=32 * MIB
+            collective_id=1, has_side_effects=True, vmem_limit_bytes=60 * MIB
         ),
         name="gather_all",
     )(shard)
 
 
 def reduce_kernel(
-    part_ref, out_ref, core_ref, y_ref, sum_ref, x_ref, line_ref, z_ref, last_ref, twin_ref, send_sems, recv_sems,
-    *, depth, split
+    part_ref, out_ref, core_ref, sum_ref, x_ref, line_ref, z_ref, last_ref, twin_ref, send_sems, recv_sems, *, depth
 ):
     z, y, x, core = whereabouts()
     along, over_x, over_y, over_core = neighbours(depth)
-    columns = part_ref.shape[2]
     copies = Copies(send_sems, recv_sems)
     greet(along + [over_x, over_y, over_core])
 
@@ -759,81 +926,60 @@
         copy.start()
         return copy
 
-    order = [(d, side) for side in (1, 0) for d in list(range(1, depth)) + [0]]
+    distances = list(range(1, depth)) + [0]
+    order = [(d, side) for side in (1, 0) for d in distances]
     place = lambda d, side: ((z + d) % depth, x if side == 0 else 1 - x)
     from_core = []
     for at, (d, side) in enumerate(order):
         to_z, to_x = place(d, side)
         from_core.append(send(part_ref.at[slot_at(to_z, to_x, 1 - core)], core_ref.at[at], over_core))
-    low, high = split, columns - split
-
-    def halves(at, to_z, to_x):
-        total = part_ref[slot_at(to_z, to_x, core)].astype(f32) + core_ref[at].astype(f32)
-        left, middle_, right = total[:, :low], total[:, low:high], total[:, high:]
-        is_low = y == 0
-        sum_ref[at, :, :low] = jnp.where(is_low, left, right).astype(bf16)
-        sum_ref[at, :, low:high] = middle_.astype(bf16)
-        sum_ref[at, :, high:] = jnp.where(is_low, right, left).astype(bf16)
-
-    from_y = []
+    from_x = []
     for at, (d, side) in enumerate(order):
         from_core[at].wait_recv()
-        halves(at, *place(d, side))
-        from_y.append(send(sum_ref.at[at, :, pl.ds(high, split)], y_ref.at[at], over_y))
-    from_x = []
-    for at, (d, side) in enumerate(order):
-        from_y[at].wait_recv()
-        sum_ref[at, :, :low] = (sum_ref[at, :, :low].astype(f32) + y_ref[at].astype(f32)).astype(bf16)
+        to_z, to_x = place(d, side)
+        sum_ref[at] = (part_ref[slot_at(to_z, to_x, core)].astype(f32) + core_ref[at].astype(f32)).astype(bf16)
         if side == 1:
-            from_x.append(send(sum_ref.at[at, :, pl.ds(0, high)], x_ref.at[at], over_x))
+            from_x.append(send(sum_ref.at[at], x_ref.at[at], over_x))
     from_z = []
-    for index, d in enumerate(list(range(1, depth)) + [0]):
-        at = depth + index
-        from_x[index].wait_recv()
-        total = (sum_ref[at, :, :high].astype(f32) + x_ref[index].astype(f32)).astype(bf16)
-        line_ref[index] = total
+    for at, d in enumerate(distances):
+        from_x[at].wait_recv()
+        line_ref[at] = (sum_ref[depth + at].astype(f32) + x_ref[at].astype(f32)).astype(bf16)
         if d:
-            from_z.append(send(line_ref.at[index], z_ref.at[index], along[d - 1]))
+            from_z.append(send(line_ref.at[at], z_ref.at[at], along[d - 1]))
     total = line_ref[depth - 1].astype(f32)
-    for index in range(depth - 1):
-        from_z[index].wait_recv()
-        total = total + z_ref[index].astype(f32)
+    for at in range(depth - 1):
+        from_z[at].wait_recv()
+        total = total + z_ref[at].astype(f32)
     last_ref[...] = total.astype(bf16)
     twin = send(last_ref, twin_ref, over_y)
     twin.wait_recv()
-    theirs = twin_ref[...].astype(f32)
-    is_low = y == 0
-    out_ref[:, :low] = jnp.where(is_low, total[:, :low], theirs[:, :low])
-    out_ref[:, low:high] = total[:, low:] + theirs[:, low:]
-    out_ref[:, high:] = jnp.where(is_low, theirs[:, :low], total[:, :low])
+    out_ref[...] = total + twin_ref[...].astype(f32)
     for copy in copies.made:
         copy.wait_send()
 
 
-def reduce_all(parts, depth, split):
+def reduce_all(parts, depth):
     slots, rows, columns = parts.shape
-    high = columns - split
-    count = 2 * depth + 2 * depth + depth + depth - 1 + 1
-    buffer = lambda *shape: pltpu.VMEM(shape, bf16)
+    count = 2 * depth + depth + depth - 1 + 1
+    buffer = lambda *count: pltpu.VMEM(count + (rows, columns), bf16)
     return pl.pallas_call(
-        functools.partial(reduce_kernel, depth=depth, split=split),
+        functools.partial(reduce_kernel, depth=depth),
         in_specs=[pl.BlockSpec(memory_space=pltpu.VMEM)],
         out_specs=pl.BlockSpec(memory_space=pltpu.VMEM),
         out_shape=jax.ShapeDtypeStruct((rows, columns), f32),
         scratch_shapes=[
-            buffer(2 * depth, rows, columns),
-            buffer(2 * depth, rows, split),
-            buffer(2 * depth, rows, columns),
-            buffer(depth, rows, high),
-            buffer(depth, rows, high),
-            buffer(depth - 1, rows, high),
-            buffer(rows, high),
-            buffer(rows, high),
+            buffer(2 * depth),
+            buffer(2 * depth),
+            buffer(depth),
+            buffer(depth),
+            buffer(depth - 1),
+            buffer(),
+            buffer(),
             pltpu.SemaphoreType.DMA((count,)),
             pltpu.SemaphoreType.DMA((count,)),
         ],
         compiler_params=pltpu.CompilerParams(
-            collective_id=2, has_side_effects=True, vmem_limit_bytes=40 * MIB
+            collective_id=2, has_side_effects=True, vmem_limit_bytes=60 * MIB
         ),
         name="reduce_all",
     )(parts)
@@ -1402,36 +1548,8 @@
     )
 
 
-SAFE_BOUND = 90.0
 OWNERS = ("group", "wshard")
 SWAP = [(0, 1), (1, 0)]
-
-
-def exact_attention(seen, q, k, v, k_other, v_other, kv_heads, prompt_rows):
-    rows = q.shape[1]
-    heads = q.shape[0] // HEAD_WIDTH
-    keys = jnp.concatenate([k_other, k], axis=1).reshape(kv_heads, HEAD_WIDTH, -1)
-    values = jnp.concatenate([v_other, v], axis=1).reshape(kv_heads, HEAD_WIDTH, -1)
-    at = jnp.arange(rows)
-    in_prompt = at < prompt_rows
-    piece = jnp.where(in_prompt, -1, (at - prompt_rows) // CONTINUE_LENGTH)
-    own = (at[None, :] <= at[:, None]) & (in_prompt[None, :] | (piece[None, :] == piece[:, None]))
-    other = jnp.broadcast_to(jnp.where(in_prompt, seen > 0, True)[:, None], (rows, k_other.shape[1]))
-    allowed = jnp.concatenate([other, own], axis=1)
-
-    def one_head(head):
-        query = lax.dynamic_index_in_dim(q.reshape(heads, HEAD_WIDTH, rows), head, 0, False)
-        key = lax.dynamic_index_in_dim(keys, head // (heads // kv_heads), 0, False)
-        value = lax.dynamic_index_in_dim(values, head // (heads // kv_heads), 0, False)
-        scores = jnp.where(allowed, contract(query, key, 0, 0), masked_score)
-        top = jnp.max(scores, axis=1, keepdims=True)
-        weights = jnp.exp2(scores - top)
-        total = jnp.sum(weights, axis=1, keepdims=True)
-        out = contract(value, (weights / total).astype(bf16), 1, 1)
-        return out.astype(bf16), (top + jnp.log2(total))[:, 0]
-
-    out, lse = lax.map(one_head, jnp.arange(heads))
-    return out.reshape(q.shape), lse.reshape(kv_heads, heads // kv_heads, rows)
 
 
 def swap(array):
@@ -1476,50 +1594,41 @@
     angles = frequency[:, None] * positions.astype(f32)[None, :]
     cos, sin = jnp.cos(angles), jnp.sin(angles)
 
-    q, k, v, h1, norm_q, norm_k = project(x, gain_a, first, cos, sin, q_rows, kv_rows)
-    k_other, v_other = swap(k[:, :prompt_rows]), swap(v[:, :prompt_rows])
-    acc = own_forward(q, k, v, kv_heads, prompt_rows)
-    other_norm = jnp.max(jnp.sum(jnp.square(k_other.astype(f32)).reshape(kv_heads, HEAD_WIDTH, -1), axis=1))
-    bound = jnp.max(norm_q) * jnp.maximum(jnp.max(norm_k), other_norm)
-    o, lse = lax.cond(
-        bound < SAFE_BOUND * SAFE_BOUND,
-        lambda: other_forward(seen[None], q, k_other, v_other, acc, kv_heads, prompt_rows),
-        lambda: exact_attention(seen, q, k, v, k_other, v_other, kv_heads, prompt_rows),
-    )
-    layer_out, h2, hid, dgate, dup, dattn, dob, delta, dgain_f = middle(
-        x, dy, o, gain_f, wide, wd, kv_heads
-    )
+    q, k, v, kv, norm_q, norm_k = project(x, gain_a, first, cos, sin, q_rows, kv_rows, prompt_rows)
+    kv_other = swap(kv)
+    acc, top, p_own = own_forward(q, k, v, norm_q, norm_k, kv_heads, prompt_rows)
+    o, own_scale, far_scale, p_far = other_forward(seen[None], q, kv_other, norm_q, acc, top, kv_heads, prompt_rows)
+    layer_out, h2, hid, dgate, dup, dattn, dob, delta, dgain_f = middle(x, dy, o, gain_f, wide, wd, kv_heads)
     scatter = lambda a: lax.psum_scatter(a, OWNERS, scatter_dimension=0, tiled=True)
     d_down = down_grads(dy, hid)
+    h2, d_down = lax.optimization_barrier((h2, d_down))
+    d_down = scatter(d_down)
     d_wide = wide_grads(o, h2, dattn, dgate, dup)
-    dob, d_down, d_wide = lax.optimization_barrier((dob, d_down, d_wide))
-    d_down, d_wide = scatter(d_down), scatter(d_wide)
-    dq_part, dk_other, dv_other = other_backward(
-        seen[None], q, dob, lse, delta, k_other, v_other, kv_heads, prompt_rows
-    )
-    dk_in, dv_in = swap(dk_other), swap(dv_other)
-    dq, dk, dv = own_backward(q, dob, lse, delta, k, v, dq_part, kv_heads, prompt_rows)
-
-    def over_ctx(part):
-        return part.astype(f32) + swap(part).astype(f32)
-
-    d_down, d_wide, dq = lax.optimization_barrier((d_down, d_wide, dq))
-    d_down, d_wide = over_ctx(d_down), over_ctx(d_wide)
-    grad_tokens, d_first = finish(
-        x, h1, dattn, gain_a, first, dq, dk, dv, dk_in, dv_in, cos, sin, dgain_f
-    )
-    d_first = reduce_all(d_first.reshape(4 * depth, shard_rows, -1), depth, split)
+    dob, d_wide = lax.optimization_barrier((dob, d_wide))
+    d_wide = scatter(d_wide)
+    dq, dkv_far = other_backward(seen[None], q, dob, far_scale, delta, kv_other, p_far, kv_heads, prompt_rows)
+    dkv_in = swap(dkv_far)
+    d_down, dkv_in = lax.optimization_barrier((d_down, dkv_in))
+    d_down_in = swap(d_down)
+    dq, dk, dv = own_backward(q, dob, own_scale, delta, k, v, p_own, dq, kv_heads, prompt_rows)
+    grad_tokens, d_first = finish(x, dattn, gain_a, first, dq, dk, dv, dkv_in, cos, sin, dgain_f)
+    d_first, d_wide = lax.optimization_barrier((d_first, d_wide))
+    d_wide_in = swap(d_wide)
+    d_first = reduce_all(d_first.reshape(4 * depth, shard_rows, -1), depth)
+    d_q, d_k, d_v, d_gain_a, d_gain_f, d_gate, d_up, d_out, d_down = settle(
+        d_first, d_wide, d_wide_in, d_down, d_down_in, (q_rows, kv_rows, kv_rows), (hidden, hidden, q_rows)
+    )
     return (
         layer_out[None],
         grad_tokens[None],
-        d_first[:, end],
-        d_first[:, :q_rows],
-        d_first[:, q_rows : q_rows + kv_rows],
-        d_first[:, q_rows + kv_rows : end],
-        d_wide[:, 2 * hidden :],
-        d_first[:, end + 1],
-        d_wide[:, :hidden],
-        d_wide[:, hidden : 2 * hidden],
+        d_gain_a[0],
+        d_q,
+        d_k,
+        d_v,
+        d_out,
+        d_gain_f[0],
+        d_gate,
+        d_up,
         d_down,
     )
 

time: 767 us -> 695 us (0.906)
  Pallas kernels: 667 us -> 622 us
  waiting for transfers between devices: 33.6 us -> 5.49 us
  starting transfers between devices: 6.27 us -> 32.5 us
  local copies, waits for them, and re-layouts: 16.1 us -> 6 us
    pallas_call x1, Pallas kernels: 114 us -> 71.3 us  [other_backward(): pl.pallas_call(functools.partial(other_backward_kernel, group=group, prom...]
    optimization_barrier x1, waiting for transfers between devices: 32.3 us -> 0.02 us  [fast_local(): d_first, d_wide = lax.optimization_barrier((d_first, d_wide))]
    ppermute x6 -> x4, starting transfers between devices: 6.11 us -> 32.4 us  [swap(): return lax.ppermute(array, 'ctx', SWAP)]
    pallas_call x1, Pallas kernels: 122 us -> 103 us  [own_backward(): pl.pallas_call(functools.partial(own_backward_kernel, group=group, prompt...]
    pallas_call x2 -> x3, Pallas kernels: 66.4 us -> 75.8 us  [the longest x1 52 us: reduce_all(): pl.pallas_call(functools.partial(reduce_kernel, depth=depth), in_specs=[p...]
  transfers between devices with their start and end apart: 10 -> 8, of which waited for: 1 -> 1; matrix products, arithmetic and copies ran while one was open for 3% -> 1% of each run, Pallas kernels for 61% -> 67%
where the time goes in v3:
time: 695 us; the launch traced here: 690 us
  Pallas kernels  622 us (89%)
  starting transfers between devices  32.5 us (5%)
  between operations  15.7 us (2%)
  other arithmetic  8.07 us (1%)
    pallas_call x1, Pallas kernels, middle(): pl.pallas_call(functools.partial(middle_kernel, chunk=chunk), grid=(rows...  133 us
    pallas_call x1, Pallas kernels, own_backward(): pl.pallas_call(functools.partial(own_backward_kernel, group=group, prompt...  103 us
    pallas_call x1, Pallas kernels, other_backward(): pl.pallas_call(functools.partial(other_backward_kernel, group=group, prom...  71.3 us
    pallas_call x1, Pallas kernels, reduce_all(): pl.pallas_call(functools.partial(reduce_kernel, depth=depth), in_specs=[p...  52 us
    pallas_call x1, Pallas kernels, own_forward(): pl.pallas_call(functools.partial(own_forward_kernel, group=group, prompt_...  51.8 us
    pallas_call x1, Pallas kernels, gather_all(): pl.pallas_call(functools.partial(gather_kernel, depth=depth, split=split)...  48 us
    pallas_call x1, Pallas kernels, wide_grads(): pl.pallas_call(functools.partial(wide_grads_kernel, each=each), grid=(ste...  47.4 us
    pallas_call x1, Pallas kernels, other_forward(): pl.pallas_call(functools.partial(other_forward_kernel, group=group, promp...  35.9 us
  transfers between devices with their start and end apart: 8, of which 1 were waited for; matrix products, arithmetic and copies ran while one was open for 1% of the time, Pallas kernels for 67%

profile of v3, /device:TPU:8, one launch (start us, length us, event | category | flops | bytes accessed | tf_op | source)
XLA Modules:
  0.0 690.1 jit_solution(3022081920007799717)
XLA Ops:
  7.2 0.7 all-gather.5.cloned.1.call-update
  8.0 2.2 pad_maximum_fusion
  10.3 0.7 pad_maximum_fusion.1
  10.9 0.1 copy.28
  11.1 1.7 fusion.1.shard_ref
  12.8 48.0 %gather_all.1 = bf16[16,72,2048]{2,1,0:T(8,128)(2,1)} custom-call(bf16[72,2048]{1,0:T(8,128)(2,1)} %fusion.1.shard_ref), custom_call_target="tpu_custom_call" | custom-call | tf_op jit(solution)/shard_map/gather_all/pallas_call | solution.py:899
  60.8 1.0 convert_bitcast_fusion
  61.8 0.2 fusion.9
  62.0 0.8 copy.29.gain_ref
  62.8 0.6 fusion.10
  64.1 1.8 multiply_sine_fusion
  65.9 20.0 %project.1 = (bf16[1152,2048]{1,0:T(8,128)(2,1)}, bf16[384,2048]{1,0:T(8,128)(2,1)}, bf16[384,2048]{1,0:T(8,128)(2,1)}, bf16[2,384,1024]{2,1,0:T(8,128)(2,1)}, f32[1,2048]{1,0:T(1,128)}, /*index=5*/f32[1,2048]{1,0:T(1,128)}) custom-call(bf16[2048,1152]{1,0:T(8,128)(2,1)} %bitcast.18, f32[1,1152]{1,0:T(1,128)} %copy.29.gain_ref, bf16[1152,2048]{1,0:T(8,128)(2,1)} %bitcast.16, ...), custom_call_target="tpu_custom_call" | custom-call | tf_op jit(solution)/shard_map/project/pallas_call | solution.py:79
  85.9 0.5 collective-permute-start
  87.0 0.8 copy.30.gain_ref
  87.8 51.8 %own_forward.1 = (f32[1440,2048]{1,0:T(8,128)}, f32[6,3,2048]{2,1,0:T(4,128)}, bf16[18,2048,1024]{2,1,0:T(8,128)(2,1)}) custom-call(bf16[1152,2048]{1,0:T(8,128)(2,1)} %get-tuple-element.57.q_ref, bf16[384,2048]{1,0:T(8,128)(2,1)} %get-tuple-element.60.k_ref, bf16[384,2048]{1,0:T(8,128)(2,1)} %get-tuple-element.61.v_ref, ...), custom_call_target="tpu_custom_call" | custom-call | tf_op jit(solution)/shard_map/own_forward/pallas_call | solution.py:222
  139.6 1.2 copy-done
  140.7 35.9 %other_forward.1 = (bf16[1152,2048]{1,0:T(8,128)(2,1)}, f32[6,3,2048]{2,1,0:T(4,128)}, f32[6,3,2048]{2,1,0:T(4,128)}, bf16[18,1024,2048]{2,1,0:T(8,128)(2,1)}) custom-call(s32[1]{0:T(128)} %bitcast.2.seen_ref, bf16[1152,2048]{1,0:T(8,128)(2,1)} %get-tuple-element.57.q_ref, bf16[2,384,1024]{2,1,0:T(8,128)(2,1)} %copy-done, bf16[2,384,1024]{2,1,0:T(8,128)(2,1)} %copy-done, ...), custom_call_target="tpu_custom_call" | custom-call | tf_op jit(solution)/shard_map/other_forward/pallas_call | solution.py:319
  176.7 4.7 all-gather.3.cloned.1.call-done.wide_any
  181.4 133.0 %middle.1 = (bf16[2048,1152]{1,0:T(8,128)(2,1)}, bf16[2048,1152]{1,0:T(8,128)(2,1)}, bf16[2048,3072]{1,0:T(8,128)(2,1)}, bf16[2048,3072]{1,0:T(8,128)(2,1)}, bf1...) custom-call(bf16[2048,1152]{1,0:T(8,128)(2,1)} %bitcast.19, ...), custom_call_target="tpu_custom_call" | custom-call | tf_op jit(solution)/shard_map/middle/pallas_call | solution.py:611
  314.4 21.5 %down_grads.1 = bf16[3072,1152]{1,0:T(8,128)(2,1)} custom-call(bf16[2048,1152]{1,0:T(8,128)(2,1)} %bitcast.22, bf16[2048,3072]{1,0:T(8,128)(2,1)} %get-tuple-element.70.hidden_ref), custom_call_target="tpu_custom_call" | custom-call | tf_op jit(solution)/shard_map/down_grads/pallas_call | solution.py:641
  336.0 47.4 %wide_grads.1 = bf16[1152,7296]{1,0:T(8,128)(2,1)} custom-call(bf16[1152,2048]{1,0:T(8,128)(2,1)} %get-tuple-element.65.o_ref, bf16[2048,1152]{1,0:T(8,128)(2,1)} %get-tuple-element.71.h2_ref, bf16[2048,3072]{1,0:T(8,128)(2,1)} %get-tuple-element.72.dgate_ref, bf16[2048,3072]{1,0:T(8,128)(2,1)} %get-tuple-element.73.dup_ref, ...), custom_call_target="tpu_custom_call" | custom-call | tf_op jit(solution)/shard_map/wide_grads/pallas_call | solution.py:674
  383.4 71.3 %other_backward.1 = (bf16[1152,2048]{1,0:T(8,128)(2,1)}, bf16[2,384,1024]{2,1,0:T(8,128)(2,1)}) custom-call(s32[1]{0:T(128)} %bitcast.2.seen_ref, bf16[1152,2048]{1,0:T(8,128)(2,1)} %get-tuple-element.57.q_ref, bf16[1152,2048]{1,0:T(8,128)(2,1)} %get-tuple-element.74.g_ref, f32[6,3,2048]{2,1,0:T(4,128)} %get-tuple-element.78.scale_ref, ...), custom_call_target="tpu_custom_call" | custom-call | tf_op jit(solution)/shard_map/other_backward/pallas_call | solution.py:430
  454.8 29.8 %collective-permute-start.1 = (bf16[2,384,1024]{2,1,0:T(8,128)(2,1)}, bf16[2,384,1024]{2,1,0:T(8,128)(2,1)S(1)}, u32[]{:S(2)}, u32[]{:S(2)}) collective-permute-start(bf16[2,384,1024]{2,1,0:T(8,128)(2,1)} %get-tuple-element.85), channel_id=1, source_target_pairs={{0,4},{4,0},{1,5},{5,1},{2,6},{6,2},{3,7},{7,3},{8,12},{12,8},{9,1... | collective-permute-start | bytes 4718600 | tf_op jit(solution)/shard_map/ppermute | solution.py:1556
  484.6 102.8 %own_backward.1 = (bf16[1152,2048]{1,0:T(8,128)(2,1)}, bf16[384,2048]{1,0:T(8,128)(2,1)}, bf16[384,2048]{1,0:T(8,128)(2,1)}) custom-call(bf16[1152,2048]{1,0:T(8,128)(2,1)} %get-tuple-element.57.q_ref, bf16[1152,2048]{1,0:T(8,128)(2,1)} %get-tuple-element.74.g_ref, f32[6,3,2048]{2,1,0:T(4,128)} %get-tuple-element.75.scale_ref, ...), custom_call_target="tpu_custom_call" | custom-call | tf_op jit(solution)/shard_map/own_backward/pallas_call | solution.py:504
  587.4 1.1 copy-done.1
  588.6 34.8 %finish.1 = (f32[2048,1152]{1,0:T(8,128)}, bf16[1152,2048]{1,0:T(8,128)(2,1)}) custom-call(bf16[2048,1152]{1,0:T(8,128)(2,1)} %bitcast.20, bf16[2048,1152]{1,0:T(8,128)(2,1)} %get-tuple-element.67.dattn_ref, f32[1,1152]{1,0:T(1,128)} %copy.29.gain_ref, bf16[1152,2048]{1,0:T(8,128)(2,1)} %bitcast.17, bf16[1152,2048]{1,0:T(8,128)(2,1)} %get-tuple-element.81.dq_ref, ...), custom_call_target="tpu_custom_call" | custom-call | tf_op jit(solution)/shard_map/finish/pallas_call | solution.py:749
  623.4 0.1 collective-permute-start.2
  623.5 2.0 collective-permute-start.3
  625.5 52.0 %reduce_all.1.first_ref = f32[72,2048]{1,0:T(8,128)} custom-call(bf16[16,72,2048]{2,1,0:T(8,128)(2,1)} %bitcast.23), custom_call_target="tpu_custom_call" | custom-call | tf_op jit(solution)/shard_map/reduce_all/pallas_call | solution.py:965
  677.5 0.7 copy-done.4
  678.2 1.0 copy-done.2
  679.2 3.8 settle.1
  (24 shorter events, 0.3 us)
Async XLA Ops:
  7.2 169.5 %all-gather.5.cloned.1.call-start = ((), (), s32[]{:S(2)}) async-start(), calls=%async_computation.3 | async-start | bytes 7520256 | tf_op jit(solution)/shard_map/all_gather | solution.py:1580
  7.9 173.5 %all-gather.3.cloned.1.call-start = ((), (), s32[]{:S(2)}) async-start(), calls=%async_computation.2 | async-start | bytes 17860608 | tf_op jit(solution)/shard_map/all_gather | solution.py:1577
  10.2 577.2 %reduce-scatter.5.cloned.1.call-start = ((), (), s32[]{:S(2)}) async-start(), calls=%async_computation.4 | async-start | bytes 7520256 | tf_op jit(solution)/shard_map/reduce_scatter | solution.py:1602
  11.1 51.7 %copy-start.5 = (s32[1,4]{1,0:T(1,128)S(1)}, s32[1,4]{1,0:T(1,128)}, u32[]{:S(2)}) copy-start(s32[1,4]{1,0:T(1,128)} %param.13) | copy-start | bytes 52
  85.9 53.7 %collective-permute-start = (bf16[2,384,1024]{2,1,0:T(8,128)(2,1)}, bf16[2,384,1024]{2,1,0:T(8,128)(2,1)S(1)}, u32[]{:S(2)}, u32[]{:S(2)}) collective-permute-start(bf16[2,384,1024]{2,1,0:T(8,128)(2,1)} %get-tuple-element.58), channel_id=1, source_target_pairs={{0,4},{4,0},{1,5},{5,1},{2,6},{6,2},{3,7},{7,3},{8,12},{12,8},{9,1... | collective-permute-start | bytes 4718600 | tf_op jit(solution)/shard_map/ppermute | solution.py:1556
  139.6 1.2 copy-start
  335.9 287.4 %reduce-scatter.7.cloned.1.call-start = ((), (), s32[]{:S(2)}) async-start(), calls=%async_computation.5 | async-start | bytes 17860608
  454.8 132.7 %collective-permute-start.1 = (bf16[2,384,1024]{2,1,0:T(8,128)(2,1)}, bf16[2,384,1024]{2,1,0:T(8,128)(2,1)S(1)}, u32[]{:S(2)}, u32[]{:S(2)}) collective-permute-start(bf16[2,384,1024]{2,1,0:T(8,128)(2,1)} %get-tuple-element.85), channel_id=1, source_target_pairs={{0,4},{4,0},{1,5},{5,1},{2,6},{6,2},{3,7},{7,3},{8,12},{12,8},{9,1... | collective-permute-start | bytes 4718600 | tf_op jit(solution)/shard_map/ppermute | solution.py:1556
  587.4 1.2 copy-start.1
  588.6 34.9 %copy-start.3 = (bf16[192,1152]{1,0:T(8,128)(2,1)S(1)}, bf16[192,1152]{1,0:T(8,128)(2,1)}, u32[]{:S(2)}) copy-start(bf16[192,1152]{1,0:T(8,128)(2,1)} %reduce-scatter.5.cloned.1.call-done.down_ref) | copy-start | bytes 1327108
  623.4 54.1 %collective-permute-start.2 = (bf16[72,7296]{1,0:T(8,128)(2,1)}, bf16[72,7296]{1,0:T(8,128)(2,1)S(1)}, u32[]{:S(2)}, u32[]{:S(2)}) collective-permute-start(bf16[72,7296]{1,0:T(8,128)(2,1)} %reduce-scatter.7.cloned.1.call-done.wide_ref), channel_id=1, source_target_pairs={{0,4},{4,0},{1,5},{5,1},{2,6},{6,2},{3,7},{7,3},{8,12},{12,8},{9,1... | collective-permute-start | bytes 3151880 | tf_op jit(solution)/shard_map/ppermute | solution.py:1556
  623.5 54.0 %collective-permute-start.3 = (bf16[192,1152]{1,0:T(8,128)(2,1)S(1)}, bf16[192,1152]{1,0:T(8,128)(2,1)S(1)}, u32[]{:S(2)}, u32[]{:S(2)}) collective-permute-start(bf16[192,1152]{1,0:T(8,128)(2,1)S(1)} %copy-done.3), channel_id=1, source_target_pairs={{0,4},{4,0},{1,5},{5,1},{2,6},{6,2},{3,7},{7,3},{8,12},{12,8},{9,1... | collective-permute-start | bytes 1327112 | tf_op jit(solution)/shard_map/ppermute | solution.py:1556
  677.5 0.8 copy-start.4
  678.2 1.0 copy-start.2
Sparse Core Ops, SparseCore 0:
  10.3 80.7 all-gather.4
  93.3 88.0 all-gather.2
  336.1 93.3 reduce-scatter.4
  434.1 176.7 reduce-scatter.6

commit v4 on v3

--- a/solution.py
+++ b/solution.py
@@ -27,10 +27,16 @@
     return pl.BlockSpec(shape, lambda *_: zeros, pipeline_mode=pl.Buffered(1))
 
 
-def project_kernel(x_ref, gain_ref, w_ref, cos_ref, sin_ref, q_ref, k_ref, v_ref, kv_ref, nq_ref, nk_ref, *, prompt_steps):
+def project_kernel(
+    x_ref, w_ref, cos_ref, sin_ref, q_ref, k_ref, v_ref, kv_ref, nq_ref, nk_ref, gains_ref, *, prompt_steps
+):
+    @pl.when(pl.program_id(0) == 0)
+    def _():
+        gains_ref[...] = w_ref[:, w_ref.shape[1] - 128 :].astype(f32).T[: gains_ref.shape[0]]
+
     x = x_ref[...].astype(f32)
     inverse = lax.rsqrt(jnp.mean(x * x, axis=-1, keepdims=True) + norm_eps)
-    h = (x * inverse * gain_ref[...]).astype(bf16)
+    h = (x * inverse * gains_ref[0:1]).astype(bf16)
     q_rows, kv_rows = q_ref.shape[0], k_ref.shape[0]
     half = HEAD_WIDTH // 2
     scale = LOG2E * HEAD_WIDTH**-0.5
@@ -72,7 +78,7 @@
         kv_ref[1] = v_ref[...]
 
 
-def project(x, gain, w, cos, sin, q_rows, kv_rows, prompt_rows, tile=512):
+def project(x, w, cos, sin, q_rows, kv_rows, prompt_rows, tile=512):
     rows, width = x.shape
     prompt_steps = prompt_rows // tile
     cols = lambda n: pl.BlockSpec((n, tile), lambda i: (0, i))
@@ -81,7 +87,6 @@
         grid=(rows // tile,),
         in_specs=[
             pl.BlockSpec((tile, width), lambda i: (i, 0)),
-            resident(gain.shape),
             resident(w.shape),
             cols(cos.shape[0]),
             cols(cos.shape[0]),
@@ -93,6 +98,7 @@
             pl.BlockSpec((2, kv_rows, tile), lambda i: (0, 0, jnp.minimum(i, prompt_steps - 1))),
             cols(1),
             cols(1),
+            pl.BlockSpec((8, width), lambda i: (0, 0)),
         ),
         out_shape=(
             jax.ShapeDtypeStruct((q_rows, rows), bf16),
@@ -101,10 +107,11 @@
             jax.ShapeDtypeStruct((2, kv_rows, prompt_rows), bf16),
             jax.ShapeDtypeStruct((1, rows), f32),
             jax.ShapeDtypeStruct((1, rows), f32),
+            jax.ShapeDtypeStruct((8, width), f32),
         ),
         compiler_params=pltpu.CompilerParams(vmem_limit_bytes=60 * MIB),
         name="project",
-    )(x, gain, w, cos, sin)
+    )(x, w, cos, sin)
 
 
 ONES = 16
@@ -525,7 +532,7 @@
 
 def middle_kernel(
     x_ref, dy_ref, o_ref, gain_ref, wide_any, wd_any,
-    out_ref, h2_ref, hidden_ref, dgate_ref, dup_ref, dattn_ref, dob_ref, delta_ref, dgain_ref,
+    out_ref, h2_ref, hidden_ref, dgate_ref, dup_ref, dattn_ref, dob_ref, delta_ref,
     wo_ref, wg_ref, wu_ref, wd_ref, sems, *, chunk
 ):
     step = pl.program_id(0)
@@ -546,13 +553,12 @@
     def _():
         for copy in copies:
             copy.start()
-        dgain_ref[...] = jnp.zeros_like(dgain_ref)
         copies[0].wait()
 
     ob = o_ref[...]
     x1 = x_ref[...].astype(f32) + contract(ob, wo_ref[...], 0, 0)
     inverse = lax.rsqrt(jnp.mean(x1 * x1, axis=-1, keepdims=True) + norm_eps)
-    gain = gain_ref[...]
+    gain = gain_ref[1:2]
     h2 = (x1 * inverse * gain).astype(bf16)
     h2_ref[...] = h2
     dy = dy_ref[...]
@@ -581,7 +587,6 @@
         part = contract(dgate, wg_ref[:, span], 1, 1) + contract(dup, wu_ref[:, span], 1, 1)
         dh2 = part if dh2 is None else dh2 + part
     out_ref[...] = result.astype(bf16)
-    dgain_ref[...] += jnp.sum(dh2 * x1 * inverse, axis=0, keepdims=True)
     u = dh2 * gain
     dx1 = dy.astype(f32) + inverse * u - x1 * (inverse * inverse * inverse) * jnp.mean(
         u * x1, axis=-1, keepdims=True
@@ -617,12 +622,11 @@
             by_row(width), by_row(width), by_row(hidden), by_row(hidden), by_row(hidden), by_row(width),
             pl.BlockSpec((q_rows, tile), lambda i: (0, i)),
             pl.BlockSpec((kv_heads, group, tile), lambda i: (0, 0, i)),
-            pl.BlockSpec((1, width), lambda i: (0, 0)),
         ),
         out_shape=(
             shape((rows, width), bf16), shape((rows, width), bf16), shape((rows, hidden), bf16),
             shape((rows, hidden), bf16), shape((rows, hidden), bf16), shape((rows, width), bf16),
-            shape((q_rows, rows), bf16), shape((kv_heads, group, rows), f32), shape((1, width), f32),
+            shape((q_rows, rows), bf16), shape((kv_heads, group, rows), f32),
         ),
         scratch_shapes=[pltpu.VMEM(s, bf16) for s in ((width, q_rows), (width, hidden), (width, hidden), wd.shape)]
         + [pltpu.SemaphoreType.DMA((4,))],
@@ -684,17 +688,10 @@
     )(o, h2, dgate, dup, dattn)
 
 
-def finish_kernel(
-    x_ref, dattn_ref, gain_ref, w_ref, dq_ref, dk_ref, dv_ref, dkv_in_ref, cos_ref, sin_ref,
-    dgain_f_ref, out_ref, dw_ref, acc_ref, dgain_ref, *, prompt_steps
+def last_grads_kernel(
+    x_ref, gain_ref, dq_ref, dk_ref, dv_ref, dkv_in_ref, cos_ref, sin_ref, lin_ref, dw_ref, acc_ref, *, prompt_steps
 ):
     step = pl.program_id(0)
-
-    @pl.when(step == 0)
-    def _():
-        dgain_ref[...] = jnp.zeros_like(dgain_ref)
-        acc_ref[...] = jnp.zeros_like(acc_ref)
-
     half = HEAD_WIDTH // 2
     cos, sin = cos_ref[...], sin_ref[...]
 
@@ -717,79 +714,85 @@
         ],
         axis=0,
     ).astype(bf16).T
-    inner = lin.shape[1]
+    lin_ref[...] = lin
     x = x_ref[...].astype(f32)
     inverse = lax.rsqrt(jnp.mean(x * x, axis=-1, keepdims=True) + norm_eps)
-    h = (x * inverse * gain_ref[...]).astype(bf16)
-    acc_ref[...] += contract(h, lin, 0, 0)
-    dh = contract(lin, w_ref[:, :inner], 1, 1)
-    dgain_ref[0:1] += jnp.sum(dh * x * inverse, axis=0, keepdims=True)
-    u = dh * gain_ref[...]
-    out_ref[...] = (
-        dattn_ref[...].astype(f32)
-        + inverse * u
-        - x * (inverse * inverse * inverse) * jnp.mean(u * x, axis=-1, keepdims=True)
-    )
+    h = (x * inverse * gain_ref[0:1]).astype(bf16)
+    part = contract(h, lin, 0, 0)
+
+    @pl.when(step == 0)
+    def _():
+        acc_ref[...] = part
+
+    @pl.when(step > 0)
+    def _():
+        acc_ref[...] += part
 
     @pl.when(step == pl.num_programs(0) - 1)
     def _():
-        dw_ref[:, :inner] = acc_ref[...].astype(bf16)
-        dgain_ref[1:2] = dgain_f_ref[...]
-        dw_ref[:, inner:] = dgain_ref[...].T.astype(bf16)
-
-
-def finish(x, dattn, gain, w, dq, dk, dv, dkv_in, cos, sin, dgain_f, tile=256):
+        dw_ref[...] = acc_ref[...].astype(bf16)
+
+
+def last_grads(x, gains, dq, dk, dv, dkv_in, cos, sin, tile=512):
     rows, width = x.shape
-    by_row = pl.BlockSpec((tile, width), lambda i: (i, 0))
     cols = lambda n: pl.BlockSpec((n, tile), lambda i: (0, i))
     steps = dkv_in.shape[2] // tile
     few = pl.BlockSpec((2, dk.shape[0], tile), lambda i: (0, 0, jnp.minimum(i, steps - 1)))
     shape = jax.ShapeDtypeStruct
     inner = dq.shape[0] + dk.shape[0] + dv.shape[0]
     return pl.pallas_call(
-        functools.partial(finish_kernel, prompt_steps=steps),
+        functools.partial(last_grads_kernel, prompt_steps=steps),
         grid=(rows // tile,),
-        in_specs=[by_row, by_row, resident(gain.shape), resident(w.shape),
-                  cols(dq.shape[0]), cols(dk.shape[0]), cols(dv.shape[0]),
-                  few,
-                  cols(cos.shape[0]), cols(cos.shape[0]), resident(dgain_f.shape)],
-        out_specs=(by_row, pl.BlockSpec(w.shape, lambda i: (0, 0))),
-        out_shape=(shape((rows, width), f32), shape(w.shape, bf16)),
-        scratch_shapes=[pltpu.VMEM((width, inner), f32), pltpu.VMEM((w.shape[1] - inner, width), f32)],
+        in_specs=[pl.BlockSpec((tile, width), lambda i: (i, 0)), resident(gains.shape),
+                  cols(dq.shape[0]), cols(dk.shape[0]), cols(dv.shape[0]), few,
+                  cols(cos.shape[0]), cols(cos.shape[0])],
+        out_specs=(pl.BlockSpec((tile, inner), lambda i: (i, 0)), pl.BlockSpec((width, inner), lambda i: (0, 0))),
+        out_shape=(shape((rows, inner), bf16), shape((width, inner), bf16)),
+        scratch_shapes=[pltpu.VMEM((width, inner), f32)],
         compiler_params=pltpu.CompilerParams(vmem_limit_bytes=60 * MIB),
-        name="finish",
-    )(x, dattn, gain, w, dq, dk, dv, dkv_in, cos, sin, dgain_f)
-
-
-def settle_kernel(first_ref, wide_ref, wide_in_ref, down_ref, down_in_ref, *outs, widths):
-    refs = list(outs)
+        name="last_grads",
+    )(x, gains, dq, dk, dv, dkv_in, cos, sin)
+
+
+def settle_kernel(first_ref, wide_ref, wide_in_ref, down_ref, down_in_ref, gains_ref, wa_ref, wb_ref, wc_ref, wg_ref, wu_ref, *outs):
+    da, db, dc, dgate, dup, dout, ddown, gain_a, gain_f = outs
+    gains = gains_ref[...].astype(f32)
+
+    def spread(total, which):
+        return jnp.broadcast_to(total / gains[:, which : which + 1], gains.shape).T[0:1]
+
+    total = None
     at = 0
-    for width in widths[0]:
-        refs.pop(0)[...] = first_ref[:, at : at + width]
-        at += width
-    gains = first_ref[:, at:].T
-    refs.pop(0)[...] = gains[0:1]
-    refs.pop(0)[...] = gains[1:2]
+    for out, weight in ((da, wa_ref), (db, wb_ref), (dc, wc_ref)):
+        value = first_ref[:, at : at + out.shape[1]]
+        out[...] = value
+        part = jnp.sum(value * weight[...].astype(f32), axis=1, keepdims=True)
+        total = part if total is None else total + part
+        at += out.shape[1]
+    gain_a[...] = spread(total, 0)
+    total = None
     at = 0
-    for width in widths[1]:
-        span = slice(at, at + width)
-        refs.pop(0)[...] = wide_ref[:, span].astype(f32) + wide_in_ref[:, span].astype(f32)
-        at += width
-    refs.pop(0)[...] = down_ref[...].astype(f32) + down_in_ref[...].astype(f32)
-
-
-def settle(first, wide, wide_in, down, down_in, first_widths, wide_widths):
+    for out, weight in ((dgate, wg_ref), (dup, wu_ref), (dout, None)):
+        span = slice(at, at + out.shape[1])
+        value = wide_ref[:, span].astype(f32) + wide_in_ref[:, span].astype(f32)
+        out[...] = value
+        if weight is not None:
+            part = jnp.sum(value * weight[...].astype(f32), axis=1, keepdims=True)
+            total = part if total is None else total + part
+        at += out.shape[1]
+    gain_f[...] = spread(total, 1)
+    ddown[...] = down_ref[...].astype(f32) + down_in_ref[...].astype(f32)
+
+
+def settle(first, wide, wide_in, down, down_in, gains, wa, wb, wc, wo, wg, wu):
     rows = first.shape[0]
     shape = jax.ShapeDtypeStruct
     return pl.pallas_call(
-        functools.partial(settle_kernel, widths=(first_widths, wide_widths)),
-        out_shape=[shape((rows, n), f32) for n in first_widths]
-        + [shape((1, rows), f32)] * 2
-        + [shape((rows, n), f32) for n in wide_widths]
-        + [shape(down.shape, f32)],
+        settle_kernel,
+        out_shape=[shape(w.shape, f32) for w in (wa, wb, wc, wg, wu, wo, down)] + [shape((1, rows), f32)] * 2,
         compiler_params=pltpu.CompilerParams(vmem_limit_bytes=60 * MIB),
         name="settle",
-    )(first, wide, wide_in, down, down_in)
+    )(first, wide, wide_in, down, down_in, gains, wa, wb, wc, wg, wu)
 
 
 MESH_ID = pl.DeviceIdType.MESH
@@ -839,7 +842,8 @@
         return copy
 
 
-def gather_kernel(shard_ref, out_ref, send_sems, recv_sems, own_sem, *, depth, split):
+def gather_kernel(*refs, depth, split):
+    *shards, wo_ref, wg_ref, wu_ref, out_ref, wide_ref, send_sems, recv_sems, own_sems = refs
     z, y, x, core = whereabouts()
     along, over_x, over_y, over_core = neighbours(depth)
     columns = out_ref.shape[2]
@@ -850,10 +854,22 @@
     copies = Copies(send_sems, recv_sems)
     view = lambda slot, span: out_ref.at[slot, :, span]
 
-    own = pltpu.make_async_copy(shard_ref, out_ref.at[me], own_sem)
-    own.start()
-    own.wait()
+    def side_by_side(sources, target, first_sem):
+        at = 0
+        placed = []
+        for index, source in enumerate(sources):
+            width = source.shape[1]
+            copy = pltpu.make_async_copy(source, target.at[:, pl.ds(at, width)], own_sems.at[first_sem + index])
+            copy.start()
+            placed.append(copy)
+            at += width
+        return placed
+
+    own = side_by_side(shards, out_ref.at[me], 0)
+    wide = side_by_side((wo_ref, wg_ref, wu_ref), wide_ref, len(shards))
     greet(along + [over_x, over_y, over_core])
+    for copy in own:
+        copy.wait()
 
     def send(slot, span, device):
         copy = copies.make(view(slot, span), view(slot, span), device)
@@ -873,7 +889,8 @@
     for part in range(2):
         for d in range(1, depth):
             from_z[d, part] = send(me, spans[part], along[d - 1])
-        onward(me, part, 0, 0)
+        from_x[0, part] = send(me, spans[part], over_x)
+    from_core.append(send(me, slice(None), over_core))
     for part in range(2):
         for d in range(1, depth):
             from_z[d, part].wait_recv()
@@ -883,7 +900,7 @@
             from_x[d, part].wait_recv()
             onward(slot_at((z + depth - d) % depth, 1 - x, core), part, d, 1)
     for side in range(2):
-        for d in range(depth):
+        for d in range(1 - side, depth):
             from_y[d, side].wait_recv()
             slot = slot_at((z + depth - d) % depth, x if side == 0 else 1 - x, core)
             from_core.append(send(slot, got, over_core))
@@ -891,82 +908,146 @@
         copy.wait_recv()
     for copy in copies.made:
         copy.wait_send()
-
-
-def gather_all(shard, depth, split):
-    rows, columns = shard.shape
-    count = 2 * (depth - 1) + 2 * depth + 2 * depth + 6 * depth
+    for copy in wide:
+        copy.wait()
+
+
+def gather_all(shards, wide, depth, split):
+    rows = shards[0].shape[0]
+    columns = sum(shard.shape[1] for shard in shards)
+    count = 2 * (depth - 1) + 2 * depth + 2 * depth - 1 + 3 * (2 * depth - 1) + 1
     return pl.pallas_call(
         functools.partial(gather_kernel, depth=depth, split=split),
-        in_specs=[pl.BlockSpec(memory_space=pltpu.VMEM)],
-        out_specs=pl.BlockSpec(memory_space=pltpu.VMEM),
-        out_shape=jax.ShapeDtypeStruct((4 * depth, rows, columns), shard.dtype),
+        in_specs=[pl.BlockSpec(memory_space=pl.ANY)] * (len(shards) + len(wide)),
+        out_specs=(pl.BlockSpec(memory_space=pltpu.VMEM), pl.BlockSpec(memory_space=pl.ANY)),
+        out_shape=(
+            jax.ShapeDtypeStruct((4 * depth, rows, columns), bf16),
+            jax.ShapeDtypeStruct((rows, sum(shard.shape[1] for shard in wide)), bf16),
+        ),
         scratch_shapes=[
             pltpu.SemaphoreType.DMA((count,)),
             pltpu.SemaphoreType.DMA((count,)),
-            pltpu.SemaphoreType.DMA,
+            pltpu.SemaphoreType.DMA((len(shards) + len(wide),)),
         ],
         compiler_params=pltpu.CompilerParams(
             collective_id=1, has_side_effects=True, vmem_limit_bytes=60 * MIB
         ),
         name="gather_all",
-    )(shard)
+    )(*shards, *wide)
 
 
 def reduce_kernel(
-    part_ref, out_ref, core_ref, sum_ref, x_ref, line_ref, z_ref, last_ref, twin_ref, send_sems, recv_sems, *, depth
+    part_ref, lin_ref, w_ref, gain_ref, x_ref, dattn_ref, out_ref, tokens_ref,
+    core_ref, sum_ref, over_ref, line_ref, z_ref, last_ref, twin_ref, send_sems, recv_sems, *, depth
 ):
+    step = pl.program_id(0)
+    steps = pl.num_programs(0)
     z, y, x, core = whereabouts()
     along, over_x, over_y, over_core = neighbours(depth)
-    copies = Copies(send_sems, recv_sems)
-    greet(along + [over_x, over_y, over_core])
-
-    def send(source, target, device):
-        copy = copies.make(source, target, device)
-        copy.start()
-        return copy
 
     distances = list(range(1, depth)) + [0]
     order = [(d, side) for side in (1, 0) for d in distances]
     place = lambda d, side: ((z + d) % depth, x if side == 0 else 1 - x)
-    from_core = []
-    for at, (d, side) in enumerate(order):
-        to_z, to_x = place(d, side)
-        from_core.append(send(part_ref.at[slot_at(to_z, to_x, 1 - core)], core_ref.at[at], over_core))
-    from_x = []
-    for at, (d, side) in enumerate(order):
-        from_core[at].wait_recv()
-        to_z, to_x = place(d, side)
-        sum_ref[at] = (part_ref[slot_at(to_z, to_x, core)].astype(f32) + core_ref[at].astype(f32)).astype(bf16)
-        if side == 1:
-            from_x.append(send(sum_ref.at[at], x_ref.at[at], over_x))
-    from_z = []
-    for at, d in enumerate(distances):
-        from_x[at].wait_recv()
-        line_ref[at] = (sum_ref[depth + at].astype(f32) + x_ref[at].astype(f32)).astype(bf16)
-        if d:
-            from_z.append(send(line_ref.at[at], z_ref.at[at], along[d - 1]))
-    total = line_ref[depth - 1].astype(f32)
-    for at in range(depth - 1):
-        from_z[at].wait_recv()
-        total = total + z_ref[at].astype(f32)
-    last_ref[...] = total.astype(bf16)
-    twin = send(last_ref, twin_ref, over_y)
-    twin.wait_recv()
-    out_ref[...] = total + twin_ref[...].astype(f32)
-    for copy in copies.made:
-        copy.wait_send()
-
-
-def reduce_all(parts, depth):
+
+    def remote(source, target, device, at):
+        return pltpu.make_async_remote_copy(
+            src_ref=source,
+            dst_ref=target,
+            send_sem=send_sems.at[at],
+            recv_sem=recv_sems.at[at],
+            device_id=device,
+            device_id_type=MESH_ID,
+        )
+
+    def to_core(at):
+        to_z, to_x = place(*order[at])
+        return remote(part_ref.at[slot_at(to_z, to_x, 1 - core)], core_ref.at[at], over_core, at)
+
+    def to_x(at):
+        return remote(sum_ref.at[at], over_ref.at[at], over_x, 2 * depth + at)
+
+    def to_z(at):
+        return remote(line_ref.at[at], z_ref.at[at], along[distances[at] - 1], 3 * depth + at)
+
+    def to_y():
+        return remote(last_ref, twin_ref, over_y, 4 * depth - 1)
+
+    def core_sums(at):
+        to_core(at).wait_recv()
+        own_z, own_x = place(*order[at])
+        sum_ref[at] = (part_ref[slot_at(own_z, own_x, core)].astype(f32) + core_ref[at].astype(f32)).astype(bf16)
+
+    @pl.when(step == 0)
+    def _():
+        greet(along + [over_x, over_y, over_core])
+        for at in range(2 * depth):
+            to_core(at).start()
+
+    @pl.when(step == 1)
+    def _():
+        for at in range(depth):
+            core_sums(at)
+            to_x(at).start()
+
+    @pl.when(step == 2)
+    def _():
+        for at in range(depth, 2 * depth):
+            core_sums(at)
+
+    for at in range(depth):
+
+        @pl.when(step == jnp.minimum(3 + at, steps - 1))
+        def _():
+            to_x(at).wait_recv()
+            line_ref[at] = (sum_ref[depth + at].astype(f32) + over_ref[at].astype(f32)).astype(bf16)
+            if distances[at]:
+                to_z(at).start()
+
+    lin = lin_ref[...]
+    dh = contract(lin, w_ref[:, : lin.shape[1]], 1, 1)
+    tokens = x_ref[...].astype(f32)
+    inverse = lax.rsqrt(jnp.mean(tokens * tokens, axis=-1, keepdims=True) + norm_eps)
+    u = dh * gain_ref[0:1]
+    tokens_ref[...] = (
+        dattn_ref[...].astype(f32)
+        + inverse * u
+        - tokens * (inverse * inverse * inverse) * jnp.mean(u * tokens, axis=-1, keepdims=True)
+    )
+
+    @pl.when(step == steps - 1)
+    def _():
+        total = line_ref[depth - 1].astype(f32)
+        for at in range(depth - 1):
+            to_z(at).wait_recv()
+            total = total + z_ref[at].astype(f32)
+        last_ref[...] = total.astype(bf16)
+        to_y().start()
+        to_y().wait_recv()
+        out_ref[...] = total + twin_ref[...].astype(f32)
+        for at in range(2 * depth):
+            to_core(at).wait_send()
+        for at in range(depth):
+            to_x(at).wait_send()
+        for at in range(depth - 1):
+            to_z(at).wait_send()
+        to_y().wait_send()
+
+
+def reduce_all(parts, lin, w, gains, x, dattn, depth, tile=256):
     slots, rows, columns = parts.shape
-    count = 2 * depth + depth + depth - 1 + 1
+    count, width = x.shape
+    sems = 4 * depth
     buffer = lambda *count: pltpu.VMEM(count + (rows, columns), bf16)
+    by_row = lambda n: pl.BlockSpec((tile, n), lambda i: (i, 0))
     return pl.pallas_call(
         functools.partial(reduce_kernel, depth=depth),
-        in_specs=[pl.BlockSpec(memory_space=pltpu.VMEM)],
-        out_specs=pl.BlockSpec(memory_space=pltpu.VMEM),
-        out_shape=jax.ShapeDtypeStruct((rows, columns), f32),
+        grid=(count // tile,),
+        in_specs=[
+            resident(parts.shape), by_row(lin.shape[1]), resident(w.shape), resident(gains.shape),
+            by_row(width), by_row(width),
+        ],
+        out_specs=(pl.BlockSpec((rows, columns), lambda i: (0, 0)), by_row(width)),
+        out_shape=(jax.ShapeDtypeStruct((rows, columns), f32), jax.ShapeDtypeStruct((count, width), f32)),
         scratch_shapes=[
             buffer(2 * depth),
             buffer(2 * depth),
@@ -975,14 +1056,14 @@
             buffer(depth - 1),
             buffer(),
             buffer(),
-            pltpu.SemaphoreType.DMA((count,)),
-            pltpu.SemaphoreType.DMA((count,)),
+            pltpu.SemaphoreType.DMA((sems,)),
+            pltpu.SemaphoreType.DMA((sems,)),
         ],
         compiler_params=pltpu.CompilerParams(
             collective_id=2, has_side_effects=True, vmem_limit_bytes=60 * MIB
         ),
         name="reduce_all",
-    )(parts)
+    )(parts, lin, w, gains, x, dattn)
 
 
 rope_base = 10000.0
@@ -1573,17 +1654,13 @@
 
     depth = lax.axis_size("group")
 
-    gains = jnp.pad(jnp.stack([attention_gain, feedforward_gain], axis=1), ((0, 0), (0, 126)))
-    wide = lax.all_gather(
-        jnp.concatenate([output_weight, gate_weight, up_weight], axis=1), OWNERS, axis=0, tiled=True
-    )
+    gain_columns = jnp.pad(jnp.stack([attention_gain, feedforward_gain], axis=1), ((0, 0), (0, 126)))
+    shards = (query_weight, key_matrix, value_matrix, gain_columns)
+    split = sum(shard.shape[1] for shard in shards) // 3 // 128 * 128
     wd = lax.all_gather(down_weight, OWNERS, axis=0, tiled=True)
-    shard = jnp.concatenate([query_weight, key_matrix, value_matrix, gains], axis=1)
-    end = q_rows + 2 * kv_rows
-    split = shard.shape[1] // 3 // 128 * 128
-    first = gather_all(shard, depth, split).reshape(width, -1)
-    gain_pair = first[:, end : end + 2].astype(f32).T
-    gain_a, gain_f = gain_pair[0:1], gain_pair[1:2]
+    first, wide = gather_all(shards, (output_weight, gate_weight, up_weight), depth, split)
+    first = first.reshape(width, -1)
+    wide = lax.all_gather(wide, OWNERS, axis=0, tiled=True)
 
     at = jnp.arange(rows, dtype=jnp.int32)
     positions = jnp.where(
@@ -1594,11 +1671,11 @@
     angles = frequency[:, None] * positions.astype(f32)[None, :]
     cos, sin = jnp.cos(angles), jnp.sin(angles)
 
-    q, k, v, kv, norm_q, norm_k = project(x, gain_a, first, cos, sin, q_rows, kv_rows, prompt_rows)
+    q, k, v, kv, norm_q, norm_k, gains = project(x, first, cos, sin, q_rows, kv_rows, prompt_rows)
     kv_other = swap(kv)
     acc, top, p_own = own_forward(q, k, v, norm_q, norm_k, kv_heads, prompt_rows)
     o, own_scale, far_scale, p_far = other_forward(seen[None], q, kv_other, norm_q, acc, top, kv_heads, prompt_rows)
-    layer_out, h2, hid, dgate, dup, dattn, dob, delta, dgain_f = middle(x, dy, o, gain_f, wide, wd, kv_heads)
+    layer_out, h2, hid, dgate, dup, dattn, dob, delta = middle(x, dy, o, gains, wide, wd, kv_heads)
     scatter = lambda a: lax.psum_scatter(a, OWNERS, scatter_dimension=0, tiled=True)
     d_down = down_grads(dy, hid)
     h2, d_down = lax.optimization_barrier((h2, d_down))
@@ -1611,12 +1688,13 @@
     d_down, dkv_in = lax.optimization_barrier((d_down, dkv_in))
     d_down_in = swap(d_down)
     dq, dk, dv = own_backward(q, dob, own_scale, delta, k, v, p_own, dq, kv_heads, prompt_rows)
-    grad_tokens, d_first = finish(x, dattn, gain_a, first, dq, dk, dv, dkv_in, cos, sin, dgain_f)
+    lin, d_first = last_grads(x, gains, dq, dk, dv, dkv_in, cos, sin)
     d_first, d_wide = lax.optimization_barrier((d_first, d_wide))
     d_wide_in = swap(d_wide)
-    d_first = reduce_all(d_first.reshape(4 * depth, shard_rows, -1), depth)
-    d_q, d_k, d_v, d_gain_a, d_gain_f, d_gate, d_up, d_out, d_down = settle(
-        d_first, d_wide, d_wide_in, d_down, d_down_in, (q_rows, kv_rows, kv_rows), (hidden, hidden, q_rows)
+    d_first, grad_tokens = reduce_all(d_first.reshape(4 * depth, shard_rows, -1), lin, first, gains, x, dattn, depth)
+    d_q, d_k, d_v, d_gate, d_up, d_out, d_down, d_gain_a, d_gain_f = settle(
+        d_first, d_wide, d_wide_in, d_down, d_down_in, gain_columns,
+        query_weight, key_matrix, value_matrix, output_weight, gate_weight, up_weight,
     )
     return (
         layer_out[None],

time: 695 us -> 681 us (0.980)
  Pallas kernels: 622 us -> 607 us
    pallas_call x3, Pallas kernels: 90.6 us -> 78.7 us  [the longest x1 52.2 us: reduce_all(): pl.pallas_call(functools.partial(reduce_kernel, depth=depth), grid=(count...]
    unnamed x12 -> x11, local copies, waits for them, and re-layouts: 4.04 us -> 11.4 us
  transfers between devices with their start and end apart: 8 -> 8, of which waited for: 1 -> 1; matrix products, arithmetic and copies ran while one was open for 1% -> 1% of each run, Pallas kernels for 67% -> 66%
where the time goes in v4:
time: 681 us; the launch traced here: 677 us
  Pallas kernels  607 us (89%)
  starting transfers between devices  29 us (4%)
  between operations  15.4 us (2%)
  local copies, waits for them, and re-layouts  12.1 us (2%)
  waiting for transfers between devices  9.05 us (1%)
    pallas_call x1, Pallas kernels, middle(): pl.pallas_call(functools.partial(middle_kernel, chunk=chunk), grid=(rows...  132 us
    pallas_call x1, Pallas kernels, own_backward(): pl.pallas_call(functools.partial(own_backward_kernel, group=group, prompt...  103 us
    pallas_call x1, Pallas kernels, other_backward(): pl.pallas_call(functools.partial(other_backward_kernel, group=group, prom...  71.8 us
    pallas_call x1, Pallas kernels, reduce_all(): pl.pallas_call(functools.partial(reduce_kernel, depth=depth), grid=(count...  52.2 us
    pallas_call x1, Pallas kernels, own_forward(): pl.pallas_call(functools.partial(own_forward_kernel, group=group, prompt_...  51.7 us
    pallas_call x1, Pallas kernels, wide_grads(): pl.pallas_call(functools.partial(wide_grads_kernel, each=each), grid=(ste...  47.4 us
    pallas_call x1, Pallas kernels, gather_all(): pl.pallas_call(functools.partial(gather_kernel, depth=depth, split=split)...  44.7 us
    pallas_call x1, Pallas kernels, other_forward(): pl.pallas_call(functools.partial(other_forward_kernel, group=group, promp...  36.3 us
  transfers between devices with their start and end apart: 8, of which 1 were waited for; matrix products, arithmetic and copies ran while one was open for 1% of the time, Pallas kernels for 66%

profile of v4, /device:TPU:8, one launch (start us, length us, event | category | flops | bytes accessed | tf_op | source)
XLA Modules:
  0.0 676.8 jit_solution(12841440410154407653)
XLA Ops:
  7.2 0.0 all-gather.5.cloned.1.call-start
  7.2 0.7 all-gather.5.cloned.1.call-update
  7.9 0.0 all-gather.3.cloned.1.call-start
  8.0 0.7 pad_maximum_fusion
  8.6 0.1 copy.25
  8.8 0.6 pad.4.refs_3_.gains_ref
  9.4 44.7 %gather_all.1 = (bf16[16,72,2048]{2,1,0:T(8,128)(2,1)}, bf16[72,7296]{1,0:T(8,128)(2,1)}) custom-call(bf16[72,1152]{1,0:T(8,128)(2,1)} %wa_ref.1, bf16[72,384]{1,0:T(8,128)(2,1)} %wb_ref.1, bf16[72,384]{1,0:T(8,128)(2,1)} %wc_ref.1, bf16[72,128]{1,0:T(8,128)(2,1)} %pad.4.refs_3_.gains_ref, bf16[72,1152]{1,0:T(8,128)(2,1)} %refs_4_.1, ...), custom_call_target="tpu_custom_call" | custom-call | tf_op jit(solution)/shard_map/gather_all/pallas_call | solution.py:919
  54.1 0.0 reduce-scatter.5.cloned.1.call-start
  54.2 1.2 fusion.7
  56.1 1.8 multiply_sine_fusion
  57.9 20.2 %project.1 = (bf16[1152,2048]{1,0:T(8,128)(2,1)}, bf16[384,2048]{1,0:T(8,128)(2,1)}, bf16[384,2048]{1,0:T(8,128)(2,1)}, bf16[2,384,1024]{2,1,0:T(8,128)(2,1)}, f...) custom-call(bf16[2048,1152]{1,0:T(8,128)(2,1)} %bitcast.13, bf16[1152,2048]{1,0:T(8,128)(2,1)} %bitcast.19, ...), custom_call_target="tpu_custom_call" | custom-call | tf_op jit(solution)/shard_map/project/pallas_call | solution.py:85
  78.1 0.2 collective-permute-start
  79.0 51.7 %own_forward.1 = (f32[1440,2048]{1,0:T(8,128)}, f32[6,3,2048]{2,1,0:T(4,128)}, bf16[18,2048,1024]{2,1,0:T(8,128)(2,1)}) custom-call(bf16[1152,2048]{1,0:T(8,128)(2,1)} %get-tuple-element.62.q_ref, bf16[384,2048]{1,0:T(8,128)(2,1)} %get-tuple-element.65.k_ref, bf16[384,2048]{1,0:T(8,128)(2,1)} %get-tuple-element.66.v_ref, ...), custom_call_target="tpu_custom_call" | custom-call | tf_op jit(solution)/shard_map/own_forward/pallas_call | solution.py:229
  130.7 1.2 copy-done
  131.9 36.3 %other_forward.1 = (bf16[1152,2048]{1,0:T(8,128)(2,1)}, f32[6,3,2048]{2,1,0:T(4,128)}, f32[6,3,2048]{2,1,0:T(4,128)}, bf16[18,1024,2048]{2,1,0:T(8,128)(2,1)}) custom-call(s32[1]{0:T(128)} %bitcast.2.seen_ref, bf16[1152,2048]{1,0:T(8,128)(2,1)} %get-tuple-element.62.q_ref, bf16[2,384,1024]{2,1,0:T(8,128)(2,1)} %copy-done, bf16[2,384,1024]{2,1,0:T(8,128)(2,1)} %copy-done, ...), custom_call_target="tpu_custom_call" | custom-call | tf_op jit(solution)/shard_map/other_forward/pallas_call | solution.py:326
  168.2 8.3 %all-gather.3.cloned.1.call-done.wide_any = bf16[1152,7296]{1,0:T(8,128)(2,1)} async-done(((bf16[72,7296]{1,0:T(8,128)(2,1)}), bf16[1152,7296]{1,0:T(8,128)(2,1)}) %all-gather.3.cloned.1.call-update) | async-done | bytes 16810000 | tf_op jit(solution)/shard_map/all_gather | solution.py:1663
  176.4 132.2 %middle.1 = (bf16[2048,1152]{1,0:T(8,128)(2,1)}, bf16[2048,1152]{1,0:T(8,128)(2,1)}, bf16[2048,3072]{1,0:T(8,128)(2,1)}, bf16[2048,3072]{1,0:T(8,128)(2,1)}, bf1...) custom-call(bf16[2048,1152]{1,0:T(8,128)(2,1)} %bitcast.14, ...), custom_call_target="tpu_custom_call" | custom-call | tf_op jit(solution)/shard_map/middle/pallas_call | solution.py:616
  308.6 21.5 %down_grads.1 = bf16[3072,1152]{1,0:T(8,128)(2,1)} custom-call(bf16[2048,1152]{1,0:T(8,128)(2,1)} %bitcast.18, bf16[2048,3072]{1,0:T(8,128)(2,1)} %get-tuple-element.76.hidden_ref), custom_call_target="tpu_custom_call" | custom-call | tf_op jit(solution)/shard_map/down_grads/pallas_call | solution.py:645
  330.2 0.0 reduce-scatter.7.cloned.1.call-start
  330.2 47.4 %wide_grads.1 = bf16[1152,7296]{1,0:T(8,128)(2,1)} custom-call(bf16[1152,2048]{1,0:T(8,128)(2,1)} %get-tuple-element.70.o_ref, bf16[2048,1152]{1,0:T(8,128)(2,1)} %get-tuple-element.77.h2_ref, bf16[2048,3072]{1,0:T(8,128)(2,1)} %get-tuple-element.78.dgate_ref, bf16[2048,3072]{1,0:T(8,128)(2,1)} %get-tuple-element.79.dup_ref, ...), custom_call_target="tpu_custom_call" | custom-call | tf_op jit(solution)/shard_map/wide_grads/pallas_call | solution.py:678
  377.6 71.8 %other_backward.1 = (bf16[1152,2048]{1,0:T(8,128)(2,1)}, bf16[2,384,1024]{2,1,0:T(8,128)(2,1)}) custom-call(s32[1]{0:T(128)} %bitcast.2.seen_ref, bf16[1152,2048]{1,0:T(8,128)(2,1)} %get-tuple-element.62.q_ref, bf16[1152,2048]{1,0:T(8,128)(2,1)} %get-tuple-element.81.g_ref, f32[6,3,2048]{2,1,0:T(4,128)} %get-tuple-element.85.scale_ref, ...), custom_call_target="tpu_custom_call" | custom-call | tf_op jit(solution)/shard_map/other_backward/pallas_call | solution.py:437
  449.4 26.5 %collective-permute-start.1 = (bf16[2,384,1024]{2,1,0:T(8,128)(2,1)}, bf16[2,384,1024]{2,1,0:T(8,128)(2,1)S(1)}, u32[]{:S(2)}, u32[]{:S(2)}) collective-permute-start(bf16[2,384,1024]{2,1,0:T(8,128)(2,1)} %get-tuple-element.92), channel_id=1, source_target_pairs={{0,4},{4,0},{1,5},{5,1},{2,6},{6,2},{3,7},{7,3},{8,12},{12,8},{9,1... | collective-permute-start | bytes 4718600 | tf_op jit(solution)/shard_map/ppermute | solution.py:1637
  475.9 103.0 %own_backward.1 = (bf16[1152,2048]{1,0:T(8,128)(2,1)}, bf16[384,2048]{1,0:T(8,128)(2,1)}, bf16[384,2048]{1,0:T(8,128)(2,1)}) custom-call(bf16[1152,2048]{1,0:T(8,128)(2,1)} %get-tuple-element.62.q_ref, bf16[1152,2048]{1,0:T(8,128)(2,1)} %get-tuple-element.81.g_ref, f32[6,3,2048]{2,1,0:T(4,128)} %get-tuple-element.82.scale_ref, ...), custom_call_target="tpu_custom_call" | custom-call | tf_op jit(solution)/shard_map/own_backward/pallas_call | solution.py:511
  579.0 1.1 copy-done.1
  580.1 22.1 %last_grads.1 = (bf16[2048,1920]{1,0:T(8,128)(2,1)}, bf16[1152,1920]{1,0:T(8,128)(2,1)}) custom-call(bf16[2048,1152]{1,0:T(8,128)(2,1)} %bitcast.15, f32[8,1152]{1,0:T(8,128)} %get-tuple-element.71.gain_ref, bf16[1152,2048]{1,0:T(8,128)(2,1)} %get-tuple-element.88.dq_ref, bf16[384,2048]{1,0:T(8,128)(2,1)} %get-tuple-element.89.dk_ref, ...), custom_call_target="tpu_custom_call" | custom-call | tf_op jit(solution)/shard_map/last_grads/pallas_call | solution.py:743
  602.2 1.3 collective-permute-start.2
  603.5 0.8 collective-permute-start.3
  604.3 52.2 %reduce_all.1 = (f32[72,1920]{1,0:T(8,128)}, f32[2048,1152]{1,0:T(8,128)}) custom-call(bf16[16,72,1920]{2,1,0:T(8,128)(2,1)} %bitcast.22, bf16[2048,1920]{1,0:T(8,128)(2,1)} %get-tuple-element.97.lin_ref, bf16[1152,2048]{1,0:T(8,128)(2,1)} %bitcast.20, f32[8,1152]{1,0:T(8,128)} %get-tuple-element.71.gain_ref, bf16[2048,1152]{1,0:T(8,128)(2,1)} %bitcast.16, ...), custom_call_target="tpu_custom_call" | custom-call | tf_op jit(solution)/shard_map/reduce_all/pallas_call | solution.py:1042
  656.6 0.7 copy-done.4
  657.3 0.4 copy-done.2
  657.6 4.4 settle.1
  662.1 8.0 %copy.27 = f32[1,2048,1152]{2,1,0:T(8,128)} copy(f32[1,2048,1152]{2,1,0:T(8,128)} %bitcast.21) | data formatting | bytes 18874368
  (18 shorter events, 0.1 us)
Async XLA Ops:
  7.2 161.0 %all-gather.5.cloned.1.call-start = ((), (), s32[]{:S(2)}) async-start(), calls=%async_computation.3 | async-start | bytes 7520256 | tf_op jit(solution)/shard_map/all_gather | solution.py:1660
  7.9 168.5 %all-gather.3.cloned.1.call-start = ((), (), s32[]{:S(2)}) async-start(), calls=%async_computation.2 | async-start | bytes 17860608 | tf_op jit(solution)/shard_map/all_gather | solution.py:1663
  54.1 524.8 %reduce-scatter.5.cloned.1.call-start = ((), (), s32[]{:S(2)}) async-start(), calls=%async_computation.4 | async-start | bytes 7520256 | tf_op jit(solution)/shard_map/reduce_scatter | solution.py:1679
  78.1 52.6 %collective-permute-start = (bf16[2,384,1024]{2,1,0:T(8,128)(2,1)}, bf16[2,384,1024]{2,1,0:T(8,128)(2,1)S(1)}, u32[]{:S(2)}, u32[]{:S(2)}) collective-permute-start(bf16[2,384,1024]{2,1,0:T(8,128)(2,1)} %get-tuple-element.63), channel_id=1, source_target_pairs={{0,4},{4,0},{1,5},{5,1},{2,6},{6,2},{3,7},{7,3},{8,12},{12,8},{9,1... | collective-permute-start | bytes 4718600 | tf_op jit(solution)/shard_map/ppermute | solution.py:1637
  130.7 1.2 copy-start
  330.2 272.0 %reduce-scatter.7.cloned.1.call-start = ((), (), s32[]{:S(2)}) async-start(), calls=%async_computation.5 | async-start | bytes 17860608
  449.4 129.5 %collective-permute-start.1 = (bf16[2,384,1024]{2,1,0:T(8,128)(2,1)}, bf16[2,384,1024]{2,1,0:T(8,128)(2,1)S(1)}, u32[]{:S(2)}, u32[]{:S(2)}) collective-permute-start(bf16[2,384,1024]{2,1,0:T(8,128)(2,1)} %get-tuple-element.92), channel_id=1, source_target_pairs={{0,4},{4,0},{1,5},{5,1},{2,6},{6,2},{3,7},{7,3},{8,12},{12,8},{9,1... | collective-permute-start | bytes 4718600 | tf_op jit(solution)/shard_map/ppermute | solution.py:1637
  578.9 1.2 copy-start.1
  580.1 23.4 %copy-start.3 = (bf16[192,1152]{1,0:T(8,128)(2,1)S(1)}, bf16[192,1152]{1,0:T(8,128)(2,1)}, u32[]{:S(2)}) copy-start(bf16[192,1152]{1,0:T(8,128)(2,1)} %reduce-scatter.5.cloned.1.call-done.down_ref) | copy-start | bytes 1327108
  602.2 54.3 %collective-permute-start.2 = (bf16[72,7296]{1,0:T(8,128)(2,1)}, bf16[72,7296]{1,0:T(8,128)(2,1)S(1)}, u32[]{:S(2)}, u32[]{:S(2)}) collective-permute-start(bf16[72,7296]{1,0:T(8,128)(2,1)} %reduce-scatter.7.cloned.1.call-done.wide_ref), channel_id=1, source_target_pairs={{0,4},{4,0},{1,5},{5,1},{2,6},{6,2},{3,7},{7,3},{8,12},{12,8},{9,1... | collective-permute-start | bytes 3151880 | tf_op jit(solution)/shard_map/ppermute | solution.py:1637
  603.5 53.0 %collective-permute-start.3 = (bf16[192,1152]{1,0:T(8,128)(2,1)S(1)}, bf16[192,1152]{1,0:T(8,128)(2,1)S(1)}, u32[]{:S(2)}, u32[]{:S(2)}) collective-permute-start(bf16[192,1152]{1,0:T(8,128)(2,1)S(1)} %copy-done.3), channel_id=1, source_target_pairs={{0,4},{4,0},{1,5},{5,1},{2,6},{6,2},{3,7},{7,3},{8,12},{12,8},{9,1... | collective-permute-start | bytes 1327112 | tf_op jit(solution)/shard_map/ppermute | solution.py:1637
  656.5 0.8 copy-start.4
  656.6 1.1 copy-start.2
Sparse Core Ops, SparseCore 0:
  10.3 76.4 all-gather.4
  88.3 88.0 all-gather.2
  330.3 90.0 reduce-scatter.4
  425.1 176.8 reduce-scatter.6

commit v5 on v4

--- a/solution.py
+++ b/solution.py
@@ -1,6 +1,8 @@
 import functools
+
 import jax
 import jax.numpy as jnp
+import numpy as np
 from jax import lax
 from jax.experimental import pallas as pl
 from jax.experimental.pallas import tpu as pltpu
@@ -537,72 +539,82 @@
 ):
     step = pl.program_id(0)
     inner, total = wo_ref.shape[1], wg_ref.shape[1]
-    copies = [
-        pltpu.make_async_copy(source, target, sems.at[i])
-        for i, (source, target) in enumerate(
-            (
-                (wide_any.at[:, pl.ds(0, inner)], wo_ref),
-                (wide_any.at[:, pl.ds(inner, total)], wg_ref),
-                (wide_any.at[:, pl.ds(inner + total, total)], wu_ref),
-                (wd_any, wd_ref),
-            )
+    lows = list(range(0, total, chunk))
+
+    def loads(index):
+        low = lows[index]
+        span = pl.ds(low, chunk)
+        places = (
+            (wide_any.at[:, pl.ds(inner + low, chunk)], wg_ref.at[:, span]),
+            (wide_any.at[:, pl.ds(inner + total + low, chunk)], wu_ref.at[:, span]),
+            (wd_any.at[span], wd_ref.at[span]),
         )
-    ]
+        return [
+            pltpu.make_async_copy(source, target, sems.at[1 + 3 * index + i])
+            for i, (source, target) in enumerate(places)
+        ]
+
+    def rows(loading):
+        if loading:
+            first = pltpu.make_async_copy(wide_any.at[:, pl.ds(0, inner)], wo_ref, sems.at[0])
+            first.start()
+            for index in range(len(lows)):
+                for copy in loads(index):
+                    copy.start()
+            first.wait()
+        ob = o_ref[...]
+        x1 = x_ref[...].astype(f32) + contract(ob, wo_ref[...], 0, 0)
+        inverse = lax.rsqrt(jnp.mean(x1 * x1, axis=-1, keepdims=True) + norm_eps)
+        gain = gain_ref[1:2]
+        h2 = (x1 * inverse * gain).astype(bf16)
+        h2_ref[...] = h2
+        dy = dy_ref[...]
+        result = x1
+        dh2 = None
+        for index, low in enumerate(lows):
+            if loading:
+                for copy in loads(index):
+                    copy.wait()
+            span = slice(low, low + chunk)
+            gate = contract(h2, wg_ref[:, span], 1, 0)
+            up = contract(h2, wu_ref[:, span], 1, 0)
+            dhidden = contract(dy, wd_ref[span], 1, 1)
+            sigma = 0.5 + 0.5 * jnp.tanh(0.5 * gate)
+            silu = gate * sigma
+            hidden = (silu * up).astype(bf16)
+            hidden_ref[:, span] = hidden
+            result = result + contract(hidden, wd_ref[span], 1, 0)
+            dgate = (dhidden * up * (sigma + silu * (1.0 - sigma))).astype(bf16)
+            dup = (dhidden * silu).astype(bf16)
+            dgate_ref[:, span] = dgate
+            dup_ref[:, span] = dup
+            part = contract(dgate, wg_ref[:, span], 1, 1) + contract(dup, wu_ref[:, span], 1, 1)
+            dh2 = part if dh2 is None else dh2 + part
+        out_ref[...] = result.astype(bf16)
+        u = dh2 * gain
+        dx1 = dy.astype(f32) + inverse * u - x1 * (inverse * inverse * inverse) * jnp.mean(
+            u * x1, axis=-1, keepdims=True
+        )
+        dattn = dx1.astype(bf16)
+        dattn_ref[...] = dattn
+        dob = contract(wo_ref[...], dattn, 1, 1).astype(bf16)
+        dob_ref[...] = dob
+        product = dob.astype(f32) * ob.astype(f32)
+        heads, group = delta_ref.shape[0], delta_ref.shape[1]
+        for kv in range(heads):
+            for member in range(group):
+                at = (kv * group + member) * HEAD_WIDTH
+                delta_ref[kv, member : member + 1] = jnp.sum(
+                    product[at : at + HEAD_WIDTH], axis=0, keepdims=True
+                )
 
     @pl.when(step == 0)
     def _():
-        for copy in copies:
-            copy.start()
-        copies[0].wait()
-
-    ob = o_ref[...]
-    x1 = x_ref[...].astype(f32) + contract(ob, wo_ref[...], 0, 0)
-    inverse = lax.rsqrt(jnp.mean(x1 * x1, axis=-1, keepdims=True) + norm_eps)
-    gain = gain_ref[1:2]
-    h2 = (x1 * inverse * gain).astype(bf16)
-    h2_ref[...] = h2
-    dy = dy_ref[...]
-
-    @pl.when(step == 0)
-    def _():
-        for copy in copies[1:]:
-            copy.wait()
-
-    result = x1
-    dh2 = None
-    for low in range(0, wg_ref.shape[1], chunk):
-        span = slice(low, low + chunk)
-        gate = contract(h2, wg_ref[:, span], 1, 0)
-        up = contract(h2, wu_ref[:, span], 1, 0)
-        dhidden = contract(dy, wd_ref[span], 1, 1)
-        sigma = 0.5 + 0.5 * jnp.tanh(0.5 * gate)
-        silu = gate * sigma
-        hidden = (silu * up).astype(bf16)
-        hidden_ref[:, span] = hidden
-        result = result + contract(hidden, wd_ref[span], 1, 0)
-        dgate = (dhidden * up * sigma * (1.0 + gate * (1.0 - sigma))).astype(bf16)
-        dup = (dhidden * silu).astype(bf16)
-        dgate_ref[:, span] = dgate
-        dup_ref[:, span] = dup
-        part = contract(dgate, wg_ref[:, span], 1, 1) + contract(dup, wu_ref[:, span], 1, 1)
-        dh2 = part if dh2 is None else dh2 + part
-    out_ref[...] = result.astype(bf16)
-    u = dh2 * gain
-    dx1 = dy.astype(f32) + inverse * u - x1 * (inverse * inverse * inverse) * jnp.mean(
-        u * x1, axis=-1, keepdims=True
-    )
-    dattn = dx1.astype(bf16)
-    dattn_ref[...] = dattn
-    dob = contract(wo_ref[...], dattn, 1, 1).astype(bf16)
-    dob_ref[...] = dob
-    product = dob.astype(f32) * ob.astype(f32)
-    heads, group = delta_ref.shape[0], delta_ref.shape[1]
-    for kv in range(heads):
-        for member in range(group):
-            at = (kv * group + member) * HEAD_WIDTH
-            delta_ref[kv, member : member + 1] = jnp.sum(
-                product[at : at + HEAD_WIDTH], axis=0, keepdims=True
-            )
+        rows(True)
+
+    @pl.when(step > 0)
+    def _():
+        rows(False)
 
 
 def middle(x, dy, o, gain, wide, wd, kv_heads, tile=256, chunk=768):
@@ -629,7 +641,7 @@
             shape((q_rows, rows), bf16), shape((kv_heads, group, rows), f32),
         ),
         scratch_shapes=[pltpu.VMEM(s, bf16) for s in ((width, q_rows), (width, hidden), (width, hidden), wd.shape)]
-        + [pltpu.SemaphoreType.DMA((4,))],
+        + [pltpu.SemaphoreType.DMA((1 + 3 * (hidden // chunk),))],
         compiler_params=pltpu.CompilerParams(vmem_limit_bytes=62 * MIB),
         name="middle",
     )(x, dy, o, gain, wide, wd)
@@ -653,8 +665,15 @@
     )(dy, hidden)
 
 
-def wide_grads_kernel(o_ref, h2_ref, dgate_ref, dup_ref, dattn_ref, out_ref, *, each):
+def wide_grads_kernel(o_any, h2_ref, dgate_ref, dup_ref, dattn_ref, out_ref, o_ref, sem, *, each):
     step = pl.program_id(0)
+    copy = pltpu.make_async_copy(o_any, o_ref, sem)
+    tile = out_ref.shape[1]
+    rest = o_ref.shape[0] % tile
+
+    @pl.when(step == 0)
+    def _():
+        copy.start()
 
     @pl.when(step < each)
     def _():
@@ -664,9 +683,20 @@
     def _():
         out_ref[...] = contract(h2_ref[...], dup_ref[...], 0, 0).astype(bf16)
 
-    @pl.when(step >= 2 * each)
+    @pl.when(step == 2 * each)
+    def _():
+        copy.wait()
+
+    last = pl.num_programs(0) - 1
+
+    @pl.when((step >= 2 * each) & (step < last))
     def _():
         out_ref[...] = contract(o_ref[...], dattn_ref[...], 1, 0).astype(bf16)
+
+    @pl.when(step == last)
+    def _():
+        width = rest or tile
+        out_ref[:, :width] = contract(o_ref[...], dattn_ref[:, :width], 1, 0).astype(bf16)
 
 
 def wide_grads(o, h2, dattn, dgate, dup, tile=512):
@@ -679,10 +709,12 @@
         functools.partial(wide_grads_kernel, each=each),
         grid=(steps,),
         in_specs=[
-            resident(o.shape), resident(h2.shape), cols(0, each), cols(each, each), cols(2 * each, steps - 2 * each)
+            pl.BlockSpec(memory_space=pl.ANY), resident(h2.shape),
+            cols(0, each), cols(each, each), cols(2 * each, steps - 2 * each),
         ],
         out_specs=pl.BlockSpec((width, tile), lambda i: (0, i)),
         out_shape=jax.ShapeDtypeStruct((width, 2 * total + width), bf16),
+        scratch_shapes=[pltpu.VMEM(o.shape, bf16), pltpu.SemaphoreType.DMA],
         compiler_params=pltpu.CompilerParams(vmem_limit_bytes=60 * MIB),
         name="wide_grads",
     )(o, h2, dgate, dup, dattn)
@@ -754,7 +786,22 @@
     )(x, gains, dq, dk, dv, dkv_in, cos, sin)
 
 
-def settle_kernel(first_ref, wide_ref, wide_in_ref, down_ref, down_in_ref, gains_ref, wa_ref, wb_ref, wc_ref, wg_ref, wu_ref, *outs):
+def settle_kernel(
+    low_ref, first_ref, wide_ref, wide_in_ref, down_ref, down_in_ref, gains_ref, wa_ref, wb_ref, wc_ref, wg_ref, wu_ref,
+    tokens_ref, *outs
+):
+    tokens_ref[...] = low_ref[...].astype(f32)
+
+    @pl.when(pl.program_id(0) == 0)
+    def _():
+        settle_weights(
+            first_ref, wide_ref, wide_in_ref, down_ref, down_in_ref, gains_ref, wa_ref, wb_ref, wc_ref, wg_ref, wu_ref, *outs
+        )
+
+
+def settle_weights(
+    first_ref, wide_ref, wide_in_ref, down_ref, down_in_ref, gains_ref, wa_ref, wb_ref, wc_ref, wg_ref, wu_ref, *outs
+):
     da, db, dc, dgate, dup, dout, ddown, gain_a, gain_f = outs
     gains = gains_ref[...].astype(f32)
 
@@ -784,15 +831,23 @@
     ddown[...] = down_ref[...].astype(f32) + down_in_ref[...].astype(f32)
 
 
-def settle(first, wide, wide_in, down, down_in, gains, wa, wb, wc, wo, wg, wu):
+def settle(low, first, wide, wide_in, down, down_in, gains, wa, wb, wc, wo, wg, wu):
     rows = first.shape[0]
+    count, width = low.shape
+    tile = count // 2
     shape = jax.ShapeDtypeStruct
+    by_row = pl.BlockSpec((tile, width), lambda i: (i, 0))
+    given = (first, wide, wide_in, down, down_in, gains, wa, wb, wc, wg, wu)
+    whole = [shape(w.shape, f32) for w in (wa, wb, wc, wg, wu, wo, down)] + [shape((1, rows), f32)] * 2
     return pl.pallas_call(
         settle_kernel,
-        out_shape=[shape(w.shape, f32) for w in (wa, wb, wc, wg, wu, wo, down)] + [shape((1, rows), f32)] * 2,
+        grid=(count // tile,),
+        in_specs=[by_row] + [resident(array.shape) for array in given],
+        out_specs=[by_row] + [pl.BlockSpec(array.shape, lambda i: (0, 0)) for array in whole],
+        out_shape=[shape(low.shape, f32)] + whole,
         compiler_params=pltpu.CompilerParams(vmem_limit_bytes=60 * MIB),
         name="settle",
-    )(first, wide, wide_in, down, down_in, gains, wa, wb, wc, wg, wu)
+    )(low, *given)
 
 
 MESH_ID = pl.DeviceIdType.MESH
@@ -1012,7 +1067,7 @@
         dattn_ref[...].astype(f32)
         + inverse * u
         - tokens * (inverse * inverse * inverse) * jnp.mean(u * tokens, axis=-1, keepdims=True)
-    )
+    ).astype(bf16)
 
     @pl.when(step == steps - 1)
     def _():
@@ -1047,7 +1102,7 @@
             by_row(width), by_row(width),
         ],
         out_specs=(pl.BlockSpec((rows, columns), lambda i: (0, 0)), by_row(width)),
-        out_shape=(jax.ShapeDtypeStruct((rows, columns), f32), jax.ShapeDtypeStruct((count, width), f32)),
+        out_shape=(jax.ShapeDtypeStruct((rows, columns), f32), jax.ShapeDtypeStruct((count, width), bf16)),
         scratch_shapes=[
             buffer(2 * depth),
             buffer(2 * depth),
@@ -1667,7 +1722,7 @@
         at < prompt_rows, block * prompt_rows + at, prompt_total + (at - prompt_rows) % CONTINUE_LENGTH
     )
     half = HEAD_WIDTH // 2
-    frequency = rope_base ** (-(jnp.arange(half, dtype=f32) * 2.0) / HEAD_WIDTH)
+    frequency = (rope_base ** (-(np.arange(half) * 2.0) / HEAD_WIDTH)).astype(np.float32)
     angles = frequency[:, None] * positions.astype(f32)[None, :]
     cos, sin = jnp.cos(angles), jnp.sin(angles)
 
@@ -1691,9 +1746,9 @@
     lin, d_first = last_grads(x, gains, dq, dk, dv, dkv_in, cos, sin)
     d_first, d_wide = lax.optimization_barrier((d_first, d_wide))
     d_wide_in = swap(d_wide)
-    d_first, grad_tokens = reduce_all(d_first.reshape(4 * depth, shard_rows, -1), lin, first, gains, x, dattn, depth)
-    d_q, d_k, d_v, d_gate, d_up, d_out, d_down, d_gain_a, d_gain_f = settle(
-        d_first, d_wide, d_wide_in, d_down, d_down_in, gain_columns,
+    d_first, low_tokens = reduce_all(d_first.reshape(4 * depth, shard_rows, -1), lin, first, gains, x, dattn, depth)
+    grad_tokens, d_q, d_k, d_v, d_gate, d_up, d_out, d_down, d_gain_a, d_gain_f = settle(
+        low_tokens, d_first, d_wide, d_wide_in, d_down, d_down_in, gain_columns,
         query_weight, key_matrix, value_matrix, output_weight, gate_weight, up_weight,
     )
     return (

time: 681 us -> 674 us (0.990)
  local copies, waits for them, and re-layouts: 12.1 us -> 4.14 us
    unnamed x11 -> x10, local copies, waits for them, and re-layouts: 11.4 us -> 3.41 us
  transfers between devices with their start and end apart: 8 -> 8, of which waited for: 1 -> 2; matrix products, arithmetic and copies ran while one was open for 1% -> 1% of each run, Pallas kernels for 66% -> 67%
where the time goes in v5:
time: 674 us; the launch traced here: 671 us
  Pallas kernels  605 us (90%)
  starting transfers between devices  29.8 us (4%)
  between operations  15.5 us (2%)
  waiting for transfers between devices  11.3 us (2%)
    pallas_call x1, Pallas kernels, middle(): pl.pallas_call(functools.partial(middle_kernel, chunk=chunk), grid=(rows...  129 us
    pallas_call x1, Pallas kernels, own_backward(): pl.pallas_call(functools.partial(own_backward_kernel, group=group, prompt...  103 us
    pallas_call x1, Pallas kernels, other_backward(): pl.pallas_call(functools.partial(other_backward_kernel, group=group, prom...  71.3 us
    pallas_call x1, Pallas kernels, reduce_all(): pl.pallas_call(functools.partial(reduce_kernel, depth=depth), grid=(count...  52.2 us
    pallas_call x1, Pallas kernels, own_forward(): pl.pallas_call(functools.partial(own_forward_kernel, group=group, prompt_...  51.8 us
    pallas_call x1, Pallas kernels, wide_grads(): pl.pallas_call(functools.partial(wide_grads_kernel, each=each), grid=(ste...  45 us
    pallas_call x1, Pallas kernels, gather_all(): pl.pallas_call(functools.partial(gather_kernel, depth=depth, split=split)...  44.7 us
    pallas_call x1, Pallas kernels, other_forward(): pl.pallas_call(functools.partial(other_forward_kernel, group=group, promp...  36.2 us
  transfers between devices with their start and end apart: 8, of which 2 were waited for; matrix products, arithmetic and copies ran while one was open for 1% of the time, Pallas kernels for 67%

profile of v5, /device:TPU:8, one launch (start us, length us, event | category | flops | bytes accessed | tf_op | source)
XLA Modules:
  0.0 670.5 jit_solution(1857239975664531840)
XLA Ops:
  7.2 0.0 all-gather.5.cloned.1.call-start
  7.2 0.7 all-gather.5.cloned.1.call-update
  7.9 0.0 all-gather.3.cloned.1.call-start
  8.0 0.7 pad_maximum_fusion
  8.6 0.1 copy.26
  8.8 0.6 pad.4.refs_3_.gains_ref
  9.4 44.7 %gather_all.1 = (bf16[16,72,2048]{2,1,0:T(8,128)(2,1)}, bf16[72,7296]{1,0:T(8,128)(2,1)}) custom-call(bf16[72,1152]{1,0:T(8,128)(2,1)} %wa_ref.1, bf16[72,384]{1,0:T(8,128)(2,1)} %wb_ref.1, bf16[72,384]{1,0:T(8,128)(2,1)} %wc_ref.1, bf16[72,128]{1,0:T(8,128)(2,1)} %pad.4.refs_3_.gains_ref, bf16[72,1152]{1,0:T(8,128)(2,1)} %refs_4_.1, ...), custom_call_target="tpu_custom_call" | custom-call | tf_op jit(solution)/shard_map/gather_all/pallas_call | solution.py:974
  54.1 0.0 reduce-scatter.5.cloned.1.call-start
  54.2 1.2 fusion.7
  56.1 2.5 multiply_sine_fusion
  58.6 20.2 %project.1 = (bf16[1152,2048]{1,0:T(8,128)(2,1)}, bf16[384,2048]{1,0:T(8,128)(2,1)}, bf16[384,2048]{1,0:T(8,128)(2,1)}, bf16[2,384,1024]{2,1,0:T(8,128)(2,1)}, f...) custom-call(bf16[2048,1152]{1,0:T(8,128)(2,1)} %bitcast.13, bf16[1152,2048]{1,0:T(8,128)(2,1)} %bitcast.19, ...), custom_call_target="tpu_custom_call" | custom-call | tf_op jit(solution)/shard_map/project/pallas_call | solution.py:87
  78.8 0.3 collective-permute-start
  79.7 51.8 %own_forward.1 = (f32[1440,2048]{1,0:T(8,128)}, f32[6,3,2048]{2,1,0:T(4,128)}, bf16[18,2048,1024]{2,1,0:T(8,128)(2,1)}) custom-call(bf16[1152,2048]{1,0:T(8,128)(2,1)} %get-tuple-element.63.q_ref, bf16[384,2048]{1,0:T(8,128)(2,1)} %get-tuple-element.66.k_ref, bf16[384,2048]{1,0:T(8,128)(2,1)} %get-tuple-element.67.v_ref, ...), custom_call_target="tpu_custom_call" | custom-call | tf_op jit(solution)/shard_map/own_forward/pallas_call | solution.py:231
  131.5 1.2 copy-done
  132.7 36.2 %other_forward.1 = (bf16[1152,2048]{1,0:T(8,128)(2,1)}, f32[6,3,2048]{2,1,0:T(4,128)}, f32[6,3,2048]{2,1,0:T(4,128)}, bf16[18,1024,2048]{2,1,0:T(8,128)(2,1)}) custom-call(s32[1]{0:T(128)} %bitcast.2.seen_ref, bf16[1152,2048]{1,0:T(8,128)(2,1)} %get-tuple-element.63.q_ref, bf16[2,384,1024]{2,1,0:T(8,128)(2,1)} %copy-done, bf16[2,384,1024]{2,1,0:T(8,128)(2,1)} %copy-done, ...), custom_call_target="tpu_custom_call" | custom-call | tf_op jit(solution)/shard_map/other_forward/pallas_call | solution.py:328
  168.9 7.4 %all-gather.3.cloned.1.call-done.wide_any = bf16[1152,7296]{1,0:T(8,128)(2,1)} async-done(((bf16[72,7296]{1,0:T(8,128)(2,1)}), bf16[1152,7296]{1,0:T(8,128)(2,1)}) %all-gather.3.cloned.1.call-update) | async-done | bytes 16810000 | tf_op jit(solution)/shard_map/all_gather | solution.py:1718
  176.3 128.9 %middle.1 = (bf16[2048,1152]{1,0:T(8,128)(2,1)}, bf16[2048,1152]{1,0:T(8,128)(2,1)}, bf16[2048,3072]{1,0:T(8,128)(2,1)}, bf16[2048,3072]{1,0:T(8,128)(2,1)}, bf1...) custom-call(bf16[2048,1152]{1,0:T(8,128)(2,1)} %bitcast.14, ...), custom_call_target="tpu_custom_call" | custom-call | tf_op jit(solution)/shard_map/middle/pallas_call | solution.py:628
  305.2 21.5 %down_grads.1 = bf16[3072,1152]{1,0:T(8,128)(2,1)} custom-call(bf16[2048,1152]{1,0:T(8,128)(2,1)} %bitcast.18, bf16[2048,3072]{1,0:T(8,128)(2,1)} %get-tuple-element.77.hidden_ref), custom_call_target="tpu_custom_call" | custom-call | tf_op jit(solution)/shard_map/down_grads/pallas_call | solution.py:657
  326.8 0.0 reduce-scatter.7.cloned.1.call-start
  326.8 45.0 %wide_grads.1 = bf16[1152,7296]{1,0:T(8,128)(2,1)} custom-call(bf16[1152,2048]{1,0:T(8,128)(2,1)} %get-tuple-element.71.o_ref.o_any, bf16[2048,1152]{1,0:T(8,128)(2,1)} %get-tuple-element.78.h2_ref, bf16[2048,3072]{1,0:T(8,128)(2,1)} %get-tuple-element.79.dgate_ref, bf16[2048,3072]{1,0:T(8,128)(2,1)} %get-tuple-element.80.dup_ref, ...), custom_call_target="tpu_custom_call" | custom-call | tf_op jit(solution)/shard_map/wide_grads/pallas_call | solution.py:708
  371.9 71.3 %other_backward.1 = (bf16[1152,2048]{1,0:T(8,128)(2,1)}, bf16[2,384,1024]{2,1,0:T(8,128)(2,1)}) custom-call(s32[1]{0:T(128)} %bitcast.2.seen_ref, bf16[1152,2048]{1,0:T(8,128)(2,1)} %get-tuple-element.63.q_ref, bf16[1152,2048]{1,0:T(8,128)(2,1)} %get-tuple-element.82.g_ref, f32[6,3,2048]{2,1,0:T(4,128)} %get-tuple-element.86.scale_ref, ...), custom_call_target="tpu_custom_call" | custom-call | tf_op jit(solution)/shard_map/other_backward/pallas_call | solution.py:439
  443.1 27.3 %collective-permute-start.1 = (bf16[2,384,1024]{2,1,0:T(8,128)(2,1)}, bf16[2,384,1024]{2,1,0:T(8,128)(2,1)S(1)}, u32[]{:S(2)}, u32[]{:S(2)}) collective-permute-start(bf16[2,384,1024]{2,1,0:T(8,128)(2,1)} %get-tuple-element.93), channel_id=1, source_target_pairs={{0,4},{4,0},{1,5},{5,1},{2,6},{6,2},{3,7},{7,3},{8,12},{12,8},{9,1... | collective-permute-start | bytes 4718600 | tf_op jit(solution)/shard_map/ppermute | solution.py:1692
  470.4 102.7 %own_backward.1 = (bf16[1152,2048]{1,0:T(8,128)(2,1)}, bf16[384,2048]{1,0:T(8,128)(2,1)}, bf16[384,2048]{1,0:T(8,128)(2,1)}) custom-call(bf16[1152,2048]{1,0:T(8,128)(2,1)} %get-tuple-element.63.q_ref, bf16[1152,2048]{1,0:T(8,128)(2,1)} %get-tuple-element.82.g_ref, f32[6,3,2048]{2,1,0:T(4,128)} %get-tuple-element.83.scale_ref, ...), custom_call_target="tpu_custom_call" | custom-call | tf_op jit(solution)/shard_map/own_backward/pallas_call | solution.py:513
  573.2 1.1 copy-done.1
  574.3 22.2 %last_grads.1 = (bf16[2048,1920]{1,0:T(8,128)(2,1)}, bf16[1152,1920]{1,0:T(8,128)(2,1)}) custom-call(bf16[2048,1152]{1,0:T(8,128)(2,1)} %bitcast.15, f32[8,1152]{1,0:T(8,128)} %get-tuple-element.72.gain_ref, bf16[1152,2048]{1,0:T(8,128)(2,1)} %get-tuple-element.89.dq_ref, bf16[384,2048]{1,0:T(8,128)(2,1)} %get-tuple-element.90.dk_ref, ...), custom_call_target="tpu_custom_call" | custom-call | tf_op jit(solution)/shard_map/last_grads/pallas_call | solution.py:775
  596.5 3.1 reduce-scatter.7.cloned.1.call-done.wide_ref
  599.6 1.5 collective-permute-start.2
  601.0 0.6 collective-permute-start.3
  601.6 52.2 %reduce_all.1 = (f32[72,1920]{1,0:T(8,128)}, bf16[2048,1152]{1,0:T(8,128)(2,1)}) custom-call(bf16[16,72,1920]{2,1,0:T(8,128)(2,1)} %bitcast.21, bf16[2048,1920]{1,0:T(8,128)(2,1)} %get-tuple-element.98.lin_ref, bf16[1152,2048]{1,0:T(8,128)(2,1)} %bitcast.20, f32[8,1152]{1,0:T(8,128)} %get-tuple-element.72.gain_ref, bf16[2048,1152]{1,0:T(8,128)(2,1)} %bitcast.16, ...), custom_call_target="tpu_custom_call" | custom-call | tf_op jit(solution)/shard_map/reduce_all/pallas_call | solution.py:1097
  653.8 0.7 copy-done.4
  654.5 0.4 copy-done.2
  654.9 8.8 %settle.1 = (f32[2048,1152]{1,0:T(8,128)}, f32[72,1152]{1,0:T(8,128)}, f32[72,384]{1,0:T(8,128)}, f32[72,384]{1,0:T(8,128)}, f32[72,3072]{1,0:T(8,128)}, /*index...) custom-call(bf16[2048,1152]{1,0:T(8,128)(2,1)} %get-tuple-element.99.low_ref, ...), custom_call_target="tpu_custom_call" | custom-call | tf_op jit(solution)/shard_map/settle/pallas_call | solution.py:842
  (16 shorter events, 0.1 us)
Async XLA Ops:
  7.2 161.7 %all-gather.5.cloned.1.call-start = ((), (), s32[]{:S(2)}) async-start(), calls=%async_computation.3 | async-start | bytes 7520256 | tf_op jit(solution)/shard_map/all_gather | solution.py:1715
  7.9 168.4 %all-gather.3.cloned.1.call-start = ((), (), s32[]{:S(2)}) async-start(), calls=%async_computation.2 | async-start | bytes 17860608 | tf_op jit(solution)/shard_map/all_gather | solution.py:1718
  54.1 519.0 %reduce-scatter.5.cloned.1.call-start = ((), (), s32[]{:S(2)}) async-start(), calls=%async_computation.4 | async-start | bytes 7520256 | tf_op jit(solution)/shard_map/reduce_scatter | solution.py:1734
  78.8 52.7 %collective-permute-start = (bf16[2,384,1024]{2,1,0:T(8,128)(2,1)}, bf16[2,384,1024]{2,1,0:T(8,128)(2,1)S(1)}, u32[]{:S(2)}, u32[]{:S(2)}) collective-permute-start(bf16[2,384,1024]{2,1,0:T(8,128)(2,1)} %get-tuple-element.64), channel_id=1, source_target_pairs={{0,4},{4,0},{1,5},{5,1},{2,6},{6,2},{3,7},{7,3},{8,12},{12,8},{9,1... | collective-permute-start | bytes 4718600 | tf_op jit(solution)/shard_map/ppermute | solution.py:1692
  131.5 1.2 copy-start
  326.8 272.8 %reduce-scatter.7.cloned.1.call-start = ((), (), s32[]{:S(2)}) async-start(), calls=%async_computation.5 | async-start | bytes 17860608
  443.1 130.0 %collective-permute-start.1 = (bf16[2,384,1024]{2,1,0:T(8,128)(2,1)}, bf16[2,384,1024]{2,1,0:T(8,128)(2,1)S(1)}, u32[]{:S(2)}, u32[]{:S(2)}) collective-permute-start(bf16[2,384,1024]{2,1,0:T(8,128)(2,1)} %get-tuple-element.93), channel_id=1, source_target_pairs={{0,4},{4,0},{1,5},{5,1},{2,6},{6,2},{3,7},{7,3},{8,12},{12,8},{9,1... | collective-permute-start | bytes 4718600 | tf_op jit(solution)/shard_map/ppermute | solution.py:1692
  573.1 1.2 copy-start.1
  574.3 26.7 %copy-start.3 = (bf16[192,1152]{1,0:T(8,128)(2,1)S(1)}, bf16[192,1152]{1,0:T(8,128)(2,1)}, u32[]{:S(2)}) copy-start(bf16[192,1152]{1,0:T(8,128)(2,1)} %reduce-scatter.5.cloned.1.call-done.down_ref) | copy-start | bytes 1327108
  599.6 54.2 %collective-permute-start.2 = (bf16[72,7296]{1,0:T(8,128)(2,1)}, bf16[72,7296]{1,0:T(8,128)(2,1)S(1)}, u32[]{:S(2)}, u32[]{:S(2)}) collective-permute-start(bf16[72,7296]{1,0:T(8,128)(2,1)} %reduce-scatter.7.cloned.1.call-done.wide_ref), channel_id=1, source_target_pairs={{0,4},{4,0},{1,5},{5,1},{2,6},{6,2},{3,7},{7,3},{8,12},{12,8},{9,1... | collective-permute-start | bytes 3151880 | tf_op jit(solution)/shard_map/ppermute | solution.py:1692
  601.0 52.8 %collective-permute-start.3 = (bf16[192,1152]{1,0:T(8,128)(2,1)S(1)}, bf16[192,1152]{1,0:T(8,128)(2,1)S(1)}, u32[]{:S(2)}, u32[]{:S(2)}) collective-permute-start(bf16[192,1152]{1,0:T(8,128)(2,1)S(1)} %copy-done.3), channel_id=1, source_target_pairs={{0,4},{4,0},{1,5},{5,1},{2,6},{6,2},{3,7},{7,3},{8,12},{12,8},{9,1... | collective-permute-start | bytes 1327112 | tf_op jit(solution)/shard_map/ppermute | solution.py:1692
  653.8 0.8 copy-start.4
  653.8 1.1 copy-start.2
Sparse Core Ops, SparseCore 0:
  10.3 76.4 all-gather.4
  88.3 87.8 all-gather.2
  326.9 90.9 reduce-scatter.4
  422.7 176.8 reduce-scatter.6

commit v6 on v5

--- a/solution.py
+++ b/solution.py
@@ -992,8 +992,9 @@
 
 
 def reduce_kernel(
-    part_ref, lin_ref, w_ref, gain_ref, x_ref, dattn_ref, out_ref, tokens_ref,
-    core_ref, sum_ref, over_ref, line_ref, z_ref, last_ref, twin_ref, send_sems, recv_sems, *, depth
+    part_any, lin_ref, w_any, gain_ref, x_ref, dattn_ref, out_ref, tokens_ref,
+    mine_ref, w_ref, core_ref, sum_ref, over_ref, line_ref, z_ref, last_ref, twin_ref, send_sems, recv_sems, local_sems,
+    *, depth
 ):
     step = pl.program_id(0)
     steps = pl.num_programs(0)
@@ -1016,7 +1017,14 @@
 
     def to_core(at):
         to_z, to_x = place(*order[at])
-        return remote(part_ref.at[slot_at(to_z, to_x, 1 - core)], core_ref.at[at], over_core, at)
+        return remote(part_any.at[slot_at(to_z, to_x, 1 - core)], core_ref.at[at], over_core, at)
+
+    def own(at):
+        own_z, own_x = place(*order[at])
+        return pltpu.make_async_copy(part_any.at[slot_at(own_z, own_x, core)], mine_ref.at[at], local_sems.at[at])
+
+    def weights():
+        return pltpu.make_async_copy(w_any.at[:, pl.ds(0, w_ref.shape[1])], w_ref, local_sems.at[2 * depth])
 
     def to_x(at):
         return remote(sum_ref.at[at], over_ref.at[at], over_x, 2 * depth + at)
@@ -1028,15 +1036,19 @@
         return remote(last_ref, twin_ref, over_y, 4 * depth - 1)
 
     def core_sums(at):
+        own(at).wait()
         to_core(at).wait_recv()
-        own_z, own_x = place(*order[at])
-        sum_ref[at] = (part_ref[slot_at(own_z, own_x, core)].astype(f32) + core_ref[at].astype(f32)).astype(bf16)
+        sum_ref[at] = (mine_ref[at].astype(f32) + core_ref[at].astype(f32)).astype(bf16)
 
     @pl.when(step == 0)
     def _():
         greet(along + [over_x, over_y, over_core])
         for at in range(2 * depth):
             to_core(at).start()
+        for at in range(2 * depth):
+            own(at).start()
+        weights().start()
+        weights().wait()
 
     @pl.when(step == 1)
     def _():
@@ -1059,7 +1071,7 @@
                 to_z(at).start()
 
     lin = lin_ref[...]
-    dh = contract(lin, w_ref[:, : lin.shape[1]], 1, 1)
+    dh = contract(lin, w_ref[...], 1, 1)
     tokens = x_ref[...].astype(f32)
     inverse = lax.rsqrt(jnp.mean(tokens * tokens, axis=-1, keepdims=True) + norm_eps)
     u = dh * gain_ref[0:1]
@@ -1098,12 +1110,15 @@
         functools.partial(reduce_kernel, depth=depth),
         grid=(count // tile,),
         in_specs=[
-            resident(parts.shape), by_row(lin.shape[1]), resident(w.shape), resident(gains.shape),
+            pl.BlockSpec(memory_space=pl.ANY), by_row(lin.shape[1]), pl.BlockSpec(memory_space=pl.ANY),
+            resident(gains.shape),
             by_row(width), by_row(width),
         ],
         out_specs=(pl.BlockSpec((rows, columns), lambda i: (0, 0)), by_row(width)),
         out_shape=(jax.ShapeDtypeStruct((rows, columns), f32), jax.ShapeDtypeStruct((count, width), bf16)),
         scratch_shapes=[
+            buffer(2 * depth),
+            pltpu.VMEM((width, columns), bf16),
             buffer(2 * depth),
             buffer(2 * depth),
             buffer(depth),
@@ -1113,6 +1128,7 @@
             buffer(),
             pltpu.SemaphoreType.DMA((sems,)),
             pltpu.SemaphoreType.DMA((sems,)),
+            pltpu.SemaphoreType.DMA((2 * depth + 1,)),
         ],
         compiler_params=pltpu.CompilerParams(
             collective_id=2, has_side_effects=True, vmem_limit_bytes=60 * MIB

time: 674 us -> 674 us (level)
  no operation moved by 1% of the time
where the time goes in v6:
time: 674 us; the launch traced here: 671 us
  Pallas kernels  606 us (90%)
  starting transfers between devices  29.8 us (4%)
  between operations  15.5 us (2%)
  waiting for transfers between devices  11.2 us (2%)
    pallas_call x1, Pallas kernels, middle(): pl.pallas_call(functools.partial(middle_kernel, chunk=chunk), grid=(rows...  129 us
    pallas_call x1, Pallas kernels, own_backward(): pl.pallas_call(functools.partial(own_backward_kernel, group=group, prompt...  103 us
    pallas_call x1, Pallas kernels, other_backward(): pl.pallas_call(functools.partial(other_backward_kernel, group=group, prom...  71.3 us
    pallas_call x1, Pallas kernels, reduce_all(): pl.pallas_call(functools.partial(reduce_kernel, depth=depth), grid=(count...  52.4 us
    pallas_call x1, Pallas kernels, own_forward(): pl.pallas_call(functools.partial(own_forward_kernel, group=group, prompt_...  51.8 us
    pallas_call x1, Pallas kernels, wide_grads(): pl.pallas_call(functools.partial(wide_grads_kernel, each=each), grid=(ste...  45 us
    pallas_call x1, Pallas kernels, gather_all(): pl.pallas_call(functools.partial(gather_kernel, depth=depth, split=split)...  44.7 us
    pallas_call x1, Pallas kernels, other_forward(): pl.pallas_call(functools.partial(other_forward_kernel, group=group, promp...  36.2 us
  transfers between devices with their start and end apart: 8, of which 2 were waited for; matrix products, arithmetic and copies ran while one was open for 1% of the time, Pallas kernels for 67%

profile of v6, /device:TPU:8, one launch (start us, length us, event | category | flops | bytes accessed | tf_op | source)
XLA Modules:
  0.0 670.7 jit_solution(332391195318969792)
XLA Ops:
  7.2 0.0 all-gather.5.cloned.1.call-start
  7.2 0.7 all-gather.5.cloned.1.call-update
  7.9 0.0 all-gather.3.cloned.1.call-start
  8.0 0.7 pad_maximum_fusion
  8.6 0.1 copy.26
  8.8 0.6 pad.4.refs_3_.gains_ref
  9.4 44.7 %gather_all.1 = (bf16[16,72,2048]{2,1,0:T(8,128)(2,1)}, bf16[72,7296]{1,0:T(8,128)(2,1)}) custom-call(bf16[72,1152]{1,0:T(8,128)(2,1)} %wa_ref.1, bf16[72,384]{1,0:T(8,128)(2,1)} %wb_ref.1, bf16[72,384]{1,0:T(8,128)(2,1)} %wc_ref.1, bf16[72,128]{1,0:T(8,128)(2,1)} %pad.4.refs_3_.gains_ref, bf16[72,1152]{1,0:T(8,128)(2,1)} %refs_4_.1, ...), custom_call_target="tpu_custom_call" | custom-call | tf_op jit(solution)/shard_map/gather_all/pallas_call | solution.py:974
  54.1 0.0 reduce-scatter.5.cloned.1.call-start
  54.2 1.2 fusion.7
  56.1 2.5 multiply_sine_fusion
  58.6 20.2 %project.1 = (bf16[1152,2048]{1,0:T(8,128)(2,1)}, bf16[384,2048]{1,0:T(8,128)(2,1)}, bf16[384,2048]{1,0:T(8,128)(2,1)}, bf16[2,384,1024]{2,1,0:T(8,128)(2,1)}, f...) custom-call(bf16[2048,1152]{1,0:T(8,128)(2,1)} %bitcast.13, bf16[1152,2048]{1,0:T(8,128)(2,1)} %bitcast.19, ...), custom_call_target="tpu_custom_call" | custom-call | tf_op jit(solution)/shard_map/project/pallas_call | solution.py:87
  78.8 0.3 collective-permute-start
  79.7 51.8 %own_forward.1 = (f32[1440,2048]{1,0:T(8,128)}, f32[6,3,2048]{2,1,0:T(4,128)}, bf16[18,2048,1024]{2,1,0:T(8,128)(2,1)}) custom-call(bf16[1152,2048]{1,0:T(8,128)(2,1)} %get-tuple-element.63.q_ref, bf16[384,2048]{1,0:T(8,128)(2,1)} %get-tuple-element.66.k_ref, bf16[384,2048]{1,0:T(8,128)(2,1)} %get-tuple-element.67.v_ref, ...), custom_call_target="tpu_custom_call" | custom-call | tf_op jit(solution)/shard_map/own_forward/pallas_call | solution.py:231
  131.5 1.2 copy-done
  132.7 36.2 %other_forward.1 = (bf16[1152,2048]{1,0:T(8,128)(2,1)}, f32[6,3,2048]{2,1,0:T(4,128)}, f32[6,3,2048]{2,1,0:T(4,128)}, bf16[18,1024,2048]{2,1,0:T(8,128)(2,1)}) custom-call(s32[1]{0:T(128)} %bitcast.2.seen_ref, bf16[1152,2048]{1,0:T(8,128)(2,1)} %get-tuple-element.63.q_ref, bf16[2,384,1024]{2,1,0:T(8,128)(2,1)} %copy-done, bf16[2,384,1024]{2,1,0:T(8,128)(2,1)} %copy-done, ...), custom_call_target="tpu_custom_call" | custom-call | tf_op jit(solution)/shard_map/other_forward/pallas_call | solution.py:328
  168.9 7.4 %all-gather.3.cloned.1.call-done.wide_any = bf16[1152,7296]{1,0:T(8,128)(2,1)} async-done(((bf16[72,7296]{1,0:T(8,128)(2,1)}), bf16[1152,7296]{1,0:T(8,128)(2,1)}) %all-gather.3.cloned.1.call-update) | async-done | bytes 16810000 | tf_op jit(solution)/shard_map/all_gather | solution.py:1734
  176.3 128.9 %middle.1 = (bf16[2048,1152]{1,0:T(8,128)(2,1)}, bf16[2048,1152]{1,0:T(8,128)(2,1)}, bf16[2048,3072]{1,0:T(8,128)(2,1)}, bf16[2048,3072]{1,0:T(8,128)(2,1)}, bf1...) custom-call(bf16[2048,1152]{1,0:T(8,128)(2,1)} %bitcast.14, ...), custom_call_target="tpu_custom_call" | custom-call | tf_op jit(solution)/shard_map/middle/pallas_call | solution.py:628
  305.2 21.5 %down_grads.1 = bf16[3072,1152]{1,0:T(8,128)(2,1)} custom-call(bf16[2048,1152]{1,0:T(8,128)(2,1)} %bitcast.18, bf16[2048,3072]{1,0:T(8,128)(2,1)} %get-tuple-element.77.hidden_ref), custom_call_target="tpu_custom_call" | custom-call | tf_op jit(solution)/shard_map/down_grads/pallas_call | solution.py:657
  326.8 0.0 reduce-scatter.7.cloned.1.call-start
  326.8 45.0 %wide_grads.1 = bf16[1152,7296]{1,0:T(8,128)(2,1)} custom-call(bf16[1152,2048]{1,0:T(8,128)(2,1)} %get-tuple-element.71.o_ref.o_any, bf16[2048,1152]{1,0:T(8,128)(2,1)} %get-tuple-element.78.h2_ref, bf16[2048,3072]{1,0:T(8,128)(2,1)} %get-tuple-element.79.dgate_ref, bf16[2048,3072]{1,0:T(8,128)(2,1)} %get-tuple-element.80.dup_ref, ...), custom_call_target="tpu_custom_call" | custom-call | tf_op jit(solution)/shard_map/wide_grads/pallas_call | solution.py:708
  371.9 71.3 %other_backward.1 = (bf16[1152,2048]{1,0:T(8,128)(2,1)}, bf16[2,384,1024]{2,1,0:T(8,128)(2,1)}) custom-call(s32[1]{0:T(128)} %bitcast.2.seen_ref, bf16[1152,2048]{1,0:T(8,128)(2,1)} %get-tuple-element.63.q_ref, bf16[1152,2048]{1,0:T(8,128)(2,1)} %get-tuple-element.82.g_ref, f32[6,3,2048]{2,1,0:T(4,128)} %get-tuple-element.86.scale_ref, ...), custom_call_target="tpu_custom_call" | custom-call | tf_op jit(solution)/shard_map/other_backward/pallas_call | solution.py:439
  443.1 27.3 %collective-permute-start.1 = (bf16[2,384,1024]{2,1,0:T(8,128)(2,1)}, bf16[2,384,1024]{2,1,0:T(8,128)(2,1)S(1)}, u32[]{:S(2)}, u32[]{:S(2)}) collective-permute-start(bf16[2,384,1024]{2,1,0:T(8,128)(2,1)} %get-tuple-element.93), channel_id=1, source_target_pairs={{0,4},{4,0},{1,5},{5,1},{2,6},{6,2},{3,7},{7,3},{8,12},{12,8},{9,1... | collective-permute-start | bytes 4718600 | tf_op jit(solution)/shard_map/ppermute | solution.py:1708
  470.4 102.7 %own_backward.1 = (bf16[1152,2048]{1,0:T(8,128)(2,1)}, bf16[384,2048]{1,0:T(8,128)(2,1)}, bf16[384,2048]{1,0:T(8,128)(2,1)}) custom-call(bf16[1152,2048]{1,0:T(8,128)(2,1)} %get-tuple-element.63.q_ref, bf16[1152,2048]{1,0:T(8,128)(2,1)} %get-tuple-element.82.g_ref, f32[6,3,2048]{2,1,0:T(4,128)} %get-tuple-element.83.scale_ref, ...), custom_call_target="tpu_custom_call" | custom-call | tf_op jit(solution)/shard_map/own_backward/pallas_call | solution.py:513
  573.2 1.1 copy-done.1
  574.3 22.2 %last_grads.1 = (bf16[2048,1920]{1,0:T(8,128)(2,1)}, bf16[1152,1920]{1,0:T(8,128)(2,1)}) custom-call(bf16[2048,1152]{1,0:T(8,128)(2,1)} %bitcast.15, f32[8,1152]{1,0:T(8,128)} %get-tuple-element.72.gain_ref, bf16[1152,2048]{1,0:T(8,128)(2,1)} %get-tuple-element.89.dq_ref, bf16[384,2048]{1,0:T(8,128)(2,1)} %get-tuple-element.90.dk_ref, ...), custom_call_target="tpu_custom_call" | custom-call | tf_op jit(solution)/shard_map/last_grads/pallas_call | solution.py:775
  596.5 3.0 reduce-scatter.7.cloned.1.call-done.wide_ref
  599.5 1.5 collective-permute-start.2
  601.0 0.6 collective-permute-start.3
  601.5 52.4 %reduce_all.1 = (f32[72,1920]{1,0:T(8,128)}, bf16[2048,1152]{1,0:T(8,128)(2,1)}) custom-call(bf16[16,72,1920]{2,1,0:T(8,128)(2,1)} %bitcast.21, bf16[2048,1920]{1,0:T(8,128)(2,1)} %get-tuple-element.98.lin_ref, bf16[1152,2048]{1,0:T(8,128)(2,1)} %bitcast.20, f32[8,1152]{1,0:T(8,128)} %get-tuple-element.72.gain_ref, bf16[2048,1152]{1,0:T(8,128)(2,1)} %bitcast.16, ...), custom_call_target="tpu_custom_call" | custom-call | tf_op jit(solution)/shard_map/reduce_all/pallas_call | solution.py:1109
  654.0 0.7 copy-done.4
  654.7 0.4 copy-done.2
  655.1 8.8 %settle.1 = (f32[2048,1152]{1,0:T(8,128)}, f32[72,1152]{1,0:T(8,128)}, f32[72,384]{1,0:T(8,128)}, f32[72,384]{1,0:T(8,128)}, f32[72,3072]{1,0:T(8,128)}, /*index...) custom-call(bf16[2048,1152]{1,0:T(8,128)(2,1)} %get-tuple-element.99.low_ref, ...), custom_call_target="tpu_custom_call" | custom-call | tf_op jit(solution)/shard_map/settle/pallas_call | solution.py:842
  (16 shorter events, 0.1 us)
Async XLA Ops:
  7.2 161.7 %all-gather.5.cloned.1.call-start = ((), (), s32[]{:S(2)}) async-start(), calls=%async_computation.3 | async-start | bytes 7520256 | tf_op jit(solution)/shard_map/all_gather | solution.py:1731
  7.9 168.4 %all-gather.3.cloned.1.call-start = ((), (), s32[]{:S(2)}) async-start(), calls=%async_computation.2 | async-start | bytes 17860608 | tf_op jit(solution)/shard_map/all_gather | solution.py:1734
  54.1 519.0 %reduce-scatter.5.cloned.1.call-start = ((), (), s32[]{:S(2)}) async-start(), calls=%async_computation.4 | async-start | bytes 7520256 | tf_op jit(solution)/shard_map/reduce_scatter | solution.py:1750
  78.8 52.7 %collective-permute-start = (bf16[2,384,1024]{2,1,0:T(8,128)(2,1)}, bf16[2,384,1024]{2,1,0:T(8,128)(2,1)S(1)}, u32[]{:S(2)}, u32[]{:S(2)}) collective-permute-start(bf16[2,384,1024]{2,1,0:T(8,128)(2,1)} %get-tuple-element.64), channel_id=1, source_target_pairs={{0,4},{4,0},{1,5},{5,1},{2,6},{6,2},{3,7},{7,3},{8,12},{12,8},{9,1... | collective-permute-start | bytes 4718600 | tf_op jit(solution)/shard_map/ppermute | solution.py:1708
  131.5 1.2 copy-start
  326.8 272.7 %reduce-scatter.7.cloned.1.call-start = ((), (), s32[]{:S(2)}) async-start(), calls=%async_computation.5 | async-start | bytes 17860608
  443.1 130.0 %collective-permute-start.1 = (bf16[2,384,1024]{2,1,0:T(8,128)(2,1)}, bf16[2,384,1024]{2,1,0:T(8,128)(2,1)S(1)}, u32[]{:S(2)}, u32[]{:S(2)}) collective-permute-start(bf16[2,384,1024]{2,1,0:T(8,128)(2,1)} %get-tuple-element.93), channel_id=1, source_target_pairs={{0,4},{4,0},{1,5},{5,1},{2,6},{6,2},{3,7},{7,3},{8,12},{12,8},{9,1... | collective-permute-start | bytes 4718600 | tf_op jit(solution)/shard_map/ppermute | solution.py:1708
  573.1 1.2 copy-start.1
  574.3 26.7 %copy-start.3 = (bf16[192,1152]{1,0:T(8,128)(2,1)S(1)}, bf16[192,1152]{1,0:T(8,128)(2,1)}, u32[]{:S(2)}) copy-start(bf16[192,1152]{1,0:T(8,128)(2,1)} %reduce-scatter.5.cloned.1.call-done.down_ref) | copy-start | bytes 1327108
  599.5 54.5 %collective-permute-start.2 = (bf16[72,7296]{1,0:T(8,128)(2,1)}, bf16[72,7296]{1,0:T(8,128)(2,1)S(1)}, u32[]{:S(2)}, u32[]{:S(2)}) collective-permute-start(bf16[72,7296]{1,0:T(8,128)(2,1)} %reduce-scatter.7.cloned.1.call-done.wide_ref), channel_id=1, source_target_pairs={{0,4},{4,0},{1,5},{5,1},{2,6},{6,2},{3,7},{7,3},{8,12},{12,8},{9,1... | collective-permute-start | bytes 3151880 | tf_op jit(solution)/shard_map/ppermute | solution.py:1708
  601.0 53.0 %collective-permute-start.3 = (bf16[192,1152]{1,0:T(8,128)(2,1)S(1)}, bf16[192,1152]{1,0:T(8,128)(2,1)S(1)}, u32[]{:S(2)}, u32[]{:S(2)}) collective-permute-start(bf16[192,1152]{1,0:T(8,128)(2,1)S(1)} %copy-done.3), channel_id=1, source_target_pairs={{0,4},{4,0},{1,5},{5,1},{2,6},{6,2},{3,7},{7,3},{8,12},{12,8},{9,1... | collective-permute-start | bytes 1327112 | tf_op jit(solution)/shard_map/ppermute | solution.py:1708
  654.0 0.8 copy-start.4
  654.0 1.1 copy-start.2
Sparse Core Ops, SparseCore 0:
  10.3 76.4 all-gather.4
  88.3 87.8 all-gather.2
  326.9 90.9 reduce-scatter.4
  422.6 176.8 reduce-scatter.6
